TPU v7x, 256 devices: a whole 4x4x8 slice. The times are simulated.
256 devices in a mesh: row: 8 (over x, core), col: 32 (over z, y).
Axes of the slice: x: 4, y: 4, z: 8, core: 2. Of those that a mesh axis runs over, the one named last changes fastest.
Arguments:
- tokens: bfloat16 [1024, 8192], P('col', 'row'), may hold values from -6 to 6
- gate_weight: bfloat16 [8192, 24576], P('row', 'col'), may hold values from -0.0625 to 0.0625
- up_weight: bfloat16 [8192, 24576], P('row', 'col'), may hold values from -0.0625 to 0.0625
- down_weight: bfloat16 [24576, 8192], P('col', 'row'), may hold values from -0.0390625 to 0.0390625
- out_grad: bfloat16 [1024, 8192], P('col', 'row'), may hold values from -6 to 6
Outputs:
- mixed: bfloat16 [1024, 8192], P('col', 'row')
- input_grad: bfloat16 [1024, 8192], P('col', 'row')
- gate_grad: bfloat16 [8192, 24576], P('row', 'col')
- up_grad: bfloat16 [8192, 24576], P('row', 'col')
- down_grad: bfloat16 [24576, 8192], P('col', 'row')
All inputs are finite; a program needn't handle non-finite values.
Results may differ from a plain program's by a relative error of at most 0.034.
Values may be sent and summed in bfloat16 or wider, within the bound.
No kernel may reach another device: no remote copies, remote signals or barrier semaphores. Data moves between devices by JAX's collectives and lax.ppermute only.
A program may use at most 128 MiB of HBM per device.

v0:
```python
import jax
import jax.numpy as jnp
from jax import lax
from jax.sharding import PartitionSpec as P


def contract_rows(left, right):
    return lax.dot_general(
        left, right, (((0,), (0,)), ((), ())), preferred_element_type=jnp.float32
    )


def contract_cols(left, right):
    return lax.dot_general(
        left, right, (((1,), (1,)), ((), ())), preferred_element_type=jnp.float32
    )


def pre_grads(hidden_grad, gate, up):
    sig = jax.nn.sigmoid(gate)
    pre_gate = (hidden_grad * up * sig * (1.0 + gate * (1.0 - sig))).astype(jnp.bfloat16)
    pre_up = (hidden_grad * gate * sig).astype(jnp.bfloat16)
    return (pre_gate, pre_up)


def body(tokens, gate_weight, up_weight, down_weight, out_grad):
    all_tokens = lax.all_gather(tokens, "col", axis=0, tiled=True)
    gate_term = jnp.dot(all_tokens, gate_weight, preferred_element_type=jnp.float32)
    up_term = jnp.dot(all_tokens, up_weight, preferred_element_type=jnp.float32)
    gate, up = (
        lax.psum_scatter(
            gate_term.astype(jnp.bfloat16), "row", scatter_dimension=0, tiled=True
        ).astype(jnp.float32),
        lax.psum_scatter(
            up_term.astype(jnp.bfloat16), "row", scatter_dimension=0, tiled=True
        ).astype(jnp.float32),
    )
    hidden_own = (gate * jax.nn.sigmoid(gate) * up).astype(jnp.bfloat16)
    hidden = lax.all_gather(hidden_own, "row", axis=0, tiled=True)
    mixed = lax.psum_scatter(
        jnp.dot(hidden, down_weight, preferred_element_type=jnp.float32).astype(jnp.bfloat16),
        "col",
        scatter_dimension=0,
        tiled=True,
    )
    all_grads = lax.all_gather(out_grad, "col", axis=0, tiled=True)
    down_grad = contract_rows(hidden, all_grads).astype(jnp.bfloat16)
    hidden_term = contract_cols(all_grads, down_weight)
    hidden_grad = lax.psum_scatter(
        hidden_term.astype(jnp.bfloat16), "row", scatter_dimension=0, tiled=True
    ).astype(jnp.float32)
    gate_own, up_own = pre_grads(hidden_grad, gate, up)
    pre_gate, pre_up = (
        lax.all_gather(gate_own, "row", axis=0, tiled=True),
        lax.all_gather(up_own, "row", axis=0, tiled=True),
    )
    gate_grad = contract_rows(all_tokens, pre_gate).astype(jnp.bfloat16)
    up_grad = contract_rows(all_tokens, pre_up).astype(jnp.bfloat16)
    input_grad = lax.psum_scatter(
        (contract_cols(pre_gate, gate_weight) + contract_cols(pre_up, up_weight)).astype(
            jnp.bfloat16
        ),
        "col",
        scatter_dimension=0,
        tiled=True,
    )
    return (mixed, input_grad, gate_grad, up_grad, down_grad)


def solution(mesh):
    in_specs = (P("col", "row"), P("row", "col"), P("row", "col"), P("col", "row"), P("col", "row"))
    out_specs = (
        P("col", "row"),
        P("col", "row"),
        P("row", "col"),
        P("row", "col"),
        P("col", "row"),
    )
    return jax.shard_map(body, mesh=mesh, in_specs=in_specs, out_specs=out_specs, check_vma=False)
```

profile of v0, /device:TPU:1, one launch (start us, length us, event | category | flops | bytes accessed | tf_op | source)
XLA Modules:
  0.0 809.7 jit_solution(7231066160111135222)
XLA Ops:
  7.2 0.0 copy-start
  7.2 0.0 all-gather.10.cloned.1.call-start
  7.2 0.7 all-gather.10.cloned.1.call-update
  7.9 0.0 all-gather.6.cloned.1.call-start
  8.0 0.7 all-gather.6.cloned.1.call-update
  8.7 0.0 reduce-scatter.12.cloned.1.call-start
  8.7 79.8 %all-gather.10.cloned.1.call-done = bf16[1024,1024]{1,0:T(8,128)(2,1)} async-done(((bf16[32,1024]{1,0:T(8,128)(2,1)}), bf16[1024,1024]{1,0:T(8,128)(2,1)}) %all-gather.10.cloned.1.call-update) | async-done | bytes 2097168 | tf_op jit(solution)/shard_map/all_gather | solution.py:46
  88.5 0.0 copy-done
  88.5 4.6 convolution_convert_fusion.4
  93.0 0.0 copy-start.2
  93.0 0.0 reduce-scatter.12.cloned.1.call-update
  93.1 0.0 reduce-scatter.8.cloned.1.call-start
  93.1 73.1 %all-gather.6.cloned.1.call-done = bf16[1024,1024]{1,0:T(8,128)(2,1)} async-done(((bf16[32,1024]{1,0:T(8,128)(2,1)}), bf16[1024,1024]{1,0:T(8,128)(2,1)}) %all-gather.6.cloned.1.call-update) | async-done | bytes 2097168 | tf_op jit(solution)/shard_map/all_gather | solution.py:27
  166.2 0.0 copy-done.2
  166.2 4.5 convolution_convert_fusion.5
  170.8 0.0 copy-start.1
  170.8 0.0 reduce-scatter.8.cloned.1.call-update
  170.8 0.0 reduce-scatter.6.cloned.1.call-start
  170.8 1.3 copy-done.1
  172.2 4.5 convolution_convert_fusion.6
  176.7 0.0 reduce-scatter.6.cloned.1.call-update
  176.7 0.0 all-gather.8.cloned.1.call-start
  176.8 26.5 %reduce-scatter.12.cloned.1.call-done = bf16[128,768]{1,0:T(8,128)(2,1)} async-done(((bf16[1024,768]{1,0:T(8,128)(2,1)}), bf16[128,768]{1,0:T(8,128)(2,1)}) %reduce-scatter.12.cloned.1.call-update) | async-done | bytes 196624 | tf_op jit(solution)/shard_map/reduce_scatter | solution.py:49
  203.2 37.1 %reduce-scatter.8.cloned.1.call-done = bf16[128,768]{1,0:T(8,128)(2,1)} async-done(((bf16[1024,768]{1,0:T(8,128)(2,1)}), bf16[128,768]{1,0:T(8,128)(2,1)}) %reduce-scatter.8.cloned.1.call-update) | async-done | bytes 196624 | tf_op jit(solution)/shard_map/reduce_scatter | solution.py:34
  240.4 37.1 %reduce-scatter.6.cloned.1.call-done = bf16[128,768]{1,0:T(8,128)(2,1)} async-done(((bf16[1024,768]{1,0:T(8,128)(2,1)}), bf16[128,768]{1,0:T(8,128)(2,1)}) %reduce-scatter.6.cloned.1.call-update) | async-done | bytes 196624 | tf_op jit(solution)/shard_map/reduce_scatter | solution.py:31
  277.4 2.1 fusion.11
  279.6 0.0 all-gather.8.cloned.1.call-update
  279.6 0.0 all-gather.12.cloned.1.call-start
  279.7 0.7 all-gather.12.cloned.1.call-update
  280.4 0.0 all-gather.14.cloned.1.call-start
  280.4 0.7 all-gather.14.cloned.1.call-update
  281.1 0.0 reduce-scatter.10.cloned.1.call-start
  281.2 27.2 %all-gather.8.cloned.1.call-done = bf16[1024,768]{1,0:T(8,128)(2,1)} async-done(((bf16[128,768]{1,0:T(8,128)(2,1)}), bf16[1024,768]{1,0:T(8,128)(2,1)}) %all-gather.8.cloned.1.call-update) | async-done | bytes 1572880 | tf_op jit(solution)/shard_map/all_gather | solution.py:39
  308.4 4.6 convolution_convert_fusion
  313.0 0.0 reduce-scatter.10.cloned.1.call-update
  313.0 0.2 reduce-scatter.14.cloned.1.call-start
  313.2 24.9 %all-gather.12.cloned.1.call-done = bf16[1024,768]{1,0:T(8,128)(2,1)} async-done(((bf16[128,768]{1,0:T(8,128)(2,1)}), bf16[1024,768]{1,0:T(8,128)(2,1)}) %all-gather.12.cloned.1.call-update) | async-done | bytes 1572880 | tf_op jit(solution)/shard_map/all_gather | solution.py:54
  338.1 5.2 fusion.12
  343.3 24.5 %all-gather.14.cloned.1.call-done = bf16[1024,768]{1,0:T(8,128)(2,1)} async-done(((bf16[128,768]{1,0:T(8,128)(2,1)}), bf16[1024,768]{1,0:T(8,128)(2,1)}) %all-gather.14.cloned.1.call-update) | async-done | bytes 1572880 | tf_op jit(solution)/shard_map/all_gather | solution.py:55
  367.8 6.3 add_convert_fusion
  374.1 0.0 reduce-scatter.14.cloned.1.call-update
  374.1 3.9 fusion.1
  378.0 1.6 copy.11
  379.6 3.9 fusion
  383.5 1.6 copy.10
  385.1 5.0 convolution_convert_fusion.1
  390.1 193.0 %reduce-scatter.10.cloned.1.call-done = bf16[32,1024]{1,0:T(8,128)(2,1)} async-done(((bf16[1024,1024]{1,0:T(8,128)(2,1)}), bf16[32,1024]{1,0:T(8,128)(2,1)}) %reduce-scatter.10.cloned.1.call-update) | async-done | bytes 65552 | tf_op jit(solution)/shard_map/reduce_scatter | solution.py:40
  583.1 219.7 %reduce-scatter.14.cloned.1.call-done = bf16[32,1024]{1,0:T(8,128)(2,1)} async-done(((bf16[1024,1024]{1,0:T(8,128)(2,1)}), bf16[32,1024]{1,0:T(8,128)(2,1)}) %reduce-scatter.14.cloned.1.call-update) | async-done | bytes 65552 | tf_op jit(solution)/shard_map/reduce_scatter | solution.py:59
Async XLA Ops:
  7.2 81.3 %copy-start = (bf16[768,1024]{1,0:T(8,128)(2,1)S(1)}, bf16[768,1024]{1,0:T(8,128)(2,1)}, u32[]{:S(2)}) copy-start(bf16[768,1024]{1,0:T(8,128)(2,1)} %param.8) | copy-start | bytes 4718596
  7.2 81.3 %all-gather.10.cloned.1.call-start = ((), (), s32[]{:S(2)}) async-start(), calls=%async_computation.10 | async-start | bytes 2162688 | tf_op jit(solution)/shard_map/all_gather | solution.py:46
  7.9 158.3 %all-gather.6.cloned.1.call-start = ((), (), s32[]{:S(2)}) async-start(), calls=%async_computation.5 | async-start | bytes 2162688 | tf_op jit(solution)/shard_map/all_gather | solution.py:27
  8.7 194.6 %reduce-scatter.12.cloned.1.call-start = ((), (), s32[]{:S(2)}) async-start(), calls=%async_computation.11 | async-start | bytes 1769472 | tf_op jit(solution)/shard_map/reduce_scatter | solution.py:49
  93.0 73.2 %copy-start.2 = (bf16[1024,768]{1,0:T(8,128)(2,1)S(1)}, bf16[1024,768]{1,0:T(8,128)(2,1)}, u32[]{:S(2)}) copy-start(bf16[1024,768]{1,0:T(8,128)(2,1)} %param.7) | copy-start | bytes 4718596
  93.1 147.3 %reduce-scatter.8.cloned.1.call-start = ((), (), s32[]{:S(2)}) async-start(), calls=%async_computation.7 | async-start | bytes 1769472 | tf_op jit(solution)/shard_map/reduce_scatter | solution.py:34
  170.8 1.4 copy-start.1
  170.8 106.6 %reduce-scatter.6.cloned.1.call-start = ((), (), s32[]{:S(2)}) async-start(), calls=%async_computation.6 | async-start | bytes 1769472 | tf_op jit(solution)/shard_map/reduce_scatter | solution.py:31
  176.7 131.6 %all-gather.8.cloned.1.call-start = ((), (), s32[]{:S(2)}) async-start(), calls=%async_computation.8 | async-start | bytes 1769472 | tf_op jit(solution)/shard_map/all_gather | solution.py:39
  279.6 58.5 %all-gather.12.cloned.1.call-start = ((), (), s32[]{:S(2)}) async-start(), calls=%async_computation.12 | async-start | bytes 1769472 | tf_op jit(solution)/shard_map/all_gather | solution.py:54
  280.4 87.4 %all-gather.14.cloned.1.call-start = ((), (), s32[]{:S(2)}) async-start(), calls=%async_computation.13 | async-start | bytes 1769472 | tf_op jit(solution)/shard_map/all_gather | solution.py:55
  281.1 302.0 %reduce-scatter.10.cloned.1.call-start = ((), (), s32[]{:S(2)}) async-start(), calls=%async_computation.9 | async-start | bytes 2162688 | tf_op jit(solution)/shard_map/reduce_scatter | solution.py:40
  313.0 489.9 %reduce-scatter.14.cloned.1.call-start = ((), (), s32[]{:S(2)}) async-start(), calls=%async_computation.14 | async-start | bytes 2162688 | tf_op jit(solution)/shard_map/reduce_scatter | solution.py:59
Sparse Core Ops, SparseCore 0:
  10.6 77.8 all-gather.9
  91.1 75.1 all-gather.5
  169.4 33.8 reduce-scatter.11
  206.2 34.0 reduce-scatter.7
  243.3 34.0 reduce-scatter.5
  279.7 28.5 all-gather.7
  310.8 27.2 all-gather.11
  340.5 27.2 all-gather.13
  372.2 210.8 reduce-scatter.9
  587.9 214.9 reduce-scatter.13
where the time goes:
time: 814 us; the launch traced here: 810 us
  waiting for transfers between devices  746 us (92%)
  matrix products  42.5 us (5%)
  between operations  14.2 us (2%)
    reduce_scatter x1, waiting for transfers between devices, body(): lax.psum_scatter((contract_cols(pre_gate, gate_weight) + contract_cols(pr...  220 us
    reduce_scatter x1, waiting for transfers between devices, body(): lax.psum_scatter(jnp.dot(hidden, down_weight, preferred_element_type=jnp....  193 us
    all_gather x1, waiting for transfers between devices, body(): all_grads = lax.all_gather(out_grad, 'col', axis=0, tiled=True)  79.8 us
    all_gather x1, waiting for transfers between devices, body(): all_tokens = lax.all_gather(tokens, 'col', axis=0, tiled=True)  73.1 us
    reduce_scatter x1, waiting for transfers between devices, body(): lax.psum_scatter(up_term.astype(jnp.bfloat16), 'row', scatter_dimension=0...  37.1 us
    reduce_scatter x1, waiting for transfers between devices, body(): lax.psum_scatter(gate_term.astype(jnp.bfloat16), 'row', scatter_dimension...  37.1 us
    all_gather x1, waiting for transfers between devices, body(): hidden = lax.all_gather(hidden_own, 'row', axis=0, tiled=True)  27.2 us
    reduce_scatter x1, waiting for transfers between devices, body(): lax.psum_scatter(hidden_term.astype(jnp.bfloat16), 'row', scatter_dimensi...  26.5 us
  transfers between devices with their start and end apart: 10, of which 10 were waited for; matrix products, arithmetic and copies ran while one was open for 6% of the time, Pallas kernels for 0%

commit v1 on v0

v1 whole, which is shorter than its diff:
```python
import jax
import jax.numpy as jnp
from jax import lax
from jax.sharding import PartitionSpec as P

BF16 = jnp.bfloat16
F32 = jnp.float32
NX, NC, NZ, NY = 4, 2, 8, 4

X_GROUPS = [[x * NC + c for x in range(NX)] for c in range(NC)]
Y_GROUPS = [[z * NY + y for y in range(NY)] for z in range(NZ)]
Z_GROUPS = [[z * NY + y for z in range(NZ)] for y in range(NY)]
CORE_PAIRS = [(r, r ^ 1) for r in range(NX * NC)]


def swap_core(value):
    return lax.ppermute(value, "row", CORE_PAIRS)


def exchange(value, axis, groups):
    return lax.all_to_all(value, axis, 0, 0, axis_index_groups=groups, tiled=True)


def share(value, axis, groups):
    return exchange(jnp.tile(value, (len(groups[0]), 1)), axis, groups)


def scatter_sum(value, axis, groups):
    count = len(groups[0])
    got = exchange(value, axis, groups)
    return got.reshape(count, value.shape[0] // count, value.shape[1]).astype(F32).sum(0)


def dot(left, right):
    return jnp.dot(left, right, preferred_element_type=F32)


def dot_rows(left, right):
    return lax.dot_general(left, right, (((0,), (0,)), ((), ())), preferred_element_type=F32)


def dot_cols(left, right):
    return lax.dot_general(left, right, (((1,), (1,)), ((), ())), preferred_element_type=F32)


def after(value, *others):
    return lax.optimization_barrier((value,) + others)[0]


def body(tokens, gate_weight, up_weight, down_weight, out_grad):
    core = lax.axis_index("row") % NC
    half = tokens.shape[0] // NC

    def halves(value):
        mine = lax.dynamic_slice_in_dim(value, core * half, half, 0)
        other = lax.dynamic_slice_in_dim(value, (1 - core) * half, half, 0)
        return jnp.concatenate([mine, swap_core(other)], axis=1)

    def join(value):
        width = value.shape[1] // 2
        mine = value[:, :width]
        got = swap_core(value[:, width:])
        first = jnp.where(core == 0, mine, got)
        second = jnp.where(core == 0, got, mine)
        return jnp.concatenate([first, second], axis=0)

    width = tokens.shape[1]
    hidden_width = gate_weight.shape[1]

    tok = halves(tokens)
    grad = halves(out_grad)
    gate_up = jnp.concatenate([gate_weight, up_weight], axis=1)
    gate_up = jnp.concatenate([gate_up, swap_core(gate_up)], axis=0)
    down = jnp.concatenate([down_weight, swap_core(down_weight)], axis=1)

    tok_z = share(tok, "col", Z_GROUPS)
    grad_z = lax.all_gather(grad, "col", axis=0, axis_index_groups=Z_GROUPS, tiled=True)
    tok_all = share(tok_z, "col", Y_GROUPS)
    grad_all = share(after(grad_z, tok_all), "col", Y_GROUPS)

    gate_up_sum = scatter_sum(dot(tok_all, gate_up).astype(BF16), "row", X_GROUPS)
    gate, up = gate_up_sum[:, :hidden_width], gate_up_sum[:, hidden_width:]
    hidden_grad = scatter_sum(dot_cols(grad_all, down).astype(BF16), "row", X_GROUPS)

    sig = jax.nn.sigmoid(gate)
    hidden_own = (gate * sig * up).astype(BF16)
    pre_gate_own = (hidden_grad * up * sig * (1.0 + gate * (1.0 - sig))).astype(BF16)
    pre_up_own = (hidden_grad * gate * sig).astype(BF16)

    def gather_x(value):
        return lax.all_gather(value, "row", axis=0, axis_index_groups=X_GROUPS, tiled=True)

    hidden = gather_x(hidden_own)
    pre_gate = gather_x(pre_gate_own)
    pre_up = gather_x(pre_up_own)

    mixed_y = scatter_sum(dot(hidden, down).astype(BF16), "col", Y_GROUPS)
    pre = jnp.concatenate([pre_gate, pre_up], axis=1)
    input_y = scatter_sum(dot_cols(pre, gate_up).astype(BF16), "col", Y_GROUPS)
    both = jnp.concatenate([mixed_y.astype(BF16), input_y.astype(BF16)], axis=1)
    both = scatter_sum(both, "col", Z_GROUPS).astype(BF16)
    mixed = join(both[:, : 2 * width])
    input_grad = join(both[:, 2 * width :])

    def all_tokens(value):
        return jnp.concatenate([value, swap_core(value)], axis=0)

    def all_rows(value):
        return jnp.concatenate([value[:, :width], swap_core(value[:, width:])], axis=0)

    tok_rows = all_rows(tok_all)
    grad_rows = all_rows(grad_all)
    down_grad = dot_rows(all_tokens(hidden), grad_rows).astype(BF16)
    gate_grad = dot_rows(tok_rows, all_tokens(pre_gate)).astype(BF16)
    up_grad = dot_rows(tok_rows, all_tokens(pre_up)).astype(BF16)
    return (mixed, input_grad, gate_grad, up_grad, down_grad)


def solution(mesh):
    in_specs = (P("col", "row"), P("row", "col"), P("row", "col"), P("col", "row"), P("col", "row"))
    out_specs = (
        P("col", "row"),
        P("col", "row"),
        P("row", "col"),
        P("row", "col"),
        P("col", "row"),
    )
    return jax.shard_map(body, mesh=mesh, in_specs=in_specs, out_specs=out_specs, check_vma=False)
```

time: 814 us -> 246 us (0.30)
  waiting for transfers between devices: 746 us -> 38.5 us
  blocking collectives: 0 us -> 81.2 us
  starting transfers between devices: 0.58 us -> 58.3 us
  between operations: 14.2 us -> 0.84 us
  local copies, waits for them, and re-layouts: 4.49 us -> 16.3 us
  other arithmetic: 2.14 us -> 10.6 us
    reduce_scatter x5 -> x0, waiting for transfers between devices: 513 us -> none  [the longest x1 220 us: body(): lax.psum_scatter((contract_cols(pre_gate, gate_weight) + contract_cols(pr...]
    all_gather x5 -> x0, waiting for transfers between devices: 229 us -> none  [the longest x1 79.8 us: body(): all_grads = lax.all_gather(out_grad, 'col', axis=0, tiled=True)]
    all_gather x0 -> x4, blocking collectives: none -> 58.6 us  [the longest x3 37.4 us: gather_x(): lax.all_gather(value, 'row', axis=0, axis_index_groups=X_GROUPS, tiled=True)]
    all_to_all x0 -> x7, waiting for transfers between devices: none -> 36.1 us  [exchange(): lax.all_to_all(value, axis, 0, 0, axis_index_groups=groups, tiled=True)]
    ppermute x0 -> x11, starting transfers between devices: none -> 29.4 us  [swap_core(): return lax.ppermute(value, 'row', CORE_PAIRS)]
    all_to_all x0 -> x7, starting transfers between devices: none -> 28.9 us  [exchange(): lax.all_to_all(value, axis, 0, 0, axis_index_groups=groups, tiled=True)]
    all_to_all x0 -> x1, blocking collectives: none -> 22.5 us  [exchange(): lax.all_to_all(value, axis, 0, 0, axis_index_groups=groups, tiled=True)]
    dot_general x9 -> x7, matrix products: 42.5 us -> 39.7 us  [the longest x3 14.5 us: dot_rows(): lax.dot_general(left, right, (((0,), (0,)), ((), ())), preferred_element_...]
  transfers between devices with their start and end apart: 10 -> 18, of which waited for: 10 -> 7; matrix products, arithmetic and copies ran while one was open for 6% -> 21% of each run, Pallas kernels for 0% -> 0%
where the time goes in v1:
time: 246 us; the launch traced here: 245 us
  blocking collectives  81.2 us (33%)
  starting transfers between devices  58.3 us (24%)
  matrix products  39.7 us (16%)
  waiting for transfers between devices  38.5 us (16%)
  local copies, waits for them, and re-layouts  16.3 us (7%)
  other arithmetic  10.6 us (4%)
    all_gather x3, blocking collectives, gather_x(): lax.all_gather(value, 'row', axis=0, axis_index_groups=X_GROUPS, tiled=True)  37.4 us
    all_to_all x7, waiting for transfers between devices, exchange(): lax.all_to_all(value, axis, 0, 0, axis_index_groups=groups, tiled=True)  36.1 us
    ppermute x11, starting transfers between devices, swap_core(): return lax.ppermute(value, 'row', CORE_PAIRS)  29.4 us
    all_to_all x7, starting transfers between devices, exchange(): lax.all_to_all(value, axis, 0, 0, axis_index_groups=groups, tiled=True)  28.9 us
    all_to_all x1, blocking collectives, exchange(): lax.all_to_all(value, axis, 0, 0, axis_index_groups=groups, tiled=True)  22.5 us
    all_gather x1, blocking collectives, body(): lax.all_gather(grad, 'col', axis=0, axis_index_groups=Z_GROUPS, tiled=True)  21.2 us
    dot_general x3, matrix products, dot_rows(): lax.dot_general(left, right, (((0,), (0,)), ((), ())), preferred_element_...  14.5 us
    dot_general x2, matrix products, dot(): return jnp.dot(left, right, preferred_element_type=F32)  12.7 us
  transfers between devices with their start and end apart: 18, of which 7 were waited for; matrix products, arithmetic and copies ran while one was open for 21% of the time, Pallas kernels for 0%

profile of v1, /device:TPU:1, one launch (start us, length us, event | category | flops | bytes accessed | tf_op | source)
XLA Modules:
  0.0 245.4 jit_solution(14097872836578622793)
XLA Ops:
  0.7 0.9 constant_dynamic-slice_fusion.3
  1.6 3.2 %collective-permute-start = (bf16[16,1024]{1,0:T(8,128)(2,1)S(1)}, bf16[16,1024]{1,0:T(8,128)(2,1)S(1)}, u32[]{:S(2)}, u32[]{:S(2)}) collective-permute-start(bf16[16,1024]{1,0:T(8,128)(2,1)S(1)} %get-tuple-element.20), channel_id=1, source_target_pairs={{0,32},{32,0},{64,96},{96,64},{128,160},{160,128},{192,224},{224,1... | collective-permute-start | bytes 98312 | tf_op jit(solution)/shard_map/ppermute | solution.py:17
  4.8 2.7 %constant_dynamic-update-slice_fusion.1 = bf16[1024,1536]{1,0:T(8,128)(2,1)} fusion(bf16[1024,768]{1,0:T(8,128)(2,1)} %param.6), kind=kLoop, calls=%fused_computation.43 | loop fusion | bytes 3145728
  7.5 1.3 constant_dynamic-update-slice_fusion
  8.9 0.0 collective-permute-start.1
  8.9 0.0 collective-permute-done
  8.9 22.5 %all_to_all.69 = bf16[8,16,2048]{2,1,0:T(8,128)(2,1)S(1)} all-to-all(bf16[8,16,2048]{2,1,0:T(8,128)(2,1)S(1)} %tile.8), channel_id=1, replica_groups={{0,4,8,12,16,20,24,28},{1,5,9,13,17,21,25,29},{2,6,10,14,18,22,26,30},{..., dimensions={0} | all-to-all | bytes 1048576 | tf_op jit(solution)/shard_map/all_to_all | solution.py:21
  31.5 1.6 tile.10
  33.1 4.2 %all-to-all-start.1 = ((bf16[4,128,2048]{2,1,0:T(8,128)(2,1)}), bf16[4,128,2048]{2,1,0:T(8,128)(2,1)S(1)}, u32[]{:S(2)}, u32[]{:S(2)}) async-start(bf16[4,128,2048]{2,1,0:T(8,128)(2,1)} %tile.10), calls=%async_computation.1 | async-start | bytes 4194304 | tf_op jit(solution)/shard_map/all_to_all | solution.py:21
  37.3 2.5 %collective-permute-start.3 = (bf16[16,1024]{1,0:T(8,128)(2,1)S(1)}, bf16[16,1024]{1,0:T(8,128)(2,1)S(1)}, u32[]{:S(2)}, u32[]{:S(2)}) collective-permute-start(bf16[16,1024]{1,0:T(8,128)(2,1)S(1)} %get-tuple-element.22), channel_id=1, source_target_pairs={{0,32},{32,0},{64,96},{96,64},{128,160},{160,128},{192,224},{224,1... | collective-permute-start | bytes 98312 | tf_op jit(solution)/shard_map/ppermute | solution.py:17
  39.8 0.9 collective-permute-done.3
  40.7 21.2 %all_gather.13 = bf16[128,2048]{1,0:T(8,128)(2,1)S(1)} all-gather(bf16[16,2048]{1,0:T(8,128)(2,1)S(1)} %pad_maximum_fusion.12), channel_id=1, replica_groups={{0,4,8,12,16,20,24,28},{1,5,9,13,17,21,25,29},{2,6,10,14,18,22,26,30},{..., dimensions={0}, use_global_device_ids=true | all-gather | bytes 589824 | tf_op jit(solution)/shard_map/all_gather | solution.py:77
  61.9 0.0 all-to-all-done.1
  61.9 1.6 tile.11
  63.6 4.4 %all-to-all-start.4 = ((bf16[4,128,2048]{2,1,0:T(8,128)(2,1)}), bf16[4,128,2048]{2,1,0:T(8,128)(2,1)}, u32[]{:S(2)}, u32[]{:S(2)}) async-start(bf16[4,128,2048]{2,1,0:T(8,128)(2,1)} %tile.11), calls=%async_computation.4 | async-start | bytes 4194304 | tf_op jit(solution)/shard_map/all_to_all | solution.py:21
  68.0 4.7 %collective-permute-start.2 = (bf16[768,1024]{1,0:T(8,128)(2,1)}, bf16[768,1024]{1,0:T(8,128)(2,1)}, u32[]{:S(2)}, u32[]{:S(2)}) collective-permute-start(bf16[768,1024]{1,0:T(8,128)(2,1)} %param.8), channel_id=1, source_target_pairs={{0,32},{32,0},{64,96},{96,64},{128,160},{160,128},{192,224},{224,1... | collective-permute-start | bytes 4718600 | tf_op jit(solution)/shard_map/ppermute | solution.py:17
  72.7 0.0 collective-permute-done.1
  72.7 7.4 %fusion.2 = bf16[512,1536]{1,0:T(8,128)(2,1)} fusion(bf16[512,2048]{1,0:T(8,128)(2,1)S(1)} %bitcast.13, bf16[1024,1536]{1,0:T(8,128)(2,1)} %collective-permute-done.1, bf16[1024,1536]{1,0:T(8,128)(2,1)} %constant_dynamic-update-slice_fusion), kind=kOutput, calls=%fused_computation.4 | convolution fusion | flops 3234594816 | bytes 9961472 | tf_op jit(solution)/shard_map/dot_general | solution.py:35
  80.1 9.5 %all-to-all-done.4 = bf16[4,128,2048]{2,1,0:T(8,128)(2,1)} async-done(((bf16[4,128,2048]{2,1,0:T(8,128)(2,1)}), bf16[4,128,2048]{2,1,0:T(8,128)(2,1)}, u32[]{:S(2)}, u32[]{:S(2)}) %all-to-all-start.4) | async-done | bytes 2097184 | tf_op jit(solution)/shard_map/all_to_all | solution.py:21
  89.7 4.4 %all-to-all-start.2 = ((bf16[4,128,1536]{2,1,0:T(8,128)(2,1)}), bf16[4,128,1536]{2,1,0:T(8,128)(2,1)}, u32[]{:S(2)}, u32[]{:S(2)}) async-start(bf16[4,128,1536]{2,1,0:T(8,128)(2,1)} %bitcast.19), calls=%async_computation.2 | async-start | bytes 3145728 | tf_op jit(solution)/shard_map/all_to_all | solution.py:21
  94.0 1.6 constant_dynamic-update-slice_fusion.3
  95.6 0.0 collective-permute-done.2
  95.6 1.6 constant_dynamic-update-slice_fusion.2
  97.2 1.7 copy-done.2
  98.9 4.3 %convolution_convert_fusion.3 = bf16[512,768]{1,0:T(8,128)(2,1)} fusion(bf16[512,2048]{1,0:T(8,128)(2,1)} %bitcast.4, bf16[768,2048]{1,0:T(8,128)(2,1)S(1)} %constant_dynamic-update-slice_fusion.2), kind=kOutput, calls=%fused_computation.28 | convolution fusion | flops 1611005952 | bytes 6029312 | tf_op jit(solution)/shard_map/dot_general | solution.py:43
  103.2 5.7 %all-to-all-done.2 = bf16[4,128,1536]{2,1,0:T(8,128)(2,1)} async-done(((bf16[4,128,1536]{2,1,0:T(8,128)(2,1)}), bf16[4,128,1536]{2,1,0:T(8,128)(2,1)}, u32[]{:S(2)}, u32[]{:S(2)}) %all-to-all-start.2) | async-done | bytes 1572896 | tf_op jit(solution)/shard_map/all_to_all | solution.py:21
  108.8 3.5 %all-to-all-start.5 = ((bf16[4,128,768]{2,1,0:T(8,128)(2,1)}), bf16[4,128,768]{2,1,0:T(8,128)(2,1)S(1)}, u32[]{:S(2)}, u32[]{:S(2)}) async-start(bf16[4,128,768]{2,1,0:T(8,128)(2,1)} %bitcast.20), calls=%async_computation.5 | async-start | bytes 1572864 | tf_op jit(solution)/shard_map/all_to_all | solution.py:21
  112.3 2.6 %convert_reduce_fusion = f32[128,1536]{1,0:T(8,128)} fusion(bf16[4,128,1536]{2,1,0:T(8,128)(2,1)} %all-to-all-done.2), kind=kLoop, calls=%fused_computation.3 | loop fusion | flops 1376256 | bytes 2359296 | tf_op jit(solution)/shard_map/reduce_sum | solution.py:31
  114.9 5.7 %all-to-all-done.5 = bf16[4,128,768]{2,1,0:T(8,128)(2,1)S(1)} async-done(((bf16[4,128,768]{2,1,0:T(8,128)(2,1)}), bf16[4,128,768]{2,1,0:T(8,128)(2,1)S(1)}, u32[]{:S(2)}, u32[]{:S(2)}) %all-to-all-start.5) | async-done | bytes 786464 | tf_op jit(solution)/shard_map/all_to_all | solution.py:21
  120.6 0.1 convert_reduce_fusion.1
  120.8 1.3 multiply_convert_fusion.1
  122.1 13.1 %all_gather.15 = bf16[512,768]{1,0:T(8,128)(2,1)} all-gather(bf16[128,768]{1,0:T(8,128)(2,1)S(1)} %get-tuple-element.12), channel_id=1, replica_groups={{0,64,128,192},{32,96,160,224},{1,65,129,193},{33,97,161,225},{2,66,130..., dimensions={0}, use_global_device_ids=true | all-gather | bytes 983040 | tf_op jit(solution)/shard_map/all_gather | solution.py:91
  135.2 13.0 %all_gather.14 = bf16[512,768]{1,0:T(8,128)(2,1)} all-gather(bf16[128,768]{1,0:T(8,128)(2,1)S(1)} %get-tuple-element.11), channel_id=1, replica_groups={{0,64,128,192},{32,96,160,224},{1,65,129,193},{33,97,161,225},{2,66,130..., dimensions={0}, use_global_device_ids=true | all-gather | bytes 983040 | tf_op jit(solution)/shard_map/all_gather | solution.py:91
  148.1 8.2 %fusion.3 = bf16[512,2048]{1,0:T(8,128)(2,1)} fusion(bf16[1024,1536]{1,0:T(8,128)(2,1)} %collective-permute-done.1, bf16[1024,1536]{1,0:T(8,128)(2,1)} %constant_dynamic-update-slice_fusion, bf16[512,768]{1,0:T(8,128)(2,1)} %all_gather.15, bf16[512,768]{1,0:T(8,128)(2,1)} %all_gather.14), kind=kOutput, calls=%fused_computation.5 | convolution fusion | flops 3238002688 | bytes 9961472 | tf_op jit(solution)/shard_map/dot_general | solution.py:43
  156.4 4.5 %all-to-all-start.6 = ((bf16[4,128,2048]{2,1,0:T(8,128)(2,1)}), bf16[4,128,2048]{2,1,0:T(8,128)(2,1)}, u32[]{:S(2)}, u32[]{:S(2)}) async-start(bf16[4,128,2048]{2,1,0:T(8,128)(2,1)} %bitcast.18), calls=%async_computation.6 | async-start | bytes 4194304 | tf_op jit(solution)/shard_map/all_to_all | solution.py:21
  160.8 11.3 %all_gather.12 = bf16[512,768]{1,0:T(8,128)(2,1)} all-gather(bf16[128,768]{1,0:T(8,128)(2,1)S(1)} %get-tuple-element.13), channel_id=1, replica_groups={{0,64,128,192},{32,96,160,224},{1,65,129,193},{33,97,161,225},{2,66,130..., dimensions={0}, use_global_device_ids=true | all-gather | bytes 983040 | tf_op jit(solution)/shard_map/all_gather | solution.py:91
  172.2 5.3 %convolution_convert_fusion = bf16[512,2048]{1,0:T(8,128)(2,1)} fusion(bf16[512,768]{1,0:T(8,128)(2,1)} %all_gather.12, bf16[768,2048]{1,0:T(8,128)(2,1)} %copy-done.2), kind=kOutput, calls=%fused_computation.6 | convolution fusion | flops 1611661312 | bytes 6029312 | tf_op jit(solution)/shard_map/dot_general | solution.py:35
  177.5 0.0 all-to-all-done.6
  177.5 4.4 %all-to-all-start.3 = ((bf16[4,128,2048]{2,1,0:T(8,128)(2,1)}), bf16[4,128,2048]{2,1,0:T(8,128)(2,1)}, u32[]{:S(2)}, u32[]{:S(2)}) async-start(bf16[4,128,2048]{2,1,0:T(8,128)(2,1)} %bitcast.17), calls=%async_computation.3 | async-start | bytes 4194304 | tf_op jit(solution)/shard_map/all_to_all | solution.py:21
  181.9 2.0 reduce_sum.57
  184.0 15.2 %all-to-all-done.3 = bf16[4,128,2048]{2,1,0:T(8,128)(2,1)} async-done(((bf16[4,128,2048]{2,1,0:T(8,128)(2,1)}), bf16[4,128,2048]{2,1,0:T(8,128)(2,1)}, u32[]{:S(2)}, u32[]{:S(2)}) %all-to-all-start.3) | async-done | bytes 2097184 | tf_op jit(solution)/shard_map/all_to_all | solution.py:21
  199.2 2.0 reduce_sum.55
  201.2 1.0 pad_maximum_fusion.10
  202.3 3.6 %all-to-all-start.7 = ((bf16[8,16,4096]{2,1,0:T(8,128)(2,1)}), bf16[8,16,4096]{2,1,0:T(8,128)(2,1)S(1)}, u32[]{:S(2)}, u32[]{:S(2)}) async-start(bf16[8,16,4096]{2,1,0:T(8,128)(2,1)} %bitcast.15), calls=%async_computation.7 | async-start | bytes 2097152 | tf_op jit(solution)/shard_map/all_to_all | solution.py:21
  205.9 1.5 fusion.29
  207.4 13.8 %collective-permute-start.6 = (bf16[512,1024]{1,0:T(8,128)(2,1)}, bf16[512,1024]{1,0:T(8,128)(2,1)}, u32[]{:S(2)}, u32[]{:S(2)}) collective-permute-start(bf16[512,1024]{1,0:T(8,128)(2,1)} %get-tuple-element.10), channel_id=1, source_target_pairs={{0,32},{32,0},{64,96},{96,64},{128,160},{160,128},{192,224},{224,1... | collective-permute-start | bytes 3145736 | tf_op jit(solution)/shard_map/ppermute | solution.py:17
  221.2 0.5 collective-permute-start.8
  221.7 1.7 fusion.28
  223.4 0.1 collective-permute-start.10
  223.5 0.5 collective-permute-start.9
  224.0 0.0 collective-permute-done.6
  224.0 0.9 collective-permute-done.7
  224.9 5.1 %convolution_convert_fusion.2 = bf16[1024,768]{1,0:T(8,128)(2,1)} fusion(bf16[512,768]{1,0:T(8,128)(2,1)} %collective-permute-done.7, bf16[512,768]{1,0:T(8,128)(2,1)} %all_gather.14, bf16[512,1024]{1,0:T(8,128)(2,1)} %collective-permute-done.6, bf16[512,1024]{1,0:T(8,128)(2,1)} %get-tuple-element.9), kind=kOutput, calls=%fused_computation.14 | convolution fusion | flops 1618739200 | bytes 5242880 | tf_op jit(solution)/shard_map/dot_general | solution.py:39
  230.0 0.0 collective-permute-done.8
  230.0 4.7 %convolution_convert_fusion.1 = bf16[1024,768]{1,0:T(8,128)(2,1)} fusion(bf16[512,768]{1,0:T(8,128)(2,1)} %collective-permute-done.8, bf16[512,768]{1,0:T(8,128)(2,1)} %all_gather.15, bf16[512,1024]{1,0:T(8,128)(2,1)} %collective-permute-done.6, bf16[512,1024]{1,0:T(8,128)(2,1)S(1)} %copy-done.1), kind=kOutput, calls=%fused_computation.13 | convolution fusion | flops 1618739200 | bytes 5242880 | tf_op jit(solution)/shard_map/dot_general | solution.py:39
  234.7 0.1 reduce_sum.58
  234.9 3.9 %collective-permute-start.5 = (bf16[16,1024]{1,0:T(8,128)(2,1)S(1)}, bf16[16,1024]{1,0:T(8,128)(2,1)S(1)}, u32[]{:S(2)}, u32[]{:S(2)}) collective-permute-start(bf16[16,1024]{1,0:T(8,128)(2,1)S(1)} %slice.51), channel_id=1, source_target_pairs={{0,32},{32,0},{64,96},{96,64},{128,160},{160,128},{192,224},{224,1... | collective-permute-start | bytes 98312 | tf_op jit(solution)/shard_map/ppermute | solution.py:17
  238.8 0.0 collective-permute-done.10
  238.8 0.0 collective-permute-done.9
  238.8 4.7 %fusion.8 = bf16[768,1024]{1,0:T(8,128)(2,1)} fusion(bf16[512,1024]{1,0:T(8,128)(2,1)} %collective-permute-done.10, bf16[512,1024]{1,0:T(8,128)(2,1)S(1)} %get-tuple-element.7, bf16[512,768]{1,0:T(8,128)(2,1)} %collective-permute-done.9, bf16[512,768]{1,0:T(8,128)(2,1)} %all_gather.12), kind=kOutput, calls=%fused_computation.12 | convolution fusion | flops 1618739200 | bytes 5242880 | tf_op jit(solution)/shard_map/dot_general | solution.py:39
  243.5 0.1 collective-permute-start.4
  243.6 0.6 pad_maximum_fusion.14
  244.2 0.5 collective-permute-done.4
  244.8 0.6 pad_maximum_fusion.13
  (17 shorter events, 0.1 us)
Async XLA Ops:
  0.6 6.9 %copy-start = (bf16[1024,768]{1,0:T(8,128)(2,1)S(1)}, bf16[1024,768]{1,0:T(8,128)(2,1)}, u32[]{:S(2)}) copy-start(bf16[1024,768]{1,0:T(8,128)(2,1)} %param.7) | copy-start | bytes 4718596
  1.6 7.3 %collective-permute-start = (bf16[16,1024]{1,0:T(8,128)(2,1)S(1)}, bf16[16,1024]{1,0:T(8,128)(2,1)S(1)}, u32[]{:S(2)}, u32[]{:S(2)}) collective-permute-start(bf16[16,1024]{1,0:T(8,128)(2,1)S(1)} %get-tuple-element.20), channel_id=1, source_target_pairs={{0,32},{32,0},{64,96},{96,64},{128,160},{160,128},{192,224},{224,1... | collective-permute-start | bytes 98312 | tf_op jit(solution)/shard_map/ppermute | solution.py:17
  8.9 63.9 %collective-permute-start.1 = (bf16[1024,1536]{1,0:T(8,128)(2,1)}, bf16[1024,1536]{1,0:T(8,128)(2,1)}, u32[]{:S(2)}, u32[]{:S(2)}) collective-permute-start(bf16[1024,1536]{1,0:T(8,128)(2,1)} %constant_dynamic-update-slice_fusion), channel_id=1, source_target_pairs={{0,32},{32,0},{64,96},{96,64},{128,160},{160,128},{192,224},{224,1... | collective-permute-start | bytes 9437192 | tf_op jit(solution)/shard_map/ppermute | solution.py:17
  31.5 5.8 %copy-start.3 = (bf16[32,1024]{1,0:T(8,128)(2,1)S(1)}, bf16[32,1024]{1,0:T(8,128)(2,1)}, u32[]{:S(2)}) copy-start(bf16[32,1024]{1,0:T(8,128)(2,1)} %param.9) | copy-start | bytes 196612
  33.1 28.8 %all-to-all-start.1 = ((bf16[4,128,2048]{2,1,0:T(8,128)(2,1)}), bf16[4,128,2048]{2,1,0:T(8,128)(2,1)S(1)}, u32[]{:S(2)}, u32[]{:S(2)}) async-start(bf16[4,128,2048]{2,1,0:T(8,128)(2,1)} %tile.10), calls=%async_computation.1 | async-start | bytes 4194304 | tf_op jit(solution)/shard_map/all_to_all | solution.py:21
  37.3 3.4 %collective-permute-start.3 = (bf16[16,1024]{1,0:T(8,128)(2,1)S(1)}, bf16[16,1024]{1,0:T(8,128)(2,1)S(1)}, u32[]{:S(2)}, u32[]{:S(2)}) collective-permute-start(bf16[16,1024]{1,0:T(8,128)(2,1)S(1)} %get-tuple-element.22), channel_id=1, source_target_pairs={{0,32},{32,0},{64,96},{96,64},{128,160},{160,128},{192,224},{224,1... | collective-permute-start | bytes 98312 | tf_op jit(solution)/shard_map/ppermute | solution.py:17
  63.6 26.1 %all-to-all-start.4 = ((bf16[4,128,2048]{2,1,0:T(8,128)(2,1)}), bf16[4,128,2048]{2,1,0:T(8,128)(2,1)}, u32[]{:S(2)}, u32[]{:S(2)}) async-start(bf16[4,128,2048]{2,1,0:T(8,128)(2,1)} %tile.11), calls=%async_computation.4 | async-start | bytes 4194304 | tf_op jit(solution)/shard_map/all_to_all | solution.py:21
  68.0 27.6 %collective-permute-start.2 = (bf16[768,1024]{1,0:T(8,128)(2,1)}, bf16[768,1024]{1,0:T(8,128)(2,1)}, u32[]{:S(2)}, u32[]{:S(2)}) collective-permute-start(bf16[768,1024]{1,0:T(8,128)(2,1)} %param.8), channel_id=1, source_target_pairs={{0,32},{32,0},{64,96},{96,64},{128,160},{160,128},{192,224},{224,1... | collective-permute-start | bytes 4718600 | tf_op jit(solution)/shard_map/ppermute | solution.py:17
  89.7 19.2 %all-to-all-start.2 = ((bf16[4,128,1536]{2,1,0:T(8,128)(2,1)}), bf16[4,128,1536]{2,1,0:T(8,128)(2,1)}, u32[]{:S(2)}, u32[]{:S(2)}) async-start(bf16[4,128,1536]{2,1,0:T(8,128)(2,1)} %bitcast.19), calls=%async_computation.2 | async-start | bytes 3145728 | tf_op jit(solution)/shard_map/all_to_all | solution.py:21
  97.2 1.7 copy-start.2
  108.8 11.8 %all-to-all-start.5 = ((bf16[4,128,768]{2,1,0:T(8,128)(2,1)}), bf16[4,128,768]{2,1,0:T(8,128)(2,1)S(1)}, u32[]{:S(2)}, u32[]{:S(2)}) async-start(bf16[4,128,768]{2,1,0:T(8,128)(2,1)} %bitcast.20), calls=%async_computation.5 | async-start | bytes 1572864 | tf_op jit(solution)/shard_map/all_to_all | solution.py:21
  156.4 21.1 %all-to-all-start.6 = ((bf16[4,128,2048]{2,1,0:T(8,128)(2,1)}), bf16[4,128,2048]{2,1,0:T(8,128)(2,1)}, u32[]{:S(2)}, u32[]{:S(2)}) async-start(bf16[4,128,2048]{2,1,0:T(8,128)(2,1)} %bitcast.18), calls=%async_computation.6 | async-start | bytes 4194304 | tf_op jit(solution)/shard_map/all_to_all | solution.py:21
  177.5 21.7 %all-to-all-start.3 = ((bf16[4,128,2048]{2,1,0:T(8,128)(2,1)}), bf16[4,128,2048]{2,1,0:T(8,128)(2,1)}, u32[]{:S(2)}, u32[]{:S(2)}) async-start(bf16[4,128,2048]{2,1,0:T(8,128)(2,1)} %bitcast.17), calls=%async_computation.3 | async-start | bytes 4194304 | tf_op jit(solution)/shard_map/all_to_all | solution.py:21
  202.3 32.4 %all-to-all-start.7 = ((bf16[8,16,4096]{2,1,0:T(8,128)(2,1)}), bf16[8,16,4096]{2,1,0:T(8,128)(2,1)S(1)}, u32[]{:S(2)}, u32[]{:S(2)}) async-start(bf16[8,16,4096]{2,1,0:T(8,128)(2,1)} %bitcast.15), calls=%async_computation.7 | async-start | bytes 2097152 | tf_op jit(solution)/shard_map/all_to_all | solution.py:21
  207.4 16.6 %collective-permute-start.6 = (bf16[512,1024]{1,0:T(8,128)(2,1)}, bf16[512,1024]{1,0:T(8,128)(2,1)}, u32[]{:S(2)}, u32[]{:S(2)}) collective-permute-start(bf16[512,1024]{1,0:T(8,128)(2,1)} %get-tuple-element.10), channel_id=1, source_target_pairs={{0,32},{32,0},{64,96},{96,64},{128,160},{160,128},{192,224},{224,1... | collective-permute-start | bytes 3145736 | tf_op jit(solution)/shard_map/ppermute | solution.py:17
  221.2 3.8 %collective-permute-start.7 = (bf16[512,768]{1,0:T(8,128)(2,1)}, bf16[512,768]{1,0:T(8,128)(2,1)}, u32[]{:S(2)}, u32[]{:S(2)}) collective-permute-start(bf16[512,768]{1,0:T(8,128)(2,1)} %all_gather.14), channel_id=1, source_target_pairs={{0,32},{32,0},{64,96},{96,64},{128,160},{160,128},{192,224},{224,1... | collective-permute-start | bytes 2359304 | tf_op jit(solution)/shard_map/ppermute | solution.py:17
  221.2 8.9 %collective-permute-start.8 = (bf16[512,768]{1,0:T(8,128)(2,1)}, bf16[512,768]{1,0:T(8,128)(2,1)}, u32[]{:S(2)}, u32[]{:S(2)}) collective-permute-start(bf16[512,768]{1,0:T(8,128)(2,1)} %all_gather.15), channel_id=1, source_target_pairs={{0,32},{32,0},{64,96},{96,64},{128,160},{160,128},{192,224},{224,1... | collective-permute-start | bytes 2359304 | tf_op jit(solution)/shard_map/ppermute | solution.py:17
  223.4 15.4 %collective-permute-start.10 = (bf16[512,1024]{1,0:T(8,128)(2,1)S(1)}, bf16[512,1024]{1,0:T(8,128)(2,1)}, u32[]{:S(2)}, u32[]{:S(2)}) collective-permute-start(bf16[512,1024]{1,0:T(8,128)(2,1)S(1)} %get-tuple-element.8), channel_id=1, source_target_pairs={{0,32},{32,0},{64,96},{96,64},{128,160},{160,128},{192,224},{224,1... | collective-permute-start | bytes 3145736 | tf_op jit(solution)/shard_map/ppermute | solution.py:17
  223.5 15.3 %collective-permute-start.9 = (bf16[512,768]{1,0:T(8,128)(2,1)}, bf16[512,768]{1,0:T(8,128)(2,1)}, u32[]{:S(2)}, u32[]{:S(2)}) collective-permute-start(bf16[512,768]{1,0:T(8,128)(2,1)} %all_gather.12), channel_id=1, source_target_pairs={{0,32},{32,0},{64,96},{96,64},{128,160},{160,128},{192,224},{224,1... | collective-permute-start | bytes 2359304 | tf_op jit(solution)/shard_map/ppermute | solution.py:17
  224.9 5.1 %copy-start.1 = (bf16[512,1024]{1,0:T(8,128)(2,1)S(1)}, bf16[512,1024]{1,0:T(8,128)(2,1)}, u32[]{:S(2)}) copy-start(bf16[512,1024]{1,0:T(8,128)(2,1)} %get-tuple-element.9) | copy-start | bytes 3145732
  234.9 8.6 %collective-permute-start.5 = (bf16[16,1024]{1,0:T(8,128)(2,1)S(1)}, bf16[16,1024]{1,0:T(8,128)(2,1)S(1)}, u32[]{:S(2)}, u32[]{:S(2)}) collective-permute-start(bf16[16,1024]{1,0:T(8,128)(2,1)S(1)} %slice.51), channel_id=1, source_target_pairs={{0,32},{32,0},{64,96},{96,64},{128,160},{160,128},{192,224},{224,1... | collective-permute-start | bytes 98312 | tf_op jit(solution)/shard_map/ppermute | solution.py:17
  243.5 1.3 collective-permute-start.4

commit v2 on v1

v2 whole, which is shorter than its diff:
```python
import jax
import jax.numpy as jnp
from jax import lax
from jax.experimental import pallas as pl
from jax.experimental.pallas import tpu as pltpu
from jax.sharding import PartitionSpec as P

BF16 = jnp.bfloat16
F32 = jnp.float32
NX, NC, NZ, NY = 4, 2, 8, 4
MIB = 1024 * 1024

X_GROUPS = [[x * NC + c for x in range(NX)] for c in range(NC)]
Y_GROUPS = [[z * NY + y for y in range(NY)] for z in range(NZ)]
Z_GROUPS = [[z * NY + y for z in range(NZ)] for y in range(NY)]
Y_UP = [(z * NY + y, z * NY + (y + 1) % NY) for z in range(NZ) for y in range(NY)]
Y_DOWN = [(dst, src) for src, dst in Y_UP]
X_UP = [(x * NC + c, (x + 1) % NX * NC + c) for x in range(NX) for c in range(NC)]
X_DOWN = [(dst, src) for src, dst in X_UP]
CORE_PAIRS = [(r, r ^ 1) for r in range(NX * NC)]

NN = (((1,), (0,)), ((), ()))
NT = (((1,), (1,)), ((), ()))
TN = (((0,), (0,)), ((), ()))


def dot(left, right, dims):
    return lax.dot_general(left, right, dims, preferred_element_type=F32)


def swap_core(value):
    return lax.ppermute(value, "row", CORE_PAIRS)


def exchange(value, axis, groups):
    count = len(groups[0])
    got = lax.all_to_all(value, axis, 0, 0, axis_index_groups=groups, tiled=True)
    return got.reshape(count, value.shape[0] // count, value.shape[1])


def share(value, axis, groups):
    got = exchange(jnp.tile(value, (len(groups[0]), 1)), axis, groups)
    return got.reshape(-1, value.shape[1])


def after(value, *others):
    return lax.optimization_barrier((value,) + others)[0]


def ring_blocks(own, axis, up, down):
    half = own.shape[0] // 2
    before = lax.ppermute(own, axis, up)
    behind = lax.ppermute(own, axis, down)
    top = lax.ppermute(before[:half], axis, up)
    bottom = lax.ppermute(behind[half:], axis, down)
    return own, behind, top, bottom, before


def whole(shape):
    return pl.BlockSpec(shape, lambda *_: (0,) * len(shape))


def call(kernel, grid, in_specs, out_specs, out_shape, flops, scratch=(), limit=24):
    return pl.pallas_call(
        kernel,
        grid_spec=pltpu.PrefetchScalarGridSpec(
            num_scalar_prefetch=1,
            grid=grid,
            in_specs=in_specs,
            out_specs=out_specs,
            scratch_shapes=list(scratch),
        ),
        out_shape=out_shape,
        compiler_params=pltpu.CompilerParams(vmem_limit_bytes=limit * MIB),
        cost_estimate=pl.CostEstimate(flops=flops, bytes_accessed=10 * MIB, transcendentals=0),
    )


def place(index, own, behind, top, bottom, before, store):
    rows = own.shape[0]
    half = rows // 2
    store(lax.rem(index, 4), 0, own)
    store(lax.rem(index + 1, 4), 0, behind)
    store(lax.rem(index + 2, 4), 0, top)
    store(lax.rem(index + 2, 4), half, bottom)
    store(lax.rem(index + 3, 4), 0, before)


def gate_up_kernel(index, tok, gate_a, gate_b, up_a, up_b, out):
    del index
    step = pl.program_id(0)
    width = gate_a.shape[0]

    def part(one, two):
        total = dot(tok[:, :width], one[...], NN) + dot(tok[:, width:], two[...], NN)
        out[...] = total.astype(BF16)

    @pl.when(step < pl.num_programs(0) // 2)
    def _():
        part(gate_a, gate_b)

    @pl.when(step >= pl.num_programs(0) // 2)
    def _():
        part(up_a, up_b)


def gate_up_product(index, tok, gate_a, gate_b, up_a, up_b):
    rows, depth = tok.shape
    width, cols = gate_a.shape
    tile = 256
    steps = cols // tile
    first = pl.BlockSpec((width, tile), lambda j, _: (0, jnp.minimum(j, steps - 1)))
    second = pl.BlockSpec((width, tile), lambda j, _: (0, jnp.maximum(j - steps, 0)))
    return call(
        gate_up_kernel,
        (2 * steps,),
        [whole(tok.shape), first, first, second, second],
        pl.BlockSpec((rows, tile), lambda j, _: (0, j)),
        jax.ShapeDtypeStruct((rows, 2 * cols), BF16),
        4 * rows * depth * cols,
    )(index, tok, gate_a, gate_b, up_a, up_b)


def hidden_term_kernel(index, own, behind, top, bottom, before, down_a, down_b, out, mine, other):
    step = pl.program_id(0)
    rows = own.shape[0]
    width = own.shape[1] // 2

    @pl.when(step == 0)
    def _():
        def store(block, first, value):
            start = pl.multiple_of(block * rows + first, rows // 2)
            mine[pl.ds(start, value.shape[0]), :] = value[:, :width]
            other[pl.ds(start, value.shape[0]), :] = value[:, width:]

        place(index[0], own, behind, top, bottom, before, store)

    total = dot(mine[...], down_a[...], NT) + dot(other[...], down_b[...], NT)
    out[...] = total.astype(BF16)


def hidden_term_product(index, blocks, down_a, down_b):
    rows, depth = blocks[0].shape
    cols, width = down_a.shape
    tile = 256
    weight = pl.BlockSpec((tile, width), lambda j, _: (j, 0))
    half = jax.ShapeDtypeStruct((4 * rows, width), BF16)
    return call(
        hidden_term_kernel,
        (cols // tile,),
        [whole(block.shape) for block in blocks] + [weight, weight],
        [pl.BlockSpec((4 * rows, tile), lambda j, _: (0, j)), whole(half.shape), whole(half.shape)],
        [jax.ShapeDtypeStruct((4 * rows, cols), BF16), half, half],
        8 * rows * depth * cols,
    )(index, *blocks, down_a, down_b)


def mixed_kernel(index, own, behind, top, bottom, before, down_a, down_b, out, hidden):
    step = pl.program_id(0)
    rows = own.shape[0]

    @pl.when(step == 0)
    def _():
        def store(block, first, value):
            start = pl.multiple_of(block * rows + first, rows // 2)
            hidden[pl.ds(start, value.shape[0]), :] = value[...]

        place(index[0], own, behind, top, bottom, before, store)

    @pl.when(step < pl.num_programs(0) // 2)
    def _():
        out[...] = dot(hidden[...], down_a[...], NN).astype(BF16)

    @pl.when(step >= pl.num_programs(0) // 2)
    def _():
        out[...] = dot(hidden[...], down_b[...], NN).astype(BF16)


def mixed_product(index, blocks, down_a, down_b):
    rows, depth = blocks[0].shape
    width = down_a.shape[1]
    tile = 512
    steps = width // tile
    shape = (4 * rows, depth)
    return call(
        mixed_kernel,
        (2 * steps,),
        [whole(block.shape) for block in blocks]
        + [
            pl.BlockSpec((depth, tile), lambda j, _: (0, jnp.minimum(j, steps - 1))),
            pl.BlockSpec((depth, tile), lambda j, _: (0, jnp.maximum(j - steps, 0))),
        ],
        [pl.BlockSpec((4 * rows, tile), lambda j, _: (0, j)), whole(shape)],
        [jax.ShapeDtypeStruct((4 * rows, 2 * width), BF16), jax.ShapeDtypeStruct(shape, BF16)],
        16 * rows * depth * width,
    )(index, *blocks, down_a, down_b)


def input_kernel(
    index, own, behind, top, bottom, before, gate_a, up_a, gate_b, up_b, out, pre_gate, pre_up
):
    step = pl.program_id(0)
    rows = own.shape[0]
    cols = own.shape[1] // 2

    @pl.when(step == 0)
    def _():
        def store(block, first, value):
            start = pl.multiple_of(block * rows + first, rows // 2)
            pre_gate[pl.ds(start, value.shape[0]), :] = value[:, :cols]
            pre_up[pl.ds(start, value.shape[0]), :] = value[:, cols:]

        place(index[0], own, behind, top, bottom, before, store)

    def part(gate, up):
        total = dot(pre_gate[...], gate[...], NT) + dot(pre_up[...], up[...], NT)
        out[...] = total.astype(BF16)

    @pl.when(step < pl.num_programs(0) // 2)
    def _():
        part(gate_a, up_a)

    @pl.when(step >= pl.num_programs(0) // 2)
    def _():
        part(gate_b, up_b)


def input_product(index, blocks, gate_a, up_a, gate_b, up_b):
    rows = blocks[0].shape[0]
    width, cols = gate_a.shape
    tile = 256
    steps = width // tile
    first = pl.BlockSpec((tile, cols), lambda j, _: (jnp.minimum(j, steps - 1), 0))
    second = pl.BlockSpec((tile, cols), lambda j, _: (jnp.maximum(j - steps, 0), 0))
    half = jax.ShapeDtypeStruct((4 * rows, cols), BF16)
    return call(
        input_kernel,
        (2 * steps,),
        [whole(block.shape) for block in blocks] + [first, first, second, second],
        [pl.BlockSpec((4 * rows, tile), lambda j, _: (0, j)), whole(half.shape), whole(half.shape)],
        [jax.ShapeDtypeStruct((4 * rows, 2 * width), BF16), half, half],
        32 * rows * cols * width,
    )(index, *blocks, gate_a, up_a, gate_b, up_b)


def total_of(terms):
    total = terms[0].astype(F32)
    for k in range(1, terms.shape[0]):
        total = total + terms[k].astype(F32)
    return total


def hidden_kernel(index, terms, gate_up, hidden):
    del index
    total = total_of(terms)
    cols = hidden.shape[1]
    gate, up = total[:, :cols], total[:, cols:]
    gate_up[...] = total
    hidden[...] = (gate * jax.nn.sigmoid(gate) * up).astype(BF16)


def hidden_of(index, terms):
    _, rows, cols = terms.shape
    return call(
        hidden_kernel,
        (1,),
        [whole(terms.shape)],
        [whole((rows, cols)), whole((rows, cols // 2))],
        [
            jax.ShapeDtypeStruct((rows, cols), F32),
            jax.ShapeDtypeStruct((rows, cols // 2), BF16),
        ],
        16 * rows * cols,
    )(index, terms)


def pre_kernel(index, terms, gate_up, out):
    del index
    hidden_grad = total_of(terms)
    cols = hidden_grad.shape[1]
    gate, up = gate_up[:, :cols], gate_up[:, cols:]
    sig = jax.nn.sigmoid(gate)
    out[:, :cols] = (hidden_grad * up * sig * (1.0 + gate * (1.0 - sig))).astype(BF16)
    out[:, cols:] = (hidden_grad * gate * sig).astype(BF16)


def pre_grads(index, terms, gate_up):
    return call(
        pre_kernel,
        (1,),
        [whole(terms.shape), whole(gate_up.shape)],
        whole(gate_up.shape),
        jax.ShapeDtypeStruct(gate_up.shape, BF16),
        16 * gate_up.size,
    )(index, terms, gate_up)


def sums_kernel(index, one, two, out):
    del index
    cols = one.shape[2]
    out[:, :cols] = total_of(one).astype(BF16)
    out[:, cols:] = total_of(two).astype(BF16)


def sums_of(index, one, two):
    _, rows, cols = one.shape
    return call(
        sums_kernel,
        (1,),
        [whole(one.shape), whole(two.shape)],
        whole((rows, 2 * cols)),
        jax.ShapeDtypeStruct((rows, 2 * cols), BF16),
        16 * rows * cols,
    )(index, one, two)


def body(tokens, gate_weight, up_weight, down_weight, out_grad):
    core = lax.axis_index("row") % NC
    x = (lax.axis_index("row") // NC).astype(jnp.int32).reshape(1)
    y = (lax.axis_index("col") % NY).astype(jnp.int32).reshape(1)
    half = tokens.shape[0] // NC
    width = tokens.shape[1]

    def halves(value):
        mine = lax.dynamic_slice_in_dim(value, core * half, half, 0)
        other = lax.dynamic_slice_in_dim(value, (1 - core) * half, half, 0)
        return jnp.concatenate([mine, swap_core(other)], axis=1)

    def join(value):
        mine = value[:, :width]
        got = swap_core(value[:, width:])
        first = jnp.where(core == 0, mine, got)
        second = jnp.where(core == 0, got, mine)
        return jnp.concatenate([first, second], axis=0)

    both = jnp.concatenate([halves(tokens), halves(out_grad)], axis=1)
    gate_other = swap_core(gate_weight)
    up_other = swap_core(up_weight)
    down_other = swap_core(down_weight)

    both_z = share(both, "col", Z_GROUPS)
    tok = share(both_z[:, : 2 * width], "col", Y_GROUPS)
    grad_z = after(both_z[:, 2 * width :], tok)
    grad_blocks = ring_blocks(grad_z, "col", Y_UP, Y_DOWN)

    gate_up_term = gate_up_product(y, tok, gate_weight, gate_other, up_weight, up_other)
    gate_up, hidden_own = hidden_of(y, exchange(gate_up_term, "row", X_GROUPS))
    hidden_term, grad_mine, grad_other = hidden_term_product(y, grad_blocks, down_weight, down_other)
    pre_own = pre_grads(y, exchange(hidden_term, "row", X_GROUPS), gate_up)

    hidden_blocks = ring_blocks(hidden_own, "row", X_UP, X_DOWN)
    mixed_term, hidden = mixed_product(x, hidden_blocks, down_weight, down_other)
    pre_blocks = ring_blocks(pre_own, "row", X_UP, X_DOWN)
    input_term, pre_gate, pre_up = input_product(
        x, pre_blocks, gate_weight, up_weight, gate_other, up_other
    )
    mixed_y = exchange(mixed_term, "col", Y_GROUPS)
    input_y = exchange(input_term, "col", Y_GROUPS)
    sums = exchange(sums_of(y, mixed_y, input_y), "col", Z_GROUPS).astype(F32).sum(0).astype(BF16)
    mixed = join(sums[:, : 2 * width])
    input_grad = join(sums[:, 2 * width :])

    def all_tokens(value):
        return jnp.concatenate([value, swap_core(value)], axis=0)

    tok_rows = jnp.concatenate([tok[:, :width], swap_core(tok[:, width:])], axis=0)
    grad_rows = jnp.concatenate([grad_mine, swap_core(grad_other)], axis=0)
    down_grad = dot(all_tokens(hidden), grad_rows, TN).astype(BF16)
    gate_grad = dot(tok_rows, all_tokens(pre_gate), TN).astype(BF16)
    up_grad = dot(tok_rows, all_tokens(pre_up), TN).astype(BF16)
    return (mixed, input_grad, gate_grad, up_grad, down_grad)


def solution(mesh):
    in_specs = (P("col", "row"), P("row", "col"), P("row", "col"), P("col", "row"), P("col", "row"))
    out_specs = (
        P("col", "row"),
        P("col", "row"),
        P("row", "col"),
        P("row", "col"),
        P("col", "row"),
    )
    return jax.shard_map(body, mesh=mesh, in_specs=in_specs, out_specs=out_specs, check_vma=False)
```

time: 246 us -> 248 us (level)
  blocking collectives: 81.2 us -> 22.5 us
  waiting for transfers between devices: 38.5 us -> 91 us
  Pallas kernels: 0 us -> 29.5 us
  matrix products: 39.7 us -> 14.5 us
  other arithmetic: 10.6 us -> 2.67 us
  starting transfers between devices: 58.3 us -> 66.1 us
  local copies, waits for them, and re-layouts: 16.3 us -> 19.7 us
    all_gather x4 -> x0, blocking collectives: 58.6 us -> none  [the longest x3 37.4 us: gather_x(): lax.all_gather(value, 'row', axis=0, axis_index_groups=X_GROUPS, tiled=True)]
    ppermute x0 -> x12, waiting for transfers between devices: none -> 34.4 us  [the longest x3 22.9 us: ring_blocks(): before = lax.ppermute(own, axis, up)]
    pallas_call x0 -> x7, Pallas kernels: none -> 29.5 us  [the longest x1 9.37 us: input_product(): call(input_kernel, (2 * steps,), [whole(block.shape) for block in blocks]...]
    dot_general x7 -> x3, matrix products: 39.7 us -> 14.5 us  [dot(): return lax.dot_general(left, right, dims, preferred_element_type=F32)]
    all_to_all x7 -> x6, waiting for transfers between devices: 36.1 us -> 53.6 us  [exchange(): lax.all_to_all(value, axis, 0, 0, axis_index_groups=groups, tiled=True)]
    ppermute x0 -> x12, starting transfers between devices: none -> 16.9 us  [the longest x3 8.13 us: ring_blocks(): bottom = lax.ppermute(behind[half:], axis, down)]
    ppermute x11 -> x12, starting transfers between devices: 29.4 us -> 21.9 us  [swap_core(): return lax.ppermute(value, 'row', CORE_PAIRS)]
    unnamed x10 -> x28, local copies, waits for them, and re-layouts: 5.98 us -> 12.5 us
  transfers between devices with their start and end apart: 18 -> 30, of which waited for: 7 -> 14; matrix products, arithmetic and copies ran while one was open for 21% -> 9% of each run, Pallas kernels for 0% -> 11%
where the time goes in v2:
time: 248 us; the launch traced here: 247 us
  waiting for transfers between devices  91 us (37%)
  starting transfers between devices  66.1 us (27%)
  Pallas kernels  29.5 us (12%)
  blocking collectives  22.5 us (9%)
  local copies, waits for them, and re-layouts  19.7 us (8%)
  matrix products  14.5 us (6%)
  other arithmetic  2.67 us (1%)
    all_to_all x6, waiting for transfers between devices, exchange(): lax.all_to_all(value, axis, 0, 0, axis_index_groups=groups, tiled=True)  53.6 us
    all_to_all x6, starting transfers between devices, exchange(): lax.all_to_all(value, axis, 0, 0, axis_index_groups=groups, tiled=True)  27.3 us
    ppermute x3, waiting for transfers between devices, ring_blocks(): before = lax.ppermute(own, axis, up)  22.9 us
    all_to_all x1, blocking collectives, exchange(): lax.all_to_all(value, axis, 0, 0, axis_index_groups=groups, tiled=True)  22.5 us
    ppermute x12, starting transfers between devices, swap_core(): return lax.ppermute(value, 'row', CORE_PAIRS)  21.9 us
    dot_general x3, matrix products, dot(): return lax.dot_general(left, right, dims, preferred_element_type=F32)  14.5 us
    unnamed x28, local copies, waits for them, and re-layouts  12.5 us
    ppermute x3, waiting for transfers between devices, ring_blocks(): top = lax.ppermute(before[:half], axis, up)  11.2 us
  transfers between devices with their start and end apart: 30, of which 14 were waited for; matrix products, arithmetic and copies ran while one was open for 9% of the time, Pallas kernels for 11%

profile of v2, /device:TPU:1, one launch (start us, length us, event | category | flops | bytes accessed | tf_op | source)
XLA Modules:
  0.0 246.9 jit_solution(17991588612998442426)
XLA Ops:
  0.7 0.8 constant_dynamic-slice_fusion.3
  1.4 3.2 %collective-permute-start = (bf16[16,1024]{1,0:T(8,128)(2,1)S(1)}, bf16[16,1024]{1,0:T(8,128)(2,1)S(1)}, u32[]{:S(2)}, u32[]{:S(2)}) collective-permute-start(bf16[16,1024]{1,0:T(8,128)(2,1)S(1)} %get-tuple-element.37), channel_id=1, source_target_pairs={{0,32},{32,0},{64,96},{96,64},{128,160},{160,128},{192,224},{224,1... | collective-permute-start | bytes 98312 | tf_op jit(solution)/shard_map/ppermute | solution.py:32
  4.7 0.8 constant_dynamic-slice_fusion.1
  5.5 1.1 collective-permute-done.1
  6.7 1.1 tile.4
  7.8 6.4 %all-to-all-start = ((bf16[8,16,4096]{2,1,0:T(8,128)(2,1)}), bf16[8,16,4096]{2,1,0:T(8,128)(2,1)S(1)}, u32[]{:S(2)}, u32[]{:S(2)}) async-start(bf16[8,16,4096]{2,1,0:T(8,128)(2,1)} %tile.4), calls=%async_computation | async-start | bytes 2097152 | tf_op jit(solution)/shard_map/all_to_all | solution.py:37
  14.2 0.4 collective-permute-start.2
  14.7 28.7 %all-to-all-done = bf16[8,16,4096]{2,1,0:T(8,128)(2,1)S(1)} async-done(((bf16[8,16,4096]{2,1,0:T(8,128)(2,1)}), bf16[8,16,4096]{2,1,0:T(8,128)(2,1)S(1)}, u32[]{:S(2)}, u32[]{:S(2)}) %all-to-all-start) | async-done | bytes 1048608 | tf_op jit(solution)/shard_map/all_to_all | solution.py:37
  43.5 1.6 tile.5
  45.2 4.2 %all-to-all-start.1 = ((bf16[4,128,2048]{2,1,0:T(8,128)(2,1)}), bf16[4,128,2048]{2,1,0:T(8,128)(2,1)S(1)}, u32[]{:S(2)}, u32[]{:S(2)}) async-start(bf16[4,128,2048]{2,1,0:T(8,128)(2,1)} %tile.5), calls=%async_computation.1 | async-start | bytes 4194304 | tf_op jit(solution)/shard_map/all_to_all | solution.py:37
  49.3 0.8 collective-permute-start.8
  50.1 24.9 %all-to-all-done.1 = bf16[4,128,2048]{2,1,0:T(8,128)(2,1)S(1)} async-done(((bf16[4,128,2048]{2,1,0:T(8,128)(2,1)}), bf16[4,128,2048]{2,1,0:T(8,128)(2,1)S(1)}, u32[]{:S(2)}, u32[]{:S(2)}) %all-to-all-start.1) | async-done | bytes 2097184 | tf_op jit(solution)/shard_map/all_to_all | solution.py:37
  75.0 7.1 %shard_map.92 = bf16[512,1536]{1,0:T(8,128)(2,1)S(1)} custom-call(s32[1]{0:T(128)} %bitcast.index, bf16[512,2048]{1,0:T(8,128)(2,1)S(1)} %bitcast.9, bf16[1024,768]{1,0:T(8,128)(2,1)} %gate_a.3, bf16[1024,768]{1,0:T(8,128)(2,1)} %collective-permute-done.2.gate_b, bf16[1024,768]{1,0:T(8,128)(2,1)} %up_a.3, bf16[1024,768]{1,0:T(8,128)(2,1)} %collective-permute-done.3.up_b), custom_call_target="tpu_custom_call" | custom-call | flops 3221225472 | bytes 10485760 | tf_op jit(solution)/shard_map/pallas_call | solution.py:114
  82.1 1.1 copy-done.2
  83.2 4.4 %all-to-all-start.2 = ((bf16[4,128,1536]{2,1,0:T(8,128)(2,1)}), bf16[4,128,1536]{2,1,0:T(8,128)(2,1)}, u32[]{:S(2)}, u32[]{:S(2)}) async-start(bf16[4,128,1536]{2,1,0:T(8,128)(2,1)} %bitcast.13), calls=%async_computation.2 | async-start | bytes 3145728 | tf_op jit(solution)/shard_map/all_to_all | solution.py:37
  87.6 0.4 collective-permute-start.10
  88.0 2.4 collective-permute-start.9
  90.4 10.4 %collective-permute-done.10.before = bf16[128,2048]{1,0:T(8,128)(2,1)S(1)} collective-permute-done((bf16[128,2048]{1,0:T(8,128)(2,1)S(1)}, bf16[128,2048]{1,0:T(8,128)(2,1)S(1)}, u32[]{:S(2)}, u32[]{:S(2)}) %collective-permute-start.10) | collective-permute-done | bytes 524320 | tf_op jit(solution)/shard_map/ppermute | solution.py:52
  100.9 2.7 %collective-permute-start.12 = (bf16[64,2048]{1,0:T(8,128)(2,1)S(1)}, bf16[64,2048]{1,0:T(8,128)(2,1)S(1)}, u32[]{:S(2)}, u32[]{:S(2)}) collective-permute-start(bf16[64,2048]{1,0:T(8,128)(2,1)S(1)} %slice.67), channel_id=1, source_target_pairs={{1,0},{2,1},{3,2},{0,3},{5,4},{6,5},{7,6},{4,7},{9,8},{10,9},{11,1... | collective-permute-start | bytes 786440 | tf_op jit(solution)/shard_map/ppermute | solution.py:55
  103.6 4.0 %collective-permute-done.11.top = bf16[64,2048]{1,0:T(8,128)(2,1)S(1)} collective-permute-done((bf16[64,2048]{1,0:T(8,128)(2,1)S(1)}, bf16[64,2048]{1,0:T(8,128)(2,1)S(1)}, u32[]{:S(2)}, u32[]{:S(2)}) %collective-permute-start.11) | collective-permute-done | bytes 262176 | tf_op jit(solution)/shard_map/ppermute | solution.py:54
  107.7 1.4 copy-done.6
  109.1 3.7 %shard_map.95 = (bf16[512,768]{1,0:T(8,128)(2,1)S(1)}, bf16[512,1024]{1,0:T(8,128)(2,1)S(1)}, bf16[512,1024]{1,0:T(8,128)(2,1)S(1)}) custom-call(s32[1]{0:T(128)} %bitcast.index, bf16[128,2048]{1,0:T(8,128)(2,1)S(1)} %get-tuple-element.18.own, bf16[128,2048]{1,0:T(8,128)(2,1)S(1)} %collective-permute-done.9.behind, ...), custom_call_target="tpu_custom_call" | custom-call | flops 1610612736 | bytes 10485760 | tf_op jit(solution)/shard_map/pallas_call | solution.py:148
  112.9 0.9 copy-done.3
  113.7 1.0 copy-done.8
  114.7 1.0 copy-done.11
  115.8 3.5 %all-to-all-start.4 = ((bf16[4,128,768]{2,1,0:T(8,128)(2,1)}), bf16[4,128,768]{2,1,0:T(8,128)(2,1)S(1)}, u32[]{:S(2)}, u32[]{:S(2)}) async-start(bf16[4,128,768]{2,1,0:T(8,128)(2,1)} %bitcast.14), calls=%async_computation.4 | async-start | bytes 1572864 | tf_op jit(solution)/shard_map/all_to_all | solution.py:37
  119.3 1.6 shard_map.93
  120.9 0.9 copy-done.4
  121.8 1.4 collective-permute-start.5
  123.2 1.3 collective-permute-start.4
  124.5 7.4 %collective-permute-done.5.before = bf16[128,768]{1,0:T(8,128)(2,1)S(1)} collective-permute-done((bf16[128,768]{1,0:T(8,128)(2,1)S(1)}, bf16[128,768]{1,0:T(8,128)(2,1)S(1)}, u32[]{:S(2)}, u32[]{:S(2)}) %collective-permute-start.5) | collective-permute-done | bytes 196640 | tf_op jit(solution)/shard_map/ppermute | solution.py:52
  131.9 0.6 slice.63
  132.5 0.6 slice.64
  133.2 2.7 %collective-permute-start.7 = (bf16[64,768]{1,0:T(8,128)(2,1)}, bf16[64,768]{1,0:T(8,128)(2,1)}, u32[]{:S(2)}, u32[]{:S(2)}) collective-permute-start(bf16[64,768]{1,0:T(8,128)(2,1)} %slice.64), channel_id=1, source_target_pairs={{64,0},{96,32},{128,64},{160,96},{192,128},{224,160},{0,192},{32,2... | collective-permute-start | bytes 294920 | tf_op jit(solution)/shard_map/ppermute | solution.py:55
  135.9 1.7 collective-permute-done.6.top
  137.8 1.4 copy-done.7
  139.2 4.3 %shard_map.94 = (bf16[512,2048]{1,0:T(8,128)(2,1)S(1)}, bf16[512,768]{1,0:T(8,128)(2,1)S(1)}) custom-call(s32[1]{0:T(128)} %bitcast.1.index, bf16[128,768]{1,0:T(8,128)(2,1)S(1)} %get-tuple-element.16.own, bf16[128,768]{1,0:T(8,128)(2,1)S(1)} %collective-permute-done.4.behind, bf16[64,768]{1,0:T(8,128)(2,1)} %collective-permute-done.6.top, ...), custom_call_target="tpu_custom_call" | custom-call | flops 1610612736 | bytes 10485760 | tf_op jit(solution)/shard_map/pallas_call | solution.py:185
  143.6 1.4 copy-done
  144.9 0.9 copy-done.10
  145.8 4.5 %all-to-all-start.3 = ((bf16[4,128,2048]{2,1,0:T(8,128)(2,1)}), bf16[4,128,2048]{2,1,0:T(8,128)(2,1)}, u32[]{:S(2)}, u32[]{:S(2)}) async-start(bf16[4,128,2048]{2,1,0:T(8,128)(2,1)} %bitcast.11), calls=%async_computation.3 | async-start | bytes 4194304 | tf_op jit(solution)/shard_map/all_to_all | solution.py:37
  150.3 1.1 copy-done.5
  151.8 3.1 %collective-permute-start.13 = (bf16[128,1536]{1,0:T(8,128)(2,1)S(1)}, bf16[128,1536]{1,0:T(8,128)(2,1)S(1)}, u32[]{:S(2)}, u32[]{:S(2)}) collective-permute-start(bf16[128,1536]{1,0:T(8,128)(2,1)S(1)} %shard_map.96.own), channel_id=1, source_target_pairs={{64,0},{96,32},{128,64},{160,96},{192,128},{224,160},{0,192},{32,2... | collective-permute-start | bytes 1179656 | tf_op jit(solution)/shard_map/ppermute | solution.py:53
  154.9 5.1 %collective-permute-done.14.before = bf16[128,1536]{1,0:T(8,128)(2,1)S(1)} collective-permute-done((bf16[128,1536]{1,0:T(8,128)(2,1)S(1)}, bf16[128,1536]{1,0:T(8,128)(2,1)S(1)}, u32[]{:S(2)}, u32[]{:S(2)}) %collective-permute-start.14) | collective-permute-done | bytes 393248 | tf_op jit(solution)/shard_map/ppermute | solution.py:52
  160.1 2.7 %collective-permute-start.16 = (bf16[64,1536]{1,0:T(8,128)(2,1)S(1)}, bf16[64,1536]{1,0:T(8,128)(2,1)S(1)}, u32[]{:S(2)}, u32[]{:S(2)}) collective-permute-start(bf16[64,1536]{1,0:T(8,128)(2,1)S(1)} %slice.69), channel_id=1, source_target_pairs={{64,0},{96,32},{128,64},{160,96},{192,128},{224,160},{0,192},{32,2... | collective-permute-start | bytes 589832 | tf_op jit(solution)/shard_map/ppermute | solution.py:55
  162.8 5.5 %collective-permute-done.15.top = bf16[64,1536]{1,0:T(8,128)(2,1)S(1)} collective-permute-done((bf16[64,1536]{1,0:T(8,128)(2,1)S(1)}, bf16[64,1536]{1,0:T(8,128)(2,1)S(1)}, u32[]{:S(2)}, u32[]{:S(2)}) %collective-permute-start.15) | collective-permute-done | bytes 196640 | tf_op jit(solution)/shard_map/ppermute | solution.py:54
  168.4 9.4 %shard_map.97 = (bf16[512,2048]{1,0:T(8,128)(2,1)S(1)}, bf16[512,768]{1,0:T(8,128)(2,1)}, bf16[512,768]{1,0:T(8,128)(2,1)}) custom-call(s32[1]{0:T(128)} %bitcast.1.index, bf16[128,1536]{1,0:T(8,128)(2,1)S(1)} %shard_map.96.own, bf16[128,1536]{1,0:T(8,128)(2,1)S(1)} %collective-permute-done.13.behind, bf16[64,1536]{1,0:T(8,128)(2,1)S(1)} %collective-permute-done.15.top, ...), custom_call_target="tpu_custom_call" | custom-call | flops 3221225472 | bytes 10485760 | tf_op jit(solution)/shard_map/pallas_call | solution.py:236
  177.7 1.4 copy-done.1
  179.1 22.5 %all_to_all.62.two = bf16[4,128,2048]{2,1,0:T(8,128)(2,1)S(1)} all-to-all(bf16[4,128,2048]{2,1,0:T(8,128)(2,1)} %bitcast.12), channel_id=1, replica_groups={{0,1,2,3},{4,5,6,7},{8,9,10,11},{12,13,14,15},{16,17,18,19},{20,21,22,2..., dimensions={0} | all-to-all | bytes 4194304 | tf_op jit(solution)/shard_map/all_to_all | solution.py:37
  201.6 3.1 %shard_map.98 = bf16[128,4096]{1,0:T(8,128)(2,1)} custom-call(s32[1]{0:T(128)} %bitcast.index, bf16[4,128,2048]{2,1,0:T(8,128)(2,1)} %all-to-all-done.3.one, bf16[4,128,2048]{2,1,0:T(8,128)(2,1)S(1)} %all_to_all.62.two), custom_call_target="tpu_custom_call" | custom-call | flops 4194304 | bytes 10485760 | tf_op jit(solution)/shard_map/pallas_call | solution.py:307
  204.6 4.4 %all-to-all-start.6 = ((bf16[8,16,4096]{2,1,0:T(8,128)(2,1)}), bf16[8,16,4096]{2,1,0:T(8,128)(2,1)}, u32[]{:S(2)}, u32[]{:S(2)}) async-start(bf16[8,16,4096]{2,1,0:T(8,128)(2,1)} %bitcast.8), calls=%async_computation.6 | async-start | bytes 2097152 | tf_op jit(solution)/shard_map/all_to_all | solution.py:37
  209.0 9.2 %collective-permute-start.23 = (bf16[512,1024]{1,0:T(8,128)(2,1)S(1)}, bf16[512,1024]{1,0:T(8,128)(2,1)}, u32[]{:S(2)}, u32[]{:S(2)}) collective-permute-start(bf16[512,1024]{1,0:T(8,128)(2,1)S(1)} %copy-done.9), channel_id=1, source_target_pairs={{0,32},{32,0},{64,96},{96,64},{128,160},{160,128},{192,224},{224,1... | collective-permute-start | bytes 3145736 | tf_op jit(solution)/shard_map/ppermute | solution.py:32
  218.3 1.5 fusion.19
  219.9 0.4 collective-permute-start.19
  220.4 0.4 collective-permute-start.20
  220.8 0.4 collective-permute-done.23
  221.1 0.9 collective-permute-done.22
  222.0 5.1 %fusion.4 = bf16[768,1024]{1,0:T(8,128)(2,1)} fusion(bf16[512,1024]{1,0:T(8,128)(2,1)} %collective-permute-done.23, bf16[512,1024]{1,0:T(8,128)(2,1)} %copy-done.11, bf16[512,768]{1,0:T(8,128)(2,1)} %collective-permute-done.22, bf16[512,768]{1,0:T(8,128)(2,1)} %copy-done.10), kind=kOutput, calls=%fused_computation.5 | convolution fusion | flops 1618739200 | bytes 5242880 | tf_op jit(solution)/shard_map/dot_general | solution.py:28
  227.1 4.8 %convolution_convert_fusion = bf16[1024,768]{1,0:T(8,128)(2,1)} fusion(bf16[512,768]{1,0:T(8,128)(2,1)} %collective-permute-done.21, bf16[512,768]{1,0:T(8,128)(2,1)} %get-tuple-element.23, bf16[512,1024]{1,0:T(8,128)(2,1)S(1)} %collective-permute-done.19, bf16[512,1024]{1,0:T(8,128)(2,1)S(1)} %copy-done.12), kind=kOutput, calls=%fused_computation.6 | convolution fusion | flops 1618739200 | bytes 5242880 | tf_op jit(solution)/shard_map/dot_general | solution.py:28
  231.8 1.4 reduce_sum.12
  233.2 7.0 %collective-permute-start.18 = (bf16[16,1024]{1,0:T(8,128)(2,1)S(1)}, bf16[16,1024]{1,0:T(8,128)(2,1)S(1)}, u32[]{:S(2)}, u32[]{:S(2)}) collective-permute-start(bf16[16,1024]{1,0:T(8,128)(2,1)S(1)} %slice.73), channel_id=1, source_target_pairs={{0,32},{32,0},{64,96},{96,64},{128,160},{160,128},{192,224},{224,1... | collective-permute-start | bytes 98312 | tf_op jit(solution)/shard_map/ppermute | solution.py:32
  240.3 4.7 %convolution_convert_fusion.1 = bf16[1024,768]{1,0:T(8,128)(2,1)} fusion(bf16[512,768]{1,0:T(8,128)(2,1)} %collective-permute-done.20, bf16[512,768]{1,0:T(8,128)(2,1)} %get-tuple-element.22, bf16[512,1024]{1,0:T(8,128)(2,1)} %copy-done.13, bf16[512,1024]{1,0:T(8,128)(2,1)S(1)} %copy-done.12), kind=kOutput, calls=%fused_computation.7 | convolution fusion | flops 1618739200 | bytes 5242880 | tf_op jit(solution)/shard_map/dot_general | solution.py:28
  245.1 0.6 pad_maximum_fusion.5
  245.7 0.6 collective-permute-done.17
  246.3 0.6 pad_maximum_fusion.4
  (54 shorter events, 1.5 us)
Async XLA Ops:
  1.4 4.1 %collective-permute-start = (bf16[16,1024]{1,0:T(8,128)(2,1)S(1)}, bf16[16,1024]{1,0:T(8,128)(2,1)S(1)}, u32[]{:S(2)}, u32[]{:S(2)}) collective-permute-start(bf16[16,1024]{1,0:T(8,128)(2,1)S(1)} %get-tuple-element.37), channel_id=1, source_target_pairs={{0,32},{32,0},{64,96},{96,64},{128,160},{160,128},{192,224},{224,1... | collective-permute-start | bytes 98312 | tf_op jit(solution)/shard_map/ppermute | solution.py:32
  5.5 1.2 collective-permute-start.1
  7.8 35.7 %all-to-all-start = ((bf16[8,16,4096]{2,1,0:T(8,128)(2,1)}), bf16[8,16,4096]{2,1,0:T(8,128)(2,1)S(1)}, u32[]{:S(2)}, u32[]{:S(2)}) async-start(bf16[8,16,4096]{2,1,0:T(8,128)(2,1)} %tile.4), calls=%async_computation | async-start | bytes 2097152 | tf_op jit(solution)/shard_map/all_to_all | solution.py:37
  14.2 35.9 %collective-permute-start.2 = (bf16[1024,768]{1,0:T(8,128)(2,1)}, bf16[1024,768]{1,0:T(8,128)(2,1)}, u32[]{:S(2)}, u32[]{:S(2)}) collective-permute-start(bf16[1024,768]{1,0:T(8,128)(2,1)} %gate_a.3), channel_id=1, source_target_pairs={{0,32},{32,0},{64,96},{96,64},{128,160},{160,128},{192,224},{224,1... | collective-permute-start | bytes 4718600 | tf_op jit(solution)/shard_map/ppermute | solution.py:32
  14.6 35.5 %collective-permute-start.3 = (bf16[1024,768]{1,0:T(8,128)(2,1)}, bf16[1024,768]{1,0:T(8,128)(2,1)}, u32[]{:S(2)}, u32[]{:S(2)}) collective-permute-start(bf16[1024,768]{1,0:T(8,128)(2,1)} %up_a.3), channel_id=1, source_target_pairs={{0,32},{32,0},{64,96},{96,64},{128,160},{160,128},{192,224},{224,1... | collective-permute-start | bytes 4718600 | tf_op jit(solution)/shard_map/ppermute | solution.py:32
  45.2 29.8 %all-to-all-start.1 = ((bf16[4,128,2048]{2,1,0:T(8,128)(2,1)}), bf16[4,128,2048]{2,1,0:T(8,128)(2,1)S(1)}, u32[]{:S(2)}, u32[]{:S(2)}) async-start(bf16[4,128,2048]{2,1,0:T(8,128)(2,1)} %tile.5), calls=%async_computation.1 | async-start | bytes 4194304 | tf_op jit(solution)/shard_map/all_to_all | solution.py:37
  49.3 54.3 %collective-permute-start.8 = (bf16[768,1024]{1,0:T(8,128)(2,1)}, bf16[768,1024]{1,0:T(8,128)(2,1)}, u32[]{:S(2)}, u32[]{:S(2)}) collective-permute-start(bf16[768,1024]{1,0:T(8,128)(2,1)} %down_a.3), channel_id=1, source_target_pairs={{0,32},{32,0},{64,96},{96,64},{128,160},{160,128},{192,224},{224,1... | collective-permute-start | bytes 4718600 | tf_op jit(solution)/shard_map/ppermute | solution.py:32
  82.1 1.1 copy-start.2
  83.2 32.5 %all-to-all-start.2 = ((bf16[4,128,1536]{2,1,0:T(8,128)(2,1)}), bf16[4,128,1536]{2,1,0:T(8,128)(2,1)}, u32[]{:S(2)}, u32[]{:S(2)}) async-start(bf16[4,128,1536]{2,1,0:T(8,128)(2,1)} %bitcast.13), calls=%async_computation.2 | async-start | bytes 3145728 | tf_op jit(solution)/shard_map/all_to_all | solution.py:37
  87.6 13.2 %collective-permute-start.10 = (bf16[128,2048]{1,0:T(8,128)(2,1)S(1)}, bf16[128,2048]{1,0:T(8,128)(2,1)S(1)}, u32[]{:S(2)}, u32[]{:S(2)}) collective-permute-start(bf16[128,2048]{1,0:T(8,128)(2,1)S(1)} %get-tuple-element.18.own), channel_id=1, source_target_pairs={{0,1},{1,2},{2,3},{3,0},{4,5},{5,6},{6,7},{7,4},{8,9},{9,10},{10,1... | collective-permute-start | bytes 1572872 | tf_op jit(solution)/shard_map/ppermute | solution.py:52
  88.0 12.9 %collective-permute-start.9 = (bf16[128,2048]{1,0:T(8,128)(2,1)S(1)}, bf16[128,2048]{1,0:T(8,128)(2,1)S(1)}, u32[]{:S(2)}, u32[]{:S(2)}) collective-permute-start(bf16[128,2048]{1,0:T(8,128)(2,1)S(1)} %get-tuple-element.18.own), channel_id=1, source_target_pairs={{1,0},{2,1},{3,2},{0,3},{5,4},{6,5},{7,6},{4,7},{9,8},{10,9},{11,1... | collective-permute-start | bytes 1572872 | tf_op jit(solution)/shard_map/ppermute | solution.py:53
  100.8 6.9 %collective-permute-start.11 = (bf16[64,2048]{1,0:T(8,128)(2,1)S(1)}, bf16[64,2048]{1,0:T(8,128)(2,1)S(1)}, u32[]{:S(2)}, u32[]{:S(2)}) collective-permute-start(bf16[64,2048]{1,0:T(8,128)(2,1)S(1)} %slice.66), channel_id=1, source_target_pairs={{0,1},{1,2},{2,3},{3,0},{4,5},{5,6},{6,7},{7,4},{8,9},{9,10},{10,1... | collective-permute-start | bytes 786440 | tf_op jit(solution)/shard_map/ppermute | solution.py:54
  100.9 6.8 %collective-permute-start.12 = (bf16[64,2048]{1,0:T(8,128)(2,1)S(1)}, bf16[64,2048]{1,0:T(8,128)(2,1)S(1)}, u32[]{:S(2)}, u32[]{:S(2)}) collective-permute-start(bf16[64,2048]{1,0:T(8,128)(2,1)S(1)} %slice.67), channel_id=1, source_target_pairs={{1,0},{2,1},{3,2},{0,3},{5,4},{6,5},{7,6},{4,7},{9,8},{10,9},{11,1... | collective-permute-start | bytes 786440 | tf_op jit(solution)/shard_map/ppermute | solution.py:55
  107.7 1.4 copy-start.6
  112.9 0.9 copy-start.3
  113.7 1.0 copy-start.8
  114.7 1.0 copy-start.11
  115.8 30.1 %all-to-all-start.4 = ((bf16[4,128,768]{2,1,0:T(8,128)(2,1)}), bf16[4,128,768]{2,1,0:T(8,128)(2,1)S(1)}, u32[]{:S(2)}, u32[]{:S(2)}) async-start(bf16[4,128,768]{2,1,0:T(8,128)(2,1)} %bitcast.14), calls=%async_computation.4 | async-start | bytes 1572864 | tf_op jit(solution)/shard_map/all_to_all | solution.py:37
  120.9 0.9 copy-start.4
  121.8 10.1 %collective-permute-start.5 = (bf16[128,768]{1,0:T(8,128)(2,1)S(1)}, bf16[128,768]{1,0:T(8,128)(2,1)S(1)}, u32[]{:S(2)}, u32[]{:S(2)}) collective-permute-start(bf16[128,768]{1,0:T(8,128)(2,1)S(1)} %get-tuple-element.16.own), channel_id=1, source_target_pairs={{0,64},{32,96},{64,128},{96,160},{128,192},{160,224},{192,0},{224,... | collective-permute-start | bytes 589832 | tf_op jit(solution)/shard_map/ppermute | solution.py:52
  123.2 9.3 %collective-permute-start.4 = (bf16[128,768]{1,0:T(8,128)(2,1)S(1)}, bf16[128,768]{1,0:T(8,128)(2,1)S(1)}, u32[]{:S(2)}, u32[]{:S(2)}) collective-permute-start(bf16[128,768]{1,0:T(8,128)(2,1)S(1)} %get-tuple-element.16.own), channel_id=1, source_target_pairs={{64,0},{96,32},{128,64},{160,96},{192,128},{224,160},{0,192},{32,2... | collective-permute-start | bytes 589832 | tf_op jit(solution)/shard_map/ppermute | solution.py:53
  132.5 5.0 %collective-permute-start.6 = (bf16[64,768]{1,0:T(8,128)(2,1)}, bf16[64,768]{1,0:T(8,128)(2,1)}, u32[]{:S(2)}, u32[]{:S(2)}) collective-permute-start(bf16[64,768]{1,0:T(8,128)(2,1)} %slice.63), channel_id=1, source_target_pairs={{0,64},{32,96},{64,128},{96,160},{128,192},{160,224},{192,0},{224,... | collective-permute-start | bytes 294920 | tf_op jit(solution)/shard_map/ppermute | solution.py:54
  133.2 4.6 %collective-permute-start.7 = (bf16[64,768]{1,0:T(8,128)(2,1)}, bf16[64,768]{1,0:T(8,128)(2,1)}, u32[]{:S(2)}, u32[]{:S(2)}) collective-permute-start(bf16[64,768]{1,0:T(8,128)(2,1)} %slice.64), channel_id=1, source_target_pairs={{64,0},{96,32},{128,64},{160,96},{192,128},{224,160},{0,192},{32,2... | collective-permute-start | bytes 294920 | tf_op jit(solution)/shard_map/ppermute | solution.py:55
  137.8 1.4 copy-start.7
  143.6 1.4 copy-start
  144.9 0.9 copy-start.10
  145.8 33.3 %all-to-all-start.3 = ((bf16[4,128,2048]{2,1,0:T(8,128)(2,1)}), bf16[4,128,2048]{2,1,0:T(8,128)(2,1)}, u32[]{:S(2)}, u32[]{:S(2)}) async-start(bf16[4,128,2048]{2,1,0:T(8,128)(2,1)} %bitcast.11), calls=%async_computation.3 | async-start | bytes 4194304 | tf_op jit(solution)/shard_map/all_to_all | solution.py:37
  150.3 1.1 copy-start.5
  151.7 8.3 %collective-permute-start.14 = (bf16[128,1536]{1,0:T(8,128)(2,1)S(1)}, bf16[128,1536]{1,0:T(8,128)(2,1)S(1)}, u32[]{:S(2)}, u32[]{:S(2)}) collective-permute-start(bf16[128,1536]{1,0:T(8,128)(2,1)S(1)} %shard_map.96.own), channel_id=1, source_target_pairs={{0,64},{32,96},{64,128},{96,160},{128,192},{160,224},{192,0},{224,... | collective-permute-start | bytes 1179656 | tf_op jit(solution)/shard_map/ppermute | solution.py:52
  151.8 8.3 %collective-permute-start.13 = (bf16[128,1536]{1,0:T(8,128)(2,1)S(1)}, bf16[128,1536]{1,0:T(8,128)(2,1)S(1)}, u32[]{:S(2)}, u32[]{:S(2)}) collective-permute-start(bf16[128,1536]{1,0:T(8,128)(2,1)S(1)} %shard_map.96.own), channel_id=1, source_target_pairs={{64,0},{96,32},{128,64},{160,96},{192,128},{224,160},{0,192},{32,2... | collective-permute-start | bytes 1179656 | tf_op jit(solution)/shard_map/ppermute | solution.py:53
  160.0 8.4 %collective-permute-start.15 = (bf16[64,1536]{1,0:T(8,128)(2,1)S(1)}, bf16[64,1536]{1,0:T(8,128)(2,1)S(1)}, u32[]{:S(2)}, u32[]{:S(2)}) collective-permute-start(bf16[64,1536]{1,0:T(8,128)(2,1)S(1)} %slice.68), channel_id=1, source_target_pairs={{0,64},{32,96},{64,128},{96,160},{128,192},{160,224},{192,0},{224,... | collective-permute-start | bytes 589832 | tf_op jit(solution)/shard_map/ppermute | solution.py:54
  160.1 8.3 %collective-permute-start.16 = (bf16[64,1536]{1,0:T(8,128)(2,1)S(1)}, bf16[64,1536]{1,0:T(8,128)(2,1)S(1)}, u32[]{:S(2)}, u32[]{:S(2)}) collective-permute-start(bf16[64,1536]{1,0:T(8,128)(2,1)S(1)} %slice.69), channel_id=1, source_target_pairs={{64,0},{96,32},{128,64},{160,96},{192,128},{224,160},{0,192},{32,2... | collective-permute-start | bytes 589832 | tf_op jit(solution)/shard_map/ppermute | solution.py:55
  177.7 1.4 copy-start.1
  204.6 4.4 %copy-start.9 = (bf16[512,1024]{1,0:T(8,128)(2,1)S(1)}, bf16[512,1024]{1,0:T(8,128)(2,1)}, u32[]{:S(2)}) copy-start(bf16[512,1024]{1,0:T(8,128)(2,1)} %copy-done.8) | copy-start | bytes 3145732
  204.6 27.2 %all-to-all-start.6 = ((bf16[8,16,4096]{2,1,0:T(8,128)(2,1)}), bf16[8,16,4096]{2,1,0:T(8,128)(2,1)}, u32[]{:S(2)}, u32[]{:S(2)}) async-start(bf16[8,16,4096]{2,1,0:T(8,128)(2,1)} %bitcast.8), calls=%async_computation.6 | async-start | bytes 2097152 | tf_op jit(solution)/shard_map/all_to_all | solution.py:37
  209.0 12.1 %collective-permute-start.23 = (bf16[512,1024]{1,0:T(8,128)(2,1)S(1)}, bf16[512,1024]{1,0:T(8,128)(2,1)}, u32[]{:S(2)}, u32[]{:S(2)}) collective-permute-start(bf16[512,1024]{1,0:T(8,128)(2,1)S(1)} %copy-done.9), channel_id=1, source_target_pairs={{0,32},{32,0},{64,96},{96,64},{128,160},{160,128},{192,224},{224,1... | collective-permute-start | bytes 3145736 | tf_op jit(solution)/shard_map/ppermute | solution.py:32
  218.2 3.8 %collective-permute-start.22 = (bf16[512,768]{1,0:T(8,128)(2,1)}, bf16[512,768]{1,0:T(8,128)(2,1)}, u32[]{:S(2)}, u32[]{:S(2)}) collective-permute-start(bf16[512,768]{1,0:T(8,128)(2,1)} %copy-done.10), channel_id=1, source_target_pairs={{0,32},{32,0},{64,96},{96,64},{128,160},{160,128},{192,224},{224,1... | collective-permute-start | bytes 2359304 | tf_op jit(solution)/shard_map/ppermute | solution.py:32
  219.9 7.2 %collective-permute-start.19 = (bf16[512,1024]{1,0:T(8,128)(2,1)}, bf16[512,1024]{1,0:T(8,128)(2,1)S(1)}, u32[]{:S(2)}, u32[]{:S(2)}) collective-permute-start(bf16[512,1024]{1,0:T(8,128)(2,1)} %get-tuple-element.28), channel_id=1, source_target_pairs={{0,32},{32,0},{64,96},{96,64},{128,160},{160,128},{192,224},{224,1... | collective-permute-start | bytes 3145736 | tf_op jit(solution)/shard_map/ppermute | solution.py:32
  220.3 6.8 %collective-permute-start.21 = (bf16[512,768]{1,0:T(8,128)(2,1)}, bf16[512,768]{1,0:T(8,128)(2,1)}, u32[]{:S(2)}, u32[]{:S(2)}) collective-permute-start(bf16[512,768]{1,0:T(8,128)(2,1)} %get-tuple-element.23), channel_id=1, source_target_pairs={{0,32},{32,0},{64,96},{96,64},{128,160},{160,128},{192,224},{224,1... | collective-permute-start | bytes 2359304 | tf_op jit(solution)/shard_map/ppermute | solution.py:32
  220.4 19.9 %collective-permute-start.20 = (bf16[512,768]{1,0:T(8,128)(2,1)}, bf16[512,768]{1,0:T(8,128)(2,1)}, u32[]{:S(2)}, u32[]{:S(2)}) collective-permute-start(bf16[512,768]{1,0:T(8,128)(2,1)} %get-tuple-element.22), channel_id=1, source_target_pairs={{0,32},{32,0},{64,96},{96,64},{128,160},{160,128},{192,224},{224,1... | collective-permute-start | bytes 2359304 | tf_op jit(solution)/shard_map/ppermute | solution.py:32
  222.0 5.1 %copy-start.12 = (bf16[512,1024]{1,0:T(8,128)(2,1)S(1)}, bf16[512,1024]{1,0:T(8,128)(2,1)}, u32[]{:S(2)}) copy-start(bf16[512,1024]{1,0:T(8,128)(2,1)} %get-tuple-element.27) | copy-start | bytes 3145732
  227.1 4.8 %copy-start.13 = (bf16[512,1024]{1,0:T(8,128)(2,1)}, bf16[512,1024]{1,0:T(8,128)(2,1)S(1)}, u32[]{:S(2)}) copy-start(bf16[512,1024]{1,0:T(8,128)(2,1)S(1)} %collective-permute-done.19) | copy-start | bytes 3145732
  233.2 11.7 %collective-permute-start.18 = (bf16[16,1024]{1,0:T(8,128)(2,1)S(1)}, bf16[16,1024]{1,0:T(8,128)(2,1)S(1)}, u32[]{:S(2)}, u32[]{:S(2)}) collective-permute-start(bf16[16,1024]{1,0:T(8,128)(2,1)S(1)} %slice.73), channel_id=1, source_target_pairs={{0,32},{32,0},{64,96},{96,64},{128,160},{160,128},{192,224},{224,1... | collective-permute-start | bytes 98312 | tf_op jit(solution)/shard_map/ppermute | solution.py:32
  245.0 1.3 collective-permute-start.17

commit v3 on v2

--- a/solution.py
+++ b/solution.py
@@ -13,8 +13,8 @@
 X_GROUPS = [[x * NC + c for x in range(NX)] for c in range(NC)]
 Y_GROUPS = [[z * NY + y for y in range(NY)] for z in range(NZ)]
 Z_GROUPS = [[z * NY + y for z in range(NZ)] for y in range(NY)]
-Y_UP = [(z * NY + y, z * NY + (y + 1) % NY) for z in range(NZ) for y in range(NY)]
-Y_DOWN = [(dst, src) for src, dst in Y_UP]
+Z_UP = [(z * NY + y, (z + 1) % NZ * NY + y) for z in range(NZ) for y in range(NY)]
+Z_DOWN = [(dst, src) for src, dst in Z_UP]
 X_UP = [(x * NC + c, (x + 1) % NX * NC + c) for x in range(NX) for c in range(NC)]
 X_DOWN = [(dst, src) for src, dst in X_UP]
 CORE_PAIRS = [(r, r ^ 1) for r in range(NX * NC)]
@@ -56,8 +56,23 @@
     return own, behind, top, bottom, before
 
 
+def ring_eight(own, axis, up, down):
+    half = own.shape[0] // 2
+    before, behind = [own], [own]
+    for _ in range(3):
+        before.append(lax.ppermute(before[-1], axis, up))
+        behind.append(lax.ppermute(behind[-1], axis, down))
+    top = lax.ppermute(before[3][:half], axis, up)
+    bottom = lax.ppermute(behind[3][half:], axis, down)
+    return own, behind[1], behind[2], behind[3], top, bottom, before[3], before[2], before[1]
+
+
 def whole(shape):
     return pl.BlockSpec(shape, lambda *_: (0,) * len(shape))
+
+
+def hbm(shape, dtype=BF16):
+    return pltpu.HBM(shape, dtype)
 
 
 def call(kernel, grid, in_specs, out_specs, out_shape, flops, scratch=(), limit=24):
@@ -86,13 +101,30 @@
     store(lax.rem(index + 3, 4), 0, before)
 
 
-def gate_up_kernel(index, tok, gate_a, gate_b, up_a, up_b, out):
-    del index
+def place_eight(index, blocks, store):
+    groups = blocks[0].shape[0] // 16
+    steps = (0, 1, 2, 3, 4, 4, 5, 6, 7)
+    for block, step in zip(blocks, steps):
+        z = lax.rem(index + step, NZ)
+        first = groups // 2 if block is blocks[5] else 0
+        for k in range(block.shape[0] // 16):
+            start = pl.multiple_of((first + k) * NZ * 16 + z * 16, 16)
+            store(start, block[k * 16 : (k + 1) * 16, :])
+
+
+def gate_up_kernel(index, tok_a, *refs):
+    blocks, (gate_a, gate_b, up_a, up_b, out, tok_b) = refs[:9], refs[9:]
     step = pl.program_id(0)
-    width = gate_a.shape[0]
+
+    @pl.when(step == 0)
+    def _():
+        def store(start, value):
+            tok_b[pl.ds(start, 16), :] = value
+
+        place_eight(index[0], blocks, store)
 
     def part(one, two):
-        total = dot(tok[:, :width], one[...], NN) + dot(tok[:, width:], two[...], NN)
+        total = dot(tok_a[...], one[...], NN) + dot(tok_b[...], two[...], NN)
         out[...] = total.astype(BF16)
 
     @pl.when(step < pl.num_programs(0) // 2)
@@ -104,8 +136,12 @@
         part(up_a, up_b)
 
 
-def gate_up_product(index, tok, gate_a, gate_b, up_a, up_b):
-    rows, depth = tok.shape
+def columns(rows, width, at):
+    return pl.BlockSpec((rows, width), lambda *_: (0, at))
+
+
+def gate_up_product(index, own, blocks, gate_a, gate_b, up_a, up_b):
+    rows = own.shape[0]
     width, cols = gate_a.shape
     tile = 256
     steps = cols // tile
@@ -114,45 +150,44 @@
     return call(
         gate_up_kernel,
         (2 * steps,),
-        [whole(tok.shape), first, first, second, second],
-        pl.BlockSpec((rows, tile), lambda j, _: (0, j)),
-        jax.ShapeDtypeStruct((rows, 2 * cols), BF16),
-        4 * rows * depth * cols,
-    )(index, tok, gate_a, gate_b, up_a, up_b)
-
-
-def hidden_term_kernel(index, own, behind, top, bottom, before, down_a, down_b, out, mine, other):
-    step = pl.program_id(0)
+        [columns(rows, width, 0)]
+        + [columns(block.shape[0], width, 0) for block in blocks]
+        + [first, first, second, second],
+        [pl.BlockSpec((rows, tile), lambda j, _: (0, j)), whole((rows, width))],
+        [hbm((rows, 2 * cols)), hbm((rows, width))],
+        8 * rows * width * cols,
+    )(index, own, *blocks, gate_a, gate_b, up_a, up_b)
+
+
+def hidden_term_kernel(index, grad_a, *refs):
+    blocks, (down_a, down_b, out, grad_b) = refs[:9], refs[9:]
+
+    @pl.when(pl.program_id(0) == 0)
+    def _():
+        def store(start, value):
+            grad_b[pl.ds(start, 16), :] = value
+
+        place_eight(index[0], blocks, store)
+
+    total = dot(grad_a[...], down_a[...], NT) + dot(grad_b[...], down_b[...], NT)
+    out[...] = total.astype(BF16)
+
+
+def hidden_term_product(index, own, blocks, down_a, down_b):
     rows = own.shape[0]
-    width = own.shape[1] // 2
-
-    @pl.when(step == 0)
-    def _():
-        def store(block, first, value):
-            start = pl.multiple_of(block * rows + first, rows // 2)
-            mine[pl.ds(start, value.shape[0]), :] = value[:, :width]
-            other[pl.ds(start, value.shape[0]), :] = value[:, width:]
-
-        place(index[0], own, behind, top, bottom, before, store)
-
-    total = dot(mine[...], down_a[...], NT) + dot(other[...], down_b[...], NT)
-    out[...] = total.astype(BF16)
-
-
-def hidden_term_product(index, blocks, down_a, down_b):
-    rows, depth = blocks[0].shape
     cols, width = down_a.shape
     tile = 256
     weight = pl.BlockSpec((tile, width), lambda j, _: (j, 0))
-    half = jax.ShapeDtypeStruct((4 * rows, width), BF16)
     return call(
         hidden_term_kernel,
         (cols // tile,),
-        [whole(block.shape) for block in blocks] + [weight, weight],
-        [pl.BlockSpec((4 * rows, tile), lambda j, _: (0, j)), whole(half.shape), whole(half.shape)],
-        [jax.ShapeDtypeStruct((4 * rows, cols), BF16), half, half],
-        8 * rows * depth * cols,
-    )(index, *blocks, down_a, down_b)
+        [columns(rows, width, 1)]
+        + [columns(block.shape[0], width, 1) for block in blocks]
+        + [weight, weight],
+        [pl.BlockSpec((rows, tile), lambda j, _: (0, j)), whole((rows, width))],
+        [hbm((rows, cols)), hbm((rows, width))],
+        4 * rows * width * cols,
+    )(index, own, *blocks, down_a, down_b)
 
 
 def mixed_kernel(index, own, behind, top, bottom, before, down_a, down_b, out, hidden):
@@ -191,7 +226,7 @@
             pl.BlockSpec((depth, tile), lambda j, _: (0, jnp.maximum(j - steps, 0))),
         ],
         [pl.BlockSpec((4 * rows, tile), lambda j, _: (0, j)), whole(shape)],
-        [jax.ShapeDtypeStruct((4 * rows, 2 * width), BF16), jax.ShapeDtypeStruct(shape, BF16)],
+        [hbm((4 * rows, 2 * width)), hbm(shape)],
         16 * rows * depth * width,
     )(index, *blocks, down_a, down_b)
 
@@ -232,13 +267,13 @@
     steps = width // tile
     first = pl.BlockSpec((tile, cols), lambda j, _: (jnp.minimum(j, steps - 1), 0))
     second = pl.BlockSpec((tile, cols), lambda j, _: (jnp.maximum(j - steps, 0), 0))
-    half = jax.ShapeDtypeStruct((4 * rows, cols), BF16)
+    half = hbm((4 * rows, cols))
     return call(
         input_kernel,
         (2 * steps,),
         [whole(block.shape) for block in blocks] + [first, first, second, second],
-        [pl.BlockSpec((4 * rows, tile), lambda j, _: (0, j)), whole(half.shape), whole(half.shape)],
-        [jax.ShapeDtypeStruct((4 * rows, 2 * width), BF16), half, half],
+        [pl.BlockSpec((4 * rows, tile), lambda j, _: (0, j))] + [whole((4 * rows, cols))] * 2,
+        [hbm((4 * rows, 2 * width)), half, half],
         32 * rows * cols * width,
     )(index, *blocks, gate_a, up_a, gate_b, up_b)
 
@@ -317,14 +352,14 @@
 def body(tokens, gate_weight, up_weight, down_weight, out_grad):
     core = lax.axis_index("row") % NC
     x = (lax.axis_index("row") // NC).astype(jnp.int32).reshape(1)
-    y = (lax.axis_index("col") % NY).astype(jnp.int32).reshape(1)
+    z = (lax.axis_index("col") // NY).astype(jnp.int32).reshape(1)
     half = tokens.shape[0] // NC
     width = tokens.shape[1]
 
     def halves(value):
         mine = lax.dynamic_slice_in_dim(value, core * half, half, 0)
         other = lax.dynamic_slice_in_dim(value, (1 - core) * half, half, 0)
-        return jnp.concatenate([mine, swap_core(other)], axis=1)
+        return mine, swap_core(other)
 
     def join(value):
         mine = value[:, :width]
@@ -333,41 +368,49 @@
         second = jnp.where(core == 0, got, mine)
         return jnp.concatenate([first, second], axis=0)
 
-    both = jnp.concatenate([halves(tokens), halves(out_grad)], axis=1)
+    tok_a, tok_b = halves(tokens)
+    grad_a, grad_b = halves(out_grad)
+    own = jnp.concatenate([tok_a, grad_a], axis=1)
+    other = jnp.concatenate([tok_b, grad_b], axis=1)
     gate_other = swap_core(gate_weight)
     up_other = swap_core(up_weight)
     down_other = swap_core(down_weight)
 
-    both_z = share(both, "col", Z_GROUPS)
-    tok = share(both_z[:, : 2 * width], "col", Y_GROUPS)
-    grad_z = after(both_z[:, 2 * width :], tok)
-    grad_blocks = ring_blocks(grad_z, "col", Y_UP, Y_DOWN)
-
-    gate_up_term = gate_up_product(y, tok, gate_weight, gate_other, up_weight, up_other)
-    gate_up, hidden_own = hidden_of(y, exchange(gate_up_term, "row", X_GROUPS))
-    hidden_term, grad_mine, grad_other = hidden_term_product(y, grad_blocks, down_weight, down_other)
-    pre_own = pre_grads(y, exchange(hidden_term, "row", X_GROUPS), gate_up)
+    other_y = share(other, "col", Y_GROUPS)
+    other_blocks = ring_eight(other_y, "col", Z_UP, Z_DOWN)
+    own_z = share(after(own, other_y), "col", Z_GROUPS)
+    own_all = share(after(own_z, other_blocks[1], other_blocks[8]), "col", Y_GROUPS)
+
+    gate_up_term, tok_other = gate_up_product(
+        z, own_all, other_blocks, gate_weight, gate_other, up_weight, up_other
+    )
+    gate_up, hidden_own = hidden_of(z, exchange(gate_up_term, "row", X_GROUPS))
+    hidden_term, grad_other = hidden_term_product(
+        z, own_all, other_blocks, down_weight, down_other
+    )
+    pre_own = pre_grads(x, exchange(hidden_term, "row", X_GROUPS), gate_up)
 
     hidden_blocks = ring_blocks(hidden_own, "row", X_UP, X_DOWN)
-    mixed_term, hidden = mixed_product(x, hidden_blocks, down_weight, down_other)
-    pre_blocks = ring_blocks(pre_own, "row", X_UP, X_DOWN)
+    mixed_term, hidden = mixed_product(after(x, pre_own), hidden_blocks, down_weight, down_other)
+    pre_blocks = ring_blocks(after(pre_own, *hidden_blocks), "row", X_UP, X_DOWN)
     input_term, pre_gate, pre_up = input_product(
-        x, pre_blocks, gate_weight, up_weight, gate_other, up_other
+        after(x, mixed_term), pre_blocks, gate_weight, up_weight, gate_other, up_other
     )
     mixed_y = exchange(mixed_term, "col", Y_GROUPS)
-    input_y = exchange(input_term, "col", Y_GROUPS)
-    sums = exchange(sums_of(y, mixed_y, input_y), "col", Z_GROUPS).astype(F32).sum(0).astype(BF16)
-    mixed = join(sums[:, : 2 * width])
-    input_grad = join(sums[:, 2 * width :])
-
+    input_y = exchange(after(input_term, mixed_y), "col", Y_GROUPS)
     def all_tokens(value):
         return jnp.concatenate([value, swap_core(value)], axis=0)
 
-    tok_rows = jnp.concatenate([tok[:, :width], swap_core(tok[:, width:])], axis=0)
-    grad_rows = jnp.concatenate([grad_mine, swap_core(grad_other)], axis=0)
+    tok_rows = jnp.concatenate([own_all[:, :width], swap_core(tok_other)], axis=0)
+    grad_rows = jnp.concatenate([own_all[:, width:], swap_core(grad_other)], axis=0)
     down_grad = dot(all_tokens(hidden), grad_rows, TN).astype(BF16)
     gate_grad = dot(tok_rows, all_tokens(pre_gate), TN).astype(BF16)
     up_grad = dot(tok_rows, all_tokens(pre_up), TN).astype(BF16)
+    sums = sums_of(x, mixed_y, after(input_y, down_grad))
+    sums = exchange(sums, "col", Z_GROUPS).astype(F32).sum(0).astype(BF16)
+    mixed = join(sums[:, : 2 * width])
+    input_grad = join(sums[:, 2 * width :])
+
     return (mixed, input_grad, gate_grad, up_grad, down_grad)
 
 

time: 248 us -> 240 us (0.968)
  starting transfers between devices: 66.1 us -> 94.5 us
  blocking collectives: 22.5 us -> 0 us
  waiting for transfers between devices: 91 us -> 75.9 us
  Pallas kernels: 29.5 us -> 33.6 us
    all_to_all x6 -> x8, waiting for transfers between devices: 53.6 us -> 26.6 us  [exchange(): lax.all_to_all(value, axis, 0, 0, axis_index_groups=groups, tiled=True)]
    all_to_all x1 -> x0, blocking collectives: 22.5 us -> none  [exchange(): lax.all_to_all(value, axis, 0, 0, axis_index_groups=groups, tiled=True)]
    ppermute x0 -> x8, waiting for transfers between devices: none -> 22.3 us  [the longest x3 20.1 us: ring_eight(): before.append(lax.ppermute(before[-1], axis, up))]
    ppermute x12, starting transfers between devices: 21.9 us -> 36 us  [swap_core(): return lax.ppermute(value, 'row', CORE_PAIRS)]
    ppermute x0 -> x8, starting transfers between devices: none -> 10.8 us  [the longest x3 6.58 us: ring_eight(): behind.append(lax.ppermute(behind[-1], axis, down))]
    ppermute x3 -> x2, waiting for transfers between devices: 22.9 us -> 12.7 us  [ring_blocks(): before = lax.ppermute(own, axis, up)]
    all_to_all x6 -> x8, starting transfers between devices: 27.3 us -> 36.3 us  [exchange(): lax.all_to_all(value, axis, 0, 0, axis_index_groups=groups, tiled=True)]
    ppermute x3 -> x2, waiting for transfers between devices: 11.2 us -> 5.78 us  [ring_blocks(): top = lax.ppermute(before[:half], axis, up)]
  transfers between devices with their start and end apart: 30 -> 36, of which waited for: 14 -> 22; matrix products, arithmetic and copies ran while one was open for 9% -> 8% of each run, Pallas kernels for 11% -> 10%
where the time goes in v3:
time: 240 us; the launch traced here: 238 us
  starting transfers between devices  94.5 us (39%)
  waiting for transfers between devices  75.9 us (32%)
  Pallas kernels  33.6 us (14%)
  local copies, waits for them, and re-layouts  18.8 us (8%)
  matrix products  13.3 us (6%)
    all_to_all x8, starting transfers between devices, exchange(): lax.all_to_all(value, axis, 0, 0, axis_index_groups=groups, tiled=True)  36.3 us
    ppermute x12, starting transfers between devices, swap_core(): return lax.ppermute(value, 'row', CORE_PAIRS)  36 us
    all_to_all x8, waiting for transfers between devices, exchange(): lax.all_to_all(value, axis, 0, 0, axis_index_groups=groups, tiled=True)  26.6 us
    ppermute x3, waiting for transfers between devices, ring_eight(): before.append(lax.ppermute(before[-1], axis, up))  20.1 us
    dot_general x3, matrix products, dot(): return lax.dot_general(left, right, dims, preferred_element_type=F32)  13.3 us
    ppermute x2, waiting for transfers between devices, ring_blocks(): before = lax.ppermute(own, axis, up)  12.7 us
    unnamed x32, local copies, waits for them, and re-layouts  11.2 us
    pallas_call x1, Pallas kernels, input_product(): call(input_kernel, (2 * steps,), [whole(block.shape) for block in blocks]...  9.57 us
  transfers between devices with their start and end apart: 36, of which 22 were waited for; matrix products, arithmetic and copies ran while one was open for 8% of the time, Pallas kernels for 10%

profile of v3, /device:TPU:1, one launch (start us, length us, event | category | flops | bytes accessed | tf_op | source)
XLA Modules:
  0.0 238.5 jit_solution(12380542049244360727)
XLA Ops:
  0.7 0.8 constant_dynamic-slice_fusion.1
  1.4 3.2 %collective-permute-start = (bf16[16,1024]{1,0:T(8,128)(2,1)S(1)}, bf16[16,1024]{1,0:T(8,128)(2,1)S(1)}, u32[]{:S(2)}, u32[]{:S(2)}) collective-permute-start(bf16[16,1024]{1,0:T(8,128)(2,1)S(1)} %get-tuple-element.48), channel_id=1, source_target_pairs={{0,32},{32,0},{64,96},{96,64},{128,160},{160,128},{192,224},{224,1... | collective-permute-start | bytes 98312 | tf_op jit(solution)/shard_map/ppermute | solution.py:32
  4.7 0.8 constant_dynamic-slice_fusion
  5.5 1.1 collective-permute-done.1
  7.4 3.4 %all-to-all-start = ((bf16[4,16,2048]{2,1,0:T(8,128)(2,1)}), bf16[4,16,2048]{2,1,0:T(8,128)(2,1)S(1)}, u32[]{:S(2)}, u32[]{:S(2)}) async-start(bf16[4,16,2048]{2,1,0:T(8,128)(2,1)} %tile.6), calls=%async_computation | async-start | bytes 524288 | tf_op jit(solution)/shard_map/all_to_all | solution.py:37
  10.8 6.6 %all-to-all-done = bf16[4,16,2048]{2,1,0:T(8,128)(2,1)S(1)} async-done(((bf16[4,16,2048]{2,1,0:T(8,128)(2,1)}), bf16[4,16,2048]{2,1,0:T(8,128)(2,1)S(1)}, u32[]{:S(2)}, u32[]{:S(2)}) %all-to-all-start) | async-done | bytes 262176 | tf_op jit(solution)/shard_map/all_to_all | solution.py:37
  17.4 0.8 tile.7
  18.3 6.6 %all-to-all-start.1 = ((bf16[8,16,2048]{2,1,0:T(8,128)(2,1)}), bf16[8,16,2048]{2,1,0:T(8,128)(2,1)S(1)}, u32[]{:S(2)}, u32[]{:S(2)}) async-start(bf16[8,16,2048]{2,1,0:T(8,128)(2,1)} %tile.7), calls=%async_computation.1 | async-start | bytes 1048576 | tf_op jit(solution)/shard_map/all_to_all | solution.py:37
  24.9 1.5 collective-permute-start.3
  26.4 1.2 collective-permute-start.2
  27.6 2.4 %collective-permute-start.11 = (bf16[1024,768]{1,0:T(8,128)(2,1)}, bf16[1024,768]{1,0:T(8,128)(2,1)}, u32[]{:S(2)}, u32[]{:S(2)}) collective-permute-start(bf16[1024,768]{1,0:T(8,128)(2,1)} %gate_a.1), channel_id=1, source_target_pairs={{0,32},{32,0},{64,96},{96,64},{128,160},{160,128},{192,224},{224,1... | collective-permute-start | bytes 4718600 | tf_op jit(solution)/shard_map/ppermute | solution.py:32
  30.0 14.8 %collective-permute-done.3.refs_8_ = bf16[64,2048]{1,0:T(8,128)(2,1)S(1)} collective-permute-done((bf16[64,2048]{1,0:T(8,128)(2,1)S(1)}, bf16[64,2048]{1,0:T(8,128)(2,1)S(1)}, u32[]{:S(2)}, u32[]{:S(2)}) %collective-permute-start.3) | collective-permute-done | bytes 262176 | tf_op jit(solution)/shard_map/ppermute | solution.py:63
  44.8 1.6 tile.8
  46.5 3.6 %all-to-all-start.2 = ((bf16[4,128,2048]{2,1,0:T(8,128)(2,1)}), bf16[4,128,2048]{2,1,0:T(8,128)(2,1)S(1)}, u32[]{:S(2)}, u32[]{:S(2)}) async-start(bf16[4,128,2048]{2,1,0:T(8,128)(2,1)} %tile.8), calls=%async_computation.2 | async-start | bytes 4194304 | tf_op jit(solution)/shard_map/all_to_all | solution.py:37
  50.2 2.7 %collective-permute-start.4 = (bf16[64,2048]{1,0:T(8,128)(2,1)S(1)}, bf16[64,2048]{1,0:T(8,128)(2,1)S(1)}, u32[]{:S(2)}, u32[]{:S(2)}) collective-permute-start(bf16[64,2048]{1,0:T(8,128)(2,1)S(1)} %collective-permute-done.2.refs_1_), channel_id=1, source_target_pairs={{4,0},{5,1},{6,2},{7,3},{8,4},{9,5},{10,6},{11,7},{12,8},{13,9},{1... | collective-permute-start | bytes 786440 | tf_op jit(solution)/shard_map/ppermute | solution.py:64
  52.8 4.9 %collective-permute-done.6.refs_7_ = bf16[64,2048]{1,0:T(8,128)(2,1)S(1)} collective-permute-done((bf16[64,2048]{1,0:T(8,128)(2,1)S(1)}, bf16[64,2048]{1,0:T(8,128)(2,1)S(1)}, u32[]{:S(2)}, u32[]{:S(2)}) %collective-permute-start.6) | collective-permute-done | bytes 262176 | tf_op jit(solution)/shard_map/ppermute | solution.py:63
  58.4 2.7 %collective-permute-start.5 = (bf16[64,2048]{1,0:T(8,128)(2,1)S(1)}, bf16[64,2048]{1,0:T(8,128)(2,1)S(1)}, u32[]{:S(2)}, u32[]{:S(2)}) collective-permute-start(bf16[64,2048]{1,0:T(8,128)(2,1)S(1)} %collective-permute-done.4.refs_2_), channel_id=1, source_target_pairs={{4,0},{5,1},{6,2},{7,3},{8,4},{9,5},{10,6},{11,7},{12,8},{13,9},{1... | collective-permute-start | bytes 786440 | tf_op jit(solution)/shard_map/ppermute | solution.py:64
  61.1 2.9 %collective-permute-start.10 = (bf16[768,1024]{1,0:T(8,128)(2,1)}, bf16[768,1024]{1,0:T(8,128)(2,1)}, u32[]{:S(2)}, u32[]{:S(2)}) collective-permute-start(bf16[768,1024]{1,0:T(8,128)(2,1)} %down_a.1), channel_id=1, source_target_pairs={{0,32},{32,0},{64,96},{96,64},{128,160},{160,128},{192,224},{224,1... | collective-permute-start | bytes 4718600 | tf_op jit(solution)/shard_map/ppermute | solution.py:32
  65.8 2.7 %collective-permute-start.9 = (bf16[32,2048]{1,0:T(8,128)(2,1)}, bf16[32,2048]{1,0:T(8,128)(2,1)}, u32[]{:S(2)}, u32[]{:S(2)}) collective-permute-start(bf16[32,2048]{1,0:T(8,128)(2,1)} %slice.55), channel_id=1, source_target_pairs={{4,0},{5,1},{6,2},{7,3},{8,4},{9,5},{10,6},{11,7},{12,8},{13,9},{1... | collective-permute-start | bytes 393224 | tf_op jit(solution)/shard_map/ppermute | solution.py:66
  68.5 2.1 collective-permute-done.8.refs_4_
  70.8 4.2 %all-to-all-done.2 = bf16[4,128,2048]{2,1,0:T(8,128)(2,1)S(1)} async-done(((bf16[4,128,2048]{2,1,0:T(8,128)(2,1)}), bf16[4,128,2048]{2,1,0:T(8,128)(2,1)S(1)}, u32[]{:S(2)}, u32[]{:S(2)}) %all-to-all-start.2) | async-done | bytes 2097184 | tf_op jit(solution)/shard_map/all_to_all | solution.py:37
  74.9 0.9 copy-done.5
  75.9 0.9 copy-done.8
  76.8 8.4 %shard_map.93 = (bf16[512,1536]{1,0:T(8,128)(2,1)}, bf16[512,1024]{1,0:T(8,128)(2,1)}) custom-call(s32[1]{0:T(128)} %bitcast.1.index, bf16[512,2048]{1,0:T(8,128)(2,1)S(1)} %bitcast.10, bf16[64,2048]{1,0:T(8,128)(2,1)S(1)} %bitcast.15, bf16[64,2048]{1,0:T(8,128)(2,1)S(1)} %collective-permute-done.2.refs_1_, bf16[64,2048]{1,0:T(8,128)(2,1)S(1)} %copy-done.8, ...), custom_call_target="tpu_custom_call" | custom-call | flops 3221225472 | bytes 10485760 | tf_op jit(solution)/shard_map/pallas_call | solution.py:150
  85.2 4.5 %all-to-all-start.4 = ((bf16[4,128,1536]{2,1,0:T(8,128)(2,1)}), bf16[4,128,1536]{2,1,0:T(8,128)(2,1)}, u32[]{:S(2)}, u32[]{:S(2)}) async-start(bf16[4,128,1536]{2,1,0:T(8,128)(2,1)} %bitcast.20), calls=%async_computation.4 | async-start | bytes 3145728 | tf_op jit(solution)/shard_map/all_to_all | solution.py:37
  89.8 1.4 copy-done
  91.2 0.9 copy-done.6
  92.2 0.9 copy-done.9
  93.1 4.5 %shard_map.92 = (bf16[512,768]{1,0:T(8,128)(2,1)}, bf16[512,1024]{1,0:T(8,128)(2,1)}) custom-call(s32[1]{0:T(128)} %bitcast.1.index, bf16[512,2048]{1,0:T(8,128)(2,1)S(1)} %bitcast.11, bf16[64,2048]{1,0:T(8,128)(2,1)S(1)} %bitcast.16, bf16[64,2048]{1,0:T(8,128)(2,1)S(1)} %collective-permute-done.2.refs_1_, bf16[64,2048]{1,0:T(8,128)(2,1)S(1)} %copy-done.9, ...), custom_call_target="tpu_custom_call" | custom-call | flops 1610612736 | bytes 10485760 | tf_op jit(solution)/shard_map/pallas_call | solution.py:181
  97.6 10.4 %all-to-all-done.4.terms = bf16[4,128,1536]{2,1,0:T(8,128)(2,1)} async-done(((bf16[4,128,1536]{2,1,0:T(8,128)(2,1)}), bf16[4,128,1536]{2,1,0:T(8,128)(2,1)}, u32[]{:S(2)}, u32[]{:S(2)}) %all-to-all-start.4) | async-done | bytes 1572896 | tf_op jit(solution)/shard_map/all_to_all | solution.py:37
  108.0 3.5 %all-to-all-start.3 = ((bf16[4,128,768]{2,1,0:T(8,128)(2,1)}), bf16[4,128,768]{2,1,0:T(8,128)(2,1)S(1)}, u32[]{:S(2)}, u32[]{:S(2)}) async-start(bf16[4,128,768]{2,1,0:T(8,128)(2,1)} %bitcast.21), calls=%async_computation.3 | async-start | bytes 1572864 | tf_op jit(solution)/shard_map/all_to_all | solution.py:37
  111.5 1.6 shard_map.94
  113.2 0.9 copy-done.2
  114.1 1.4 collective-permute-start.14
  115.5 1.3 collective-permute-start.13
  116.7 7.6 %collective-permute-done.14.before = bf16[128,768]{1,0:T(8,128)(2,1)S(1)} collective-permute-done((bf16[128,768]{1,0:T(8,128)(2,1)S(1)}, bf16[128,768]{1,0:T(8,128)(2,1)S(1)}, u32[]{:S(2)}, u32[]{:S(2)}) %collective-permute-start.14) | collective-permute-done | bytes 196640 | tf_op jit(solution)/shard_map/ppermute | solution.py:52
  125.7 2.6 %collective-permute-start.16 = (bf16[64,768]{1,0:T(8,128)(2,1)}, bf16[64,768]{1,0:T(8,128)(2,1)}, u32[]{:S(2)}, u32[]{:S(2)}) collective-permute-start(bf16[64,768]{1,0:T(8,128)(2,1)} %slice.57), channel_id=1, source_target_pairs={{64,0},{96,32},{128,64},{160,96},{192,128},{224,160},{0,192},{32,2... | collective-permute-start | bytes 294920 | tf_op jit(solution)/shard_map/ppermute | solution.py:55
  128.4 1.1 copy-done.3
  130.3 1.4 copy-done.1
  131.7 0.9 copy-done.11
  132.6 0.9 copy-done.13
  133.6 5.5 %shard_map.96 = (bf16[512,2048]{1,0:T(8,128)(2,1)}, bf16[512,768]{1,0:T(8,128)(2,1)}) custom-call(s32[1]{0:T(128)} %bitcast.index, bf16[128,768]{1,0:T(8,128)(2,1)S(1)} %copy-done.13, bf16[128,768]{1,0:T(8,128)(2,1)S(1)} %copy-done.11, bf16[64,768]{1,0:T(8,128)(2,1)} %collective-permute-done.15.top, bf16[64,768]{1,0:T(8,128)(2,1)} %collective-permute-done.16.bottom, ...), custom_call_target="tpu_custom_call" | custom-call | flops 1610612736 | bytes 10485760 | tf_op jit(solution)/shard_map/pallas_call | solution.py:220
  139.0 4.5 %all-to-all-start.5 = ((bf16[4,128,2048]{2,1,0:T(8,128)(2,1)}), bf16[4,128,2048]{2,1,0:T(8,128)(2,1)}, u32[]{:S(2)}, u32[]{:S(2)}) async-start(bf16[4,128,2048]{2,1,0:T(8,128)(2,1)} %bitcast.18), calls=%async_computation.5 | async-start | bytes 4194304 | tf_op jit(solution)/shard_map/all_to_all | solution.py:37
  143.5 1.2 collective-permute-start.18
  144.7 2.0 collective-permute-start.17
  146.7 5.1 %collective-permute-done.18.before = bf16[128,1536]{1,0:T(8,128)(2,1)S(1)} collective-permute-done((bf16[128,1536]{1,0:T(8,128)(2,1)S(1)}, bf16[128,1536]{1,0:T(8,128)(2,1)S(1)}, u32[]{:S(2)}, u32[]{:S(2)}) %collective-permute-start.18) | collective-permute-done | bytes 393248 | tf_op jit(solution)/shard_map/ppermute | solution.py:52
  151.9 2.7 %collective-permute-start.20 = (bf16[64,1536]{1,0:T(8,128)(2,1)S(1)}, bf16[64,1536]{1,0:T(8,128)(2,1)S(1)}, u32[]{:S(2)}, u32[]{:S(2)}) collective-permute-start(bf16[64,1536]{1,0:T(8,128)(2,1)S(1)} %slice.59), channel_id=1, source_target_pairs={{64,0},{96,32},{128,64},{160,96},{192,128},{224,160},{0,192},{32,2... | collective-permute-start | bytes 589832 | tf_op jit(solution)/shard_map/ppermute | solution.py:55
  154.7 5.5 %collective-permute-done.19.top = bf16[64,1536]{1,0:T(8,128)(2,1)S(1)} collective-permute-done((bf16[64,1536]{1,0:T(8,128)(2,1)S(1)}, bf16[64,1536]{1,0:T(8,128)(2,1)S(1)}, u32[]{:S(2)}, u32[]{:S(2)}) %collective-permute-start.19) | collective-permute-done | bytes 196640 | tf_op jit(solution)/shard_map/ppermute | solution.py:54
  160.2 9.6 %shard_map.97 = (bf16[512,2048]{1,0:T(8,128)(2,1)}, bf16[512,768]{1,0:T(8,128)(2,1)}, bf16[512,768]{1,0:T(8,128)(2,1)}) custom-call(s32[1]{0:T(128)} %bitcast.index, bf16[128,1536]{1,0:T(8,128)(2,1)S(1)} %shard_map.95.own, bf16[128,1536]{1,0:T(8,128)(2,1)S(1)} %collective-permute-done.17.behind, bf16[64,1536]{1,0:T(8,128)(2,1)S(1)} %collective-permute-done.19.top, ...), custom_call_target="tpu_custom_call" | custom-call | flops 3221225472 | bytes 10485760 | tf_op jit(solution)/shard_map/pallas_call | solution.py:271
  169.8 4.5 %all-to-all-start.6 = ((bf16[4,128,2048]{2,1,0:T(8,128)(2,1)}), bf16[4,128,2048]{2,1,0:T(8,128)(2,1)}, u32[]{:S(2)}, u32[]{:S(2)}) async-start(bf16[4,128,2048]{2,1,0:T(8,128)(2,1)} %bitcast.19), calls=%async_computation.6 | async-start | bytes 4194304 | tf_op jit(solution)/shard_map/all_to_all | solution.py:37
  174.2 7.7 %collective-permute-start.22 = (bf16[512,1024]{1,0:T(8,128)(2,1)}, bf16[512,1024]{1,0:T(8,128)(2,1)S(1)}, u32[]{:S(2)}, u32[]{:S(2)}) collective-permute-start(bf16[512,1024]{1,0:T(8,128)(2,1)} %get-tuple-element.36), channel_id=1, source_target_pairs={{0,32},{32,0},{64,96},{96,64},{128,160},{160,128},{192,224},{224,1... | collective-permute-start | bytes 3145736 | tf_op jit(solution)/shard_map/ppermute | solution.py:32
  182.4 2.1 collective-permute-done.22
  184.5 1.1 collective-permute-done.21
  185.6 4.1 %fusion.4 = bf16[768,1024]{1,0:T(8,128)(2,1)} fusion(bf16[512,1024]{1,0:T(8,128)(2,1)S(1)} %collective-permute-done.22, bf16[512,1024]{1,0:T(8,128)(2,1)S(1)} %get-tuple-element.42, bf16[512,768]{1,0:T(8,128)(2,1)S(1)} %collective-permute-done.21, bf16[512,768]{1,0:T(8,128)(2,1)} %get-tuple-element.35), kind=kOutput, calls=%fused_computation.5 | convolution fusion | flops 1618739200 | bytes 5242880 | tf_op jit(solution)/shard_map/dot_general | solution.py:28
  189.7 2.8 %all-to-all-done.6.two = bf16[4,128,2048]{2,1,0:T(8,128)(2,1)} async-done(((bf16[4,128,2048]{2,1,0:T(8,128)(2,1)}), bf16[4,128,2048]{2,1,0:T(8,128)(2,1)}, u32[]{:S(2)}, u32[]{:S(2)}) %all-to-all-start.6) | async-done | bytes 2097184 | tf_op jit(solution)/shard_map/all_to_all | solution.py:37
  192.6 3.7 %shard_map.98 = bf16[128,4096]{1,0:T(8,128)(2,1)} custom-call(s32[1]{0:T(128)} %bitcast.index, bf16[4,128,2048]{2,1,0:T(8,128)(2,1)} %all-to-all-done.5.one, bf16[4,128,2048]{2,1,0:T(8,128)(2,1)} %all-to-all-done.6.two), custom_call_target="tpu_custom_call" | custom-call | flops 4194304 | bytes 10485760 | tf_op jit(solution)/shard_map/pallas_call | solution.py:342
  196.3 5.7 %all-to-all-start.7 = ((bf16[8,16,4096]{2,1,0:T(8,128)(2,1)}), bf16[8,16,4096]{2,1,0:T(8,128)(2,1)S(1)}, u32[]{:S(2)}, u32[]{:S(2)}) async-start(bf16[8,16,4096]{2,1,0:T(8,128)(2,1)} %bitcast.9), calls=%async_computation.7 | async-start | bytes 2097152 | tf_op jit(solution)/shard_map/all_to_all | solution.py:37
  202.0 9.1 %collective-permute-start.25 = (bf16[512,1024]{1,0:T(8,128)(2,1)S(1)}, bf16[512,1024]{1,0:T(8,128)(2,1)}, u32[]{:S(2)}, u32[]{:S(2)}) collective-permute-start(bf16[512,1024]{1,0:T(8,128)(2,1)S(1)} %copy-done.14), channel_id=1, source_target_pairs={{0,32},{32,0},{64,96},{96,64},{128,160},{160,128},{192,224},{224,1... | collective-permute-start | bytes 3145736 | tf_op jit(solution)/shard_map/ppermute | solution.py:32
  211.7 2.4 %collective-permute-done.25 = bf16[512,1024]{1,0:T(8,128)(2,1)} collective-permute-done((bf16[512,1024]{1,0:T(8,128)(2,1)S(1)}, bf16[512,1024]{1,0:T(8,128)(2,1)}, u32[]{:S(2)}, u32[]{:S(2)}) %collective-permute-start.25) | collective-permute-done | bytes 1048608 | tf_op jit(solution)/shard_map/ppermute | solution.py:32
  214.1 0.9 collective-permute-done.26
  214.9 4.8 %convolution_convert_fusion.1 = bf16[1024,768]{1,0:T(8,128)(2,1)} fusion(bf16[512,768]{1,0:T(8,128)(2,1)} %collective-permute-done.26, bf16[512,768]{1,0:T(8,128)(2,1)} %get-tuple-element.39, bf16[512,1024]{1,0:T(8,128)(2,1)} %collective-permute-done.25, bf16[512,1024]{1,0:T(8,128)(2,1)S(1)} %get-tuple-element.41), kind=kOutput, calls=%fused_computation.7 | convolution fusion | flops 1618739200 | bytes 5242880 | tf_op jit(solution)/shard_map/dot_general | solution.py:28
  219.7 2.5 %all-to-all-done.7 = bf16[8,16,4096]{2,1,0:T(8,128)(2,1)S(1)} async-done(((bf16[8,16,4096]{2,1,0:T(8,128)(2,1)}), bf16[8,16,4096]{2,1,0:T(8,128)(2,1)S(1)}, u32[]{:S(2)}, u32[]{:S(2)}) %all-to-all-start.7) | async-done | bytes 1048608 | tf_op jit(solution)/shard_map/all_to_all | solution.py:37
  222.4 9.7 %collective-permute-start.24 = (bf16[16,1024]{1,0:T(8,128)(2,1)S(1)}, bf16[16,1024]{1,0:T(8,128)(2,1)S(1)}, u32[]{:S(2)}, u32[]{:S(2)}) collective-permute-start(bf16[16,1024]{1,0:T(8,128)(2,1)S(1)} %slice.64), channel_id=1, source_target_pairs={{0,32},{32,0},{64,96},{96,64},{128,160},{160,128},{192,224},{224,1... | collective-permute-start | bytes 98312 | tf_op jit(solution)/shard_map/ppermute | solution.py:32
  232.1 4.5 %convolution_convert_fusion = bf16[1024,768]{1,0:T(8,128)(2,1)} fusion(bf16[512,768]{1,0:T(8,128)(2,1)} %collective-permute-done.27, bf16[512,768]{1,0:T(8,128)(2,1)S(1)} %copy-done.15, bf16[512,1024]{1,0:T(8,128)(2,1)} %collective-permute-done.25, bf16[512,1024]{1,0:T(8,128)(2,1)S(1)} %get-tuple-element.41), kind=kOutput, calls=%fused_computation.6 | convolution fusion | flops 1618739200 | bytes 5242880 | tf_op jit(solution)/shard_map/dot_general | solution.py:28
  (70 shorter events, 8.8 us)
Async XLA Ops:
  1.4 4.1 %collective-permute-start = (bf16[16,1024]{1,0:T(8,128)(2,1)S(1)}, bf16[16,1024]{1,0:T(8,128)(2,1)S(1)}, u32[]{:S(2)}, u32[]{:S(2)}) collective-permute-start(bf16[16,1024]{1,0:T(8,128)(2,1)S(1)} %get-tuple-element.48), channel_id=1, source_target_pairs={{0,32},{32,0},{64,96},{96,64},{128,160},{160,128},{192,224},{224,1... | collective-permute-start | bytes 98312 | tf_op jit(solution)/shard_map/ppermute | solution.py:32
  5.5 1.2 collective-permute-start.1
  7.4 10.0 %all-to-all-start = ((bf16[4,16,2048]{2,1,0:T(8,128)(2,1)}), bf16[4,16,2048]{2,1,0:T(8,128)(2,1)S(1)}, u32[]{:S(2)}, u32[]{:S(2)}) async-start(bf16[4,16,2048]{2,1,0:T(8,128)(2,1)} %tile.6), calls=%async_computation | async-start | bytes 524288 | tf_op jit(solution)/shard_map/all_to_all | solution.py:37
  18.3 26.6 %all-to-all-start.1 = ((bf16[8,16,2048]{2,1,0:T(8,128)(2,1)}), bf16[8,16,2048]{2,1,0:T(8,128)(2,1)S(1)}, u32[]{:S(2)}, u32[]{:S(2)}) async-start(bf16[8,16,2048]{2,1,0:T(8,128)(2,1)} %tile.7), calls=%async_computation.1 | async-start | bytes 1048576 | tf_op jit(solution)/shard_map/all_to_all | solution.py:37
  24.9 19.9 %collective-permute-start.3 = (bf16[64,2048]{1,0:T(8,128)(2,1)S(1)}, bf16[64,2048]{1,0:T(8,128)(2,1)S(1)}, u32[]{:S(2)}, u32[]{:S(2)}) collective-permute-start(bf16[64,2048]{1,0:T(8,128)(2,1)S(1)} %bitcast.13), channel_id=1, source_target_pairs={{0,4},{1,5},{2,6},{3,7},{4,8},{5,9},{6,10},{7,11},{8,12},{9,13},{1... | collective-permute-start | bytes 786440 | tf_op jit(solution)/shard_map/ppermute | solution.py:63
  26.4 18.5 %collective-permute-start.2 = (bf16[64,2048]{1,0:T(8,128)(2,1)S(1)}, bf16[64,2048]{1,0:T(8,128)(2,1)S(1)}, u32[]{:S(2)}, u32[]{:S(2)}) collective-permute-start(bf16[64,2048]{1,0:T(8,128)(2,1)S(1)} %bitcast.14), channel_id=1, source_target_pairs={{4,0},{5,1},{6,2},{7,3},{8,4},{9,5},{10,6},{11,7},{12,8},{13,9},{1... | collective-permute-start | bytes 786440 | tf_op jit(solution)/shard_map/ppermute | solution.py:64
  27.6 43.1 %collective-permute-start.11 = (bf16[1024,768]{1,0:T(8,128)(2,1)}, bf16[1024,768]{1,0:T(8,128)(2,1)}, u32[]{:S(2)}, u32[]{:S(2)}) collective-permute-start(bf16[1024,768]{1,0:T(8,128)(2,1)} %gate_a.1), channel_id=1, source_target_pairs={{0,32},{32,0},{64,96},{96,64},{128,160},{160,128},{192,224},{224,1... | collective-permute-start | bytes 4718600 | tf_op jit(solution)/shard_map/ppermute | solution.py:32
  30.0 40.7 %collective-permute-start.12 = (bf16[1024,768]{1,0:T(8,128)(2,1)}, bf16[1024,768]{1,0:T(8,128)(2,1)}, u32[]{:S(2)}, u32[]{:S(2)}) collective-permute-start(bf16[1024,768]{1,0:T(8,128)(2,1)} %up_a.1), channel_id=1, source_target_pairs={{0,32},{32,0},{64,96},{96,64},{128,160},{160,128},{192,224},{224,1... | collective-permute-start | bytes 4718600 | tf_op jit(solution)/shard_map/ppermute | solution.py:32
  46.5 28.5 %all-to-all-start.2 = ((bf16[4,128,2048]{2,1,0:T(8,128)(2,1)}), bf16[4,128,2048]{2,1,0:T(8,128)(2,1)S(1)}, u32[]{:S(2)}, u32[]{:S(2)}) async-start(bf16[4,128,2048]{2,1,0:T(8,128)(2,1)} %tile.8), calls=%async_computation.2 | async-start | bytes 4194304 | tf_op jit(solution)/shard_map/all_to_all | solution.py:37
  50.1 7.6 %collective-permute-start.6 = (bf16[64,2048]{1,0:T(8,128)(2,1)S(1)}, bf16[64,2048]{1,0:T(8,128)(2,1)S(1)}, u32[]{:S(2)}, u32[]{:S(2)}) collective-permute-start(bf16[64,2048]{1,0:T(8,128)(2,1)S(1)} %collective-permute-done.3.refs_8_), channel_id=1, source_target_pairs={{0,4},{1,5},{2,6},{3,7},{4,8},{5,9},{6,10},{7,11},{8,12},{9,13},{1... | collective-permute-start | bytes 786440 | tf_op jit(solution)/shard_map/ppermute | solution.py:63
  50.2 8.3 %collective-permute-start.4 = (bf16[64,2048]{1,0:T(8,128)(2,1)S(1)}, bf16[64,2048]{1,0:T(8,128)(2,1)S(1)}, u32[]{:S(2)}, u32[]{:S(2)}) collective-permute-start(bf16[64,2048]{1,0:T(8,128)(2,1)S(1)} %collective-permute-done.2.refs_1_), channel_id=1, source_target_pairs={{4,0},{5,1},{6,2},{7,3},{8,4},{9,5},{10,6},{11,7},{12,8},{13,9},{1... | collective-permute-start | bytes 786440 | tf_op jit(solution)/shard_map/ppermute | solution.py:64
  57.7 6.7 %collective-permute-start.7 = (bf16[64,2048]{1,0:T(8,128)(2,1)S(1)}, bf16[64,2048]{1,0:T(8,128)(2,1)S(1)}, u32[]{:S(2)}, u32[]{:S(2)}) collective-permute-start(bf16[64,2048]{1,0:T(8,128)(2,1)S(1)} %collective-permute-done.6.refs_7_), channel_id=1, source_target_pairs={{0,4},{1,5},{2,6},{3,7},{4,8},{5,9},{6,10},{7,11},{8,12},{9,13},{1... | collective-permute-start | bytes 786440 | tf_op jit(solution)/shard_map/ppermute | solution.py:63
  57.7 0.7 copy-start.4
  58.4 6.7 %copy-start.7 = (bf16[64,2048]{1,0:T(8,128)(2,1)}, bf16[64,2048]{1,0:T(8,128)(2,1)S(1)}, u32[]{:S(2)}) copy-start(bf16[64,2048]{1,0:T(8,128)(2,1)S(1)} %collective-permute-done.4.refs_2_) | copy-start | bytes 786436
  58.4 6.7 %collective-permute-start.5 = (bf16[64,2048]{1,0:T(8,128)(2,1)S(1)}, bf16[64,2048]{1,0:T(8,128)(2,1)S(1)}, u32[]{:S(2)}, u32[]{:S(2)}) collective-permute-start(bf16[64,2048]{1,0:T(8,128)(2,1)S(1)} %collective-permute-done.4.refs_2_), channel_id=1, source_target_pairs={{4,0},{5,1},{6,2},{7,3},{8,4},{9,5},{10,6},{11,7},{12,8},{13,9},{1... | collective-permute-start | bytes 786440 | tf_op jit(solution)/shard_map/ppermute | solution.py:64
  61.1 28.7 %collective-permute-start.10 = (bf16[768,1024]{1,0:T(8,128)(2,1)}, bf16[768,1024]{1,0:T(8,128)(2,1)}, u32[]{:S(2)}, u32[]{:S(2)}) collective-permute-start(bf16[768,1024]{1,0:T(8,128)(2,1)} %down_a.1), channel_id=1, source_target_pairs={{0,32},{32,0},{64,96},{96,64},{128,160},{160,128},{192,224},{224,1... | collective-permute-start | bytes 4718600 | tf_op jit(solution)/shard_map/ppermute | solution.py:32
  65.1 5.5 %collective-permute-start.8 = (bf16[32,2048]{1,0:T(8,128)(2,1)}, bf16[32,2048]{1,0:T(8,128)(2,1)S(1)}, u32[]{:S(2)}, u32[]{:S(2)}) collective-permute-start(bf16[32,2048]{1,0:T(8,128)(2,1)} %slice.54), channel_id=1, source_target_pairs={{0,4},{1,5},{2,6},{3,7},{4,8},{5,9},{6,10},{7,11},{8,12},{9,13},{1... | collective-permute-start | bytes 393224 | tf_op jit(solution)/shard_map/ppermute | solution.py:65
  65.8 5.0 %collective-permute-start.9 = (bf16[32,2048]{1,0:T(8,128)(2,1)}, bf16[32,2048]{1,0:T(8,128)(2,1)}, u32[]{:S(2)}, u32[]{:S(2)}) collective-permute-start(bf16[32,2048]{1,0:T(8,128)(2,1)} %slice.55), channel_id=1, source_target_pairs={{4,0},{5,1},{6,2},{7,3},{8,4},{9,5},{10,6},{11,7},{12,8},{13,9},{1... | collective-permute-start | bytes 393224 | tf_op jit(solution)/shard_map/ppermute | solution.py:66
  74.9 1.0 copy-start.5
  75.9 0.9 copy-start.8
  85.2 22.8 %all-to-all-start.4 = ((bf16[4,128,1536]{2,1,0:T(8,128)(2,1)}), bf16[4,128,1536]{2,1,0:T(8,128)(2,1)}, u32[]{:S(2)}, u32[]{:S(2)}) async-start(bf16[4,128,1536]{2,1,0:T(8,128)(2,1)} %bitcast.20), calls=%async_computation.4 | async-start | bytes 3145728 | tf_op jit(solution)/shard_map/all_to_all | solution.py:37
  89.8 1.4 copy-start
  91.2 0.9 copy-start.6
  92.2 0.9 copy-start.9
  108.0 20.3 %all-to-all-start.3 = ((bf16[4,128,768]{2,1,0:T(8,128)(2,1)}), bf16[4,128,768]{2,1,0:T(8,128)(2,1)S(1)}, u32[]{:S(2)}, u32[]{:S(2)}) async-start(bf16[4,128,768]{2,1,0:T(8,128)(2,1)} %bitcast.21), calls=%async_computation.3 | async-start | bytes 1572864 | tf_op jit(solution)/shard_map/all_to_all | solution.py:37
  113.2 0.9 copy-start.2
  114.1 11.0 %copy-start.12 = (bf16[128,768]{1,0:T(8,128)(2,1)}, bf16[128,768]{1,0:T(8,128)(2,1)S(1)}, u32[]{:S(2)}) copy-start(bf16[128,768]{1,0:T(8,128)(2,1)S(1)} %get-tuple-element.29.own) | copy-start | bytes 589828
  114.1 10.3 %collective-permute-start.14 = (bf16[128,768]{1,0:T(8,128)(2,1)S(1)}, bf16[128,768]{1,0:T(8,128)(2,1)S(1)}, u32[]{:S(2)}, u32[]{:S(2)}) collective-permute-start(bf16[128,768]{1,0:T(8,128)(2,1)S(1)} %get-tuple-element.29.own), channel_id=1, source_target_pairs={{0,64},{32,96},{64,128},{96,160},{128,192},{160,224},{192,0},{224,... | collective-permute-start | bytes 589832 | tf_op jit(solution)/shard_map/ppermute | solution.py:52
  115.5 9.5 %collective-permute-start.13 = (bf16[128,768]{1,0:T(8,128)(2,1)S(1)}, bf16[128,768]{1,0:T(8,128)(2,1)S(1)}, u32[]{:S(2)}, u32[]{:S(2)}) collective-permute-start(bf16[128,768]{1,0:T(8,128)(2,1)S(1)} %get-tuple-element.29.own), channel_id=1, source_target_pairs={{64,0},{96,32},{128,64},{160,96},{192,128},{224,160},{0,192},{32,2... | collective-permute-start | bytes 589832 | tf_op jit(solution)/shard_map/ppermute | solution.py:53
  125.0 5.0 %collective-permute-start.15 = (bf16[64,768]{1,0:T(8,128)(2,1)}, bf16[64,768]{1,0:T(8,128)(2,1)}, u32[]{:S(2)}, u32[]{:S(2)}) collective-permute-start(bf16[64,768]{1,0:T(8,128)(2,1)} %slice.56), channel_id=1, source_target_pairs={{0,64},{32,96},{64,128},{96,160},{128,192},{160,224},{192,0},{224,... | collective-permute-start | bytes 294920 | tf_op jit(solution)/shard_map/ppermute | solution.py:54
  125.0 3.3 %copy-start.10 = (bf16[128,768]{1,0:T(8,128)(2,1)}, bf16[128,768]{1,0:T(8,128)(2,1)S(1)}, u32[]{:S(2)}) copy-start(bf16[128,768]{1,0:T(8,128)(2,1)S(1)} %collective-permute-done.13.behind) | copy-start | bytes 589828
  125.7 4.6 %collective-permute-start.16 = (bf16[64,768]{1,0:T(8,128)(2,1)}, bf16[64,768]{1,0:T(8,128)(2,1)}, u32[]{:S(2)}, u32[]{:S(2)}) collective-permute-start(bf16[64,768]{1,0:T(8,128)(2,1)} %slice.57), channel_id=1, source_target_pairs={{64,0},{96,32},{128,64},{160,96},{192,128},{224,160},{0,192},{32,2... | collective-permute-start | bytes 294920 | tf_op jit(solution)/shard_map/ppermute | solution.py:55
  128.4 1.1 copy-start.3
  130.3 1.4 copy-start.1
  131.7 0.9 copy-start.11
  132.6 0.9 copy-start.13
  139.0 30.7 %all-to-all-start.5 = ((bf16[4,128,2048]{2,1,0:T(8,128)(2,1)}), bf16[4,128,2048]{2,1,0:T(8,128)(2,1)}, u32[]{:S(2)}, u32[]{:S(2)}) async-start(bf16[4,128,2048]{2,1,0:T(8,128)(2,1)} %bitcast.18), calls=%async_computation.5 | async-start | bytes 4194304 | tf_op jit(solution)/shard_map/all_to_all | solution.py:37
  143.5 8.3 %collective-permute-start.18 = (bf16[128,1536]{1,0:T(8,128)(2,1)S(1)}, bf16[128,1536]{1,0:T(8,128)(2,1)S(1)}, u32[]{:S(2)}, u32[]{:S(2)}) collective-permute-start(bf16[128,1536]{1,0:T(8,128)(2,1)S(1)} %shard_map.95.own), channel_id=1, source_target_pairs={{0,64},{32,96},{64,128},{96,160},{128,192},{160,224},{192,0},{224,... | collective-permute-start | bytes 1179656 | tf_op jit(solution)/shard_map/ppermute | solution.py:52
  144.7 7.2 %collective-permute-start.17 = (bf16[128,1536]{1,0:T(8,128)(2,1)S(1)}, bf16[128,1536]{1,0:T(8,128)(2,1)S(1)}, u32[]{:S(2)}, u32[]{:S(2)}) collective-permute-start(bf16[128,1536]{1,0:T(8,128)(2,1)S(1)} %shard_map.95.own), channel_id=1, source_target_pairs={{64,0},{96,32},{128,64},{160,96},{192,128},{224,160},{0,192},{32,2... | collective-permute-start | bytes 1179656 | tf_op jit(solution)/shard_map/ppermute | solution.py:53
  151.8 8.4 %collective-permute-start.19 = (bf16[64,1536]{1,0:T(8,128)(2,1)S(1)}, bf16[64,1536]{1,0:T(8,128)(2,1)S(1)}, u32[]{:S(2)}, u32[]{:S(2)}) collective-permute-start(bf16[64,1536]{1,0:T(8,128)(2,1)S(1)} %slice.58), channel_id=1, source_target_pairs={{0,64},{32,96},{64,128},{96,160},{128,192},{160,224},{192,0},{224,... | collective-permute-start | bytes 589832 | tf_op jit(solution)/shard_map/ppermute | solution.py:54
  151.9 8.3 %collective-permute-start.20 = (bf16[64,1536]{1,0:T(8,128)(2,1)S(1)}, bf16[64,1536]{1,0:T(8,128)(2,1)S(1)}, u32[]{:S(2)}, u32[]{:S(2)}) collective-permute-start(bf16[64,1536]{1,0:T(8,128)(2,1)S(1)} %slice.59), channel_id=1, source_target_pairs={{64,0},{96,32},{128,64},{160,96},{192,128},{224,160},{0,192},{32,2... | collective-permute-start | bytes 589832 | tf_op jit(solution)/shard_map/ppermute | solution.py:55
  169.8 22.8 %all-to-all-start.6 = ((bf16[4,128,2048]{2,1,0:T(8,128)(2,1)}), bf16[4,128,2048]{2,1,0:T(8,128)(2,1)}, u32[]{:S(2)}, u32[]{:S(2)}) async-start(bf16[4,128,2048]{2,1,0:T(8,128)(2,1)} %bitcast.19), calls=%async_computation.6 | async-start | bytes 4194304 | tf_op jit(solution)/shard_map/all_to_all | solution.py:37
  174.2 10.2 %collective-permute-start.22 = (bf16[512,1024]{1,0:T(8,128)(2,1)}, bf16[512,1024]{1,0:T(8,128)(2,1)S(1)}, u32[]{:S(2)}, u32[]{:S(2)}) collective-permute-start(bf16[512,1024]{1,0:T(8,128)(2,1)} %get-tuple-element.36), channel_id=1, source_target_pairs={{0,32},{32,0},{64,96},{96,64},{128,160},{160,128},{192,224},{224,1... | collective-permute-start | bytes 3145736 | tf_op jit(solution)/shard_map/ppermute | solution.py:32
  182.0 3.6 %collective-permute-start.21 = (bf16[512,768]{1,0:T(8,128)(2,1)}, bf16[512,768]{1,0:T(8,128)(2,1)S(1)}, u32[]{:S(2)}, u32[]{:S(2)}) collective-permute-start(bf16[512,768]{1,0:T(8,128)(2,1)} %get-tuple-element.35), channel_id=1, source_target_pairs={{0,32},{32,0},{64,96},{96,64},{128,160},{160,128},{192,224},{224,1... | collective-permute-start | bytes 2359304 | tf_op jit(solution)/shard_map/ppermute | solution.py:32
  196.3 5.8 %copy-start.14 = (bf16[512,1024]{1,0:T(8,128)(2,1)S(1)}, bf16[512,1024]{1,0:T(8,128)(2,1)}, u32[]{:S(2)}) copy-start(bf16[512,1024]{1,0:T(8,128)(2,1)} %get-tuple-element.38) | copy-start | bytes 3145732
  196.3 25.9 %all-to-all-start.7 = ((bf16[8,16,4096]{2,1,0:T(8,128)(2,1)}), bf16[8,16,4096]{2,1,0:T(8,128)(2,1)S(1)}, u32[]{:S(2)}, u32[]{:S(2)}) async-start(bf16[8,16,4096]{2,1,0:T(8,128)(2,1)} %bitcast.9), calls=%async_computation.7 | async-start | bytes 2097152 | tf_op jit(solution)/shard_map/all_to_all | solution.py:37
  202.0 12.0 %collective-permute-start.25 = (bf16[512,1024]{1,0:T(8,128)(2,1)S(1)}, bf16[512,1024]{1,0:T(8,128)(2,1)}, u32[]{:S(2)}, u32[]{:S(2)}) collective-permute-start(bf16[512,1024]{1,0:T(8,128)(2,1)S(1)} %copy-done.14), channel_id=1, source_target_pairs={{0,32},{32,0},{64,96},{96,64},{128,160},{160,128},{192,224},{224,1... | collective-permute-start | bytes 3145736 | tf_op jit(solution)/shard_map/ppermute | solution.py:32
  211.2 3.8 %collective-permute-start.26 = (bf16[512,768]{1,0:T(8,128)(2,1)}, bf16[512,768]{1,0:T(8,128)(2,1)}, u32[]{:S(2)}, u32[]{:S(2)}) collective-permute-start(bf16[512,768]{1,0:T(8,128)(2,1)} %get-tuple-element.39), channel_id=1, source_target_pairs={{0,32},{32,0},{64,96},{96,64},{128,160},{160,128},{192,224},{224,1... | collective-permute-start | bytes 2359304 | tf_op jit(solution)/shard_map/ppermute | solution.py:32
  211.3 20.8 %collective-permute-start.27 = (bf16[512,768]{1,0:T(8,128)(2,1)}, bf16[512,768]{1,0:T(8,128)(2,1)}, u32[]{:S(2)}, u32[]{:S(2)}) collective-permute-start(bf16[512,768]{1,0:T(8,128)(2,1)} %get-tuple-element.40), channel_id=1, source_target_pairs={{0,32},{32,0},{64,96},{96,64},{128,160},{160,128},{192,224},{224,1... | collective-permute-start | bytes 2359304 | tf_op jit(solution)/shard_map/ppermute | solution.py:32
  214.9 17.1 %copy-start.15 = (bf16[512,768]{1,0:T(8,128)(2,1)S(1)}, bf16[512,768]{1,0:T(8,128)(2,1)}, u32[]{:S(2)}) copy-start(bf16[512,768]{1,0:T(8,128)(2,1)} %get-tuple-element.40) | copy-start | bytes 2359300
  222.4 14.2 %collective-permute-start.24 = (bf16[16,1024]{1,0:T(8,128)(2,1)S(1)}, bf16[16,1024]{1,0:T(8,128)(2,1)S(1)}, u32[]{:S(2)}, u32[]{:S(2)}) collective-permute-start(bf16[16,1024]{1,0:T(8,128)(2,1)S(1)} %slice.64), channel_id=1, source_target_pairs={{0,32},{32,0},{64,96},{96,64},{128,160},{160,128},{192,224},{224,1... | collective-permute-start | bytes 98312 | tf_op jit(solution)/shard_map/ppermute | solution.py:32
  236.5 1.3 collective-permute-start.23

commit v4 on v3

--- a/solution.py
+++ b/solution.py
@@ -9,10 +9,15 @@
 F32 = jnp.float32
 NX, NC, NZ, NY = 4, 2, 8, 4
 MIB = 1024 * 1024
+LIMIT = 24
+TILE = 256
 
 X_GROUPS = [[x * NC + c for x in range(NX)] for c in range(NC)]
 Y_GROUPS = [[z * NY + y for y in range(NY)] for z in range(NZ)]
 Z_GROUPS = [[z * NY + y for z in range(NZ)] for y in range(NY)]
+Y_STEP = [
+    [(z * NY + y, z * NY + (y + k) % NY) for z in range(NZ) for y in range(NY)] for k in range(NY)
+]
 Z_UP = [(z * NY + y, (z + 1) % NZ * NY + y) for z in range(NZ) for y in range(NY)]
 Z_DOWN = [(dst, src) for src, dst in Z_UP]
 X_UP = [(x * NC + c, (x + 1) % NX * NC + c) for x in range(NX) for c in range(NC)]
@@ -64,6 +69,7 @@
         behind.append(lax.ppermute(behind[-1], axis, down))
     top = lax.ppermute(before[3][:half], axis, up)
     bottom = lax.ppermute(behind[3][half:], axis, down)
+    behind[2:3], before[2:3] = [in_hbm(behind[2])], [in_hbm(before[2])]
     return own, behind[1], behind[2], behind[3], top, bottom, before[3], before[2], before[1]
 
 
@@ -75,7 +81,11 @@
     return pltpu.HBM(shape, dtype)
 
 
-def call(kernel, grid, in_specs, out_specs, out_shape, flops, scratch=(), limit=24):
+def in_hbm(value):
+    return pltpu.with_memory_space_constraint(value, pltpu.HBM)
+
+
+def call(kernel, grid, in_specs, out_specs, out_shape, flops, scratch=(), limit=LIMIT):
     return pl.pallas_call(
         kernel,
         grid_spec=pltpu.PrefetchScalarGridSpec(
@@ -102,13 +112,13 @@
 
 
 def place_eight(index, blocks, store):
-    groups = blocks[0].shape[0] // 16
     steps = (0, 1, 2, 3, 4, 4, 5, 6, 7)
     for block, step in zip(blocks, steps):
-        z = lax.rem(index + step, NZ)
-        first = groups // 2 if block is blocks[5] else 0
+        z = lax.rem(index[0] + step, NZ)
+        first = NY // 2 if block is blocks[5] else 0
         for k in range(block.shape[0] // 16):
-            start = pl.multiple_of((first + k) * NZ * 16 + z * 16, 16)
+            y = lax.rem(index[1] + first + k, NY)
+            start = pl.multiple_of(y * NZ * 16 + z * 16, 16)
             store(start, block[k * 16 : (k + 1) * 16, :])
 
 
@@ -121,19 +131,13 @@
         def store(start, value):
             tok_b[pl.ds(start, 16), :] = value
 
-        place_eight(index[0], blocks, store)
-
-    def part(one, two):
-        total = dot(tok_a[...], one[...], NN) + dot(tok_b[...], two[...], NN)
-        out[...] = total.astype(BF16)
-
-    @pl.when(step < pl.num_programs(0) // 2)
-    def _():
-        part(gate_a, gate_b)
-
-    @pl.when(step >= pl.num_programs(0) // 2)
-    def _():
-        part(up_a, up_b)
+        place_eight(index, blocks, store)
+
+    tile = gate_a.shape[1]
+    gate = dot(tok_a[...], gate_a[...], NN) + dot(tok_b[...], gate_b[...], NN)
+    out[:, :tile] = gate.astype(BF16)
+    up = dot(tok_a[...], up_a[...], NN) + dot(tok_b[...], up_b[...], NN)
+    out[:, tile:] = up.astype(BF16)
 
 
 def columns(rows, width, at):
@@ -143,17 +147,14 @@
 def gate_up_product(index, own, blocks, gate_a, gate_b, up_a, up_b):
     rows = own.shape[0]
     width, cols = gate_a.shape
-    tile = 256
-    steps = cols // tile
-    first = pl.BlockSpec((width, tile), lambda j, _: (0, jnp.minimum(j, steps - 1)))
-    second = pl.BlockSpec((width, tile), lambda j, _: (0, jnp.maximum(j - steps, 0)))
+    weight = pl.BlockSpec((width, TILE), lambda j, _: (0, j))
     return call(
         gate_up_kernel,
-        (2 * steps,),
+        (cols // TILE,),
         [columns(rows, width, 0)]
         + [columns(block.shape[0], width, 0) for block in blocks]
-        + [first, first, second, second],
-        [pl.BlockSpec((rows, tile), lambda j, _: (0, j)), whole((rows, width))],
+        + [weight] * 4,
+        [pl.BlockSpec((rows, 2 * TILE), lambda j, _: (0, j)), whole((rows, width))],
         [hbm((rows, 2 * cols)), hbm((rows, width))],
         8 * rows * width * cols,
     )(index, own, *blocks, gate_a, gate_b, up_a, up_b)
@@ -167,7 +168,7 @@
         def store(start, value):
             grad_b[pl.ds(start, 16), :] = value
 
-        place_eight(index[0], blocks, store)
+        place_eight(index, blocks, store)
 
     total = dot(grad_a[...], down_a[...], NT) + dot(grad_b[...], down_b[...], NT)
     out[...] = total.astype(BF16)
@@ -176,7 +177,7 @@
 def hidden_term_product(index, own, blocks, down_a, down_b):
     rows = own.shape[0]
     cols, width = down_a.shape
-    tile = 256
+    tile = 384
     weight = pl.BlockSpec((tile, width), lambda j, _: (j, 0))
     return call(
         hidden_term_kernel,
@@ -263,7 +264,7 @@
 def input_product(index, blocks, gate_a, up_a, gate_b, up_b):
     rows = blocks[0].shape[0]
     width, cols = gate_a.shape
-    tile = 256
+    tile = 512
     steps = width // tile
     first = pl.BlockSpec((tile, cols), lambda j, _: (jnp.minimum(j, steps - 1), 0))
     second = pl.BlockSpec((tile, cols), lambda j, _: (jnp.maximum(j - steps, 0), 0))
@@ -288,10 +289,11 @@
 def hidden_kernel(index, terms, gate_up, hidden):
     del index
     total = total_of(terms)
-    cols = hidden.shape[1]
-    gate, up = total[:, :cols], total[:, cols:]
     gate_up[...] = total
-    hidden[...] = (gate * jax.nn.sigmoid(gate) * up).astype(BF16)
+    for k in range(hidden.shape[1] // TILE):
+        gate = total[:, 2 * k * TILE : (2 * k + 1) * TILE]
+        up = total[:, (2 * k + 1) * TILE : (2 * k + 2) * TILE]
+        hidden[:, k * TILE : (k + 1) * TILE] = (gate * jax.nn.sigmoid(gate) * up).astype(BF16)
 
 
 def hidden_of(index, terms):
@@ -302,7 +304,7 @@
         [whole(terms.shape)],
         [whole((rows, cols)), whole((rows, cols // 2))],
         [
-            jax.ShapeDtypeStruct((rows, cols), F32),
+            hbm((rows, cols), F32),
             jax.ShapeDtypeStruct((rows, cols // 2), BF16),
         ],
         16 * rows * cols,
@@ -311,12 +313,16 @@
 
 def pre_kernel(index, terms, gate_up, out):
     del index
-    hidden_grad = total_of(terms)
-    cols = hidden_grad.shape[1]
-    gate, up = gate_up[:, :cols], gate_up[:, cols:]
-    sig = jax.nn.sigmoid(gate)
-    out[:, :cols] = (hidden_grad * up * sig * (1.0 + gate * (1.0 - sig))).astype(BF16)
-    out[:, cols:] = (hidden_grad * gate * sig).astype(BF16)
+    total = total_of(terms)
+    cols = total.shape[1]
+    for k in range(cols // TILE):
+        hidden_grad = total[:, k * TILE : (k + 1) * TILE]
+        gate = gate_up[:, 2 * k * TILE : (2 * k + 1) * TILE]
+        up = gate_up[:, (2 * k + 1) * TILE : (2 * k + 2) * TILE]
+        sig = jax.nn.sigmoid(gate)
+        pre_gate = hidden_grad * up * sig * (1.0 + gate * (1.0 - sig))
+        out[:, k * TILE : (k + 1) * TILE] = pre_gate.astype(BF16)
+        out[:, cols + k * TILE : cols + (k + 1) * TILE] = (hidden_grad * gate * sig).astype(BF16)
 
 
 def pre_grads(index, terms, gate_up):
@@ -352,7 +358,8 @@
 def body(tokens, gate_weight, up_weight, down_weight, out_grad):
     core = lax.axis_index("row") % NC
     x = (lax.axis_index("row") // NC).astype(jnp.int32).reshape(1)
-    z = (lax.axis_index("col") // NY).astype(jnp.int32).reshape(1)
+    col = lax.axis_index("col")
+    zy = jnp.stack([col // NY, col % NY]).astype(jnp.int32)
     half = tokens.shape[0] // NC
     width = tokens.shape[1]
 
@@ -372,29 +379,30 @@
     grad_a, grad_b = halves(out_grad)
     own = jnp.concatenate([tok_a, grad_a], axis=1)
     other = jnp.concatenate([tok_b, grad_b], axis=1)
-    gate_other = swap_core(gate_weight)
-    up_other = swap_core(up_weight)
-    down_other = swap_core(down_weight)
-
-    other_y = share(other, "col", Y_GROUPS)
+    gate_own, gate_other = in_hbm(gate_weight), in_hbm(swap_core(gate_weight))
+    up_own, up_other = in_hbm(up_weight), in_hbm(swap_core(up_weight))
+    down_own, down_other = in_hbm(down_weight), in_hbm(swap_core(down_weight))
+
+    other_y = [other] + [lax.ppermute(other, "col", Y_STEP[NY - k]) for k in range(1, NY)]
+    other_y = jnp.concatenate(other_y, axis=0)
     other_blocks = ring_eight(other_y, "col", Z_UP, Z_DOWN)
-    own_z = share(after(own, other_y), "col", Z_GROUPS)
+    own_z = share(own, "col", Z_GROUPS)
     own_all = share(after(own_z, other_blocks[1], other_blocks[8]), "col", Y_GROUPS)
 
     gate_up_term, tok_other = gate_up_product(
-        z, own_all, other_blocks, gate_weight, gate_other, up_weight, up_other
+        zy, own_all, other_blocks, gate_own, gate_other, up_own, up_other
     )
-    gate_up, hidden_own = hidden_of(z, exchange(gate_up_term, "row", X_GROUPS))
+    gate_up, hidden_own = hidden_of(x, exchange(gate_up_term, "row", X_GROUPS))
     hidden_term, grad_other = hidden_term_product(
-        z, own_all, other_blocks, down_weight, down_other
+        zy, own_all, other_blocks, down_own, down_other
     )
     pre_own = pre_grads(x, exchange(hidden_term, "row", X_GROUPS), gate_up)
 
     hidden_blocks = ring_blocks(hidden_own, "row", X_UP, X_DOWN)
-    mixed_term, hidden = mixed_product(after(x, pre_own), hidden_blocks, down_weight, down_other)
+    mixed_term, hidden = mixed_product(after(x, pre_own), hidden_blocks, down_own, down_other)
     pre_blocks = ring_blocks(after(pre_own, *hidden_blocks), "row", X_UP, X_DOWN)
     input_term, pre_gate, pre_up = input_product(
-        after(x, mixed_term), pre_blocks, gate_weight, up_weight, gate_other, up_other
+        after(x, mixed_term), pre_blocks, gate_own, up_own, gate_other, up_other
     )
     mixed_y = exchange(mixed_term, "col", Y_GROUPS)
     input_y = exchange(after(input_term, mixed_y), "col", Y_GROUPS)
@@ -406,8 +414,8 @@
     down_grad = dot(all_tokens(hidden), grad_rows, TN).astype(BF16)
     gate_grad = dot(tok_rows, all_tokens(pre_gate), TN).astype(BF16)
     up_grad = dot(tok_rows, all_tokens(pre_up), TN).astype(BF16)
-    sums = sums_of(x, mixed_y, after(input_y, down_grad))
-    sums = exchange(sums, "col", Z_GROUPS).astype(F32).sum(0).astype(BF16)
+    sums = sums_of(x, mixed_y, after(input_y, down_grad, gate_grad))
+    sums = after(exchange(sums, "col", Z_GROUPS), up_grad).astype(F32).sum(0).astype(BF16)
     mixed = join(sums[:, : 2 * width])
     input_grad = join(sums[:, 2 * width :])
 

time: 240 us -> 228 us (0.950)
  local copies, waits for them, and re-layouts: 18.8 us -> 10.9 us
    all_to_all x8 -> x7, waiting for transfers between devices: 26.6 us -> 38.2 us  [exchange(): lax.all_to_all(value, axis, 0, 0, axis_index_groups=groups, tiled=True)]
    ppermute x3, waiting for transfers between devices: 20.1 us -> 12.1 us  [ring_eight(): before.append(lax.ppermute(before[-1], axis, up))]
    unnamed x32 -> x19, local copies, waits for them, and re-layouts: 11.2 us -> 3.97 us
    ppermute x12, starting transfers between devices: 36 us -> 29.9 us  [swap_core(): return lax.ppermute(value, 'row', CORE_PAIRS)]
    ppermute x2, waiting for transfers between devices: 5.78 us -> 0.25 us  [ring_blocks(): top = lax.ppermute(before[:half], axis, up)]
    ppermute x0 -> x3, starting transfers between devices: none -> 4.99 us  [body(): lax.ppermute(other, 'col', Y_STEP[NY - k])]
    ppermute x12, waiting for transfers between devices: 8.24 us -> 5.74 us  [swap_core(): return lax.ppermute(value, 'row', CORE_PAIRS)]
    ppermute x0 -> x3, waiting for transfers between devices: none -> 2.41 us  [body(): lax.ppermute(other, 'col', Y_STEP[NY - k])]
  transfers between devices with their start and end apart: 36 -> 38, of which waited for: 22 -> 20; matrix products, arithmetic and copies ran while one was open for 8% -> 8% of each run, Pallas kernels for 10% -> 10%
where the time goes in v4:
time: 228 us; the launch traced here: 227 us
  starting transfers between devices  93.8 us (41%)
  waiting for transfers between devices  73.6 us (32%)
  Pallas kernels  33.2 us (15%)
  matrix products  12.8 us (6%)
  local copies, waits for them, and re-layouts  10.9 us (5%)
    all_to_all x7, waiting for transfers between devices, exchange(): lax.all_to_all(value, axis, 0, 0, axis_index_groups=groups, tiled=True)  38.2 us
    all_to_all x7, starting transfers between devices, exchange(): lax.all_to_all(value, axis, 0, 0, axis_index_groups=groups, tiled=True)  36.3 us
    ppermute x12, starting transfers between devices, swap_core(): return lax.ppermute(value, 'row', CORE_PAIRS)  29.9 us
    dot_general x3, matrix products, dot(): return lax.dot_general(left, right, dims, preferred_element_type=F32)  12.8 us
    ppermute x2, waiting for transfers between devices, ring_blocks(): before = lax.ppermute(own, axis, up)  12.5 us
    ppermute x3, waiting for transfers between devices, ring_eight(): before.append(lax.ppermute(before[-1], axis, up))  12.1 us
    pallas_call x1, Pallas kernels, input_product(): call(input_kernel, (2 * steps,), [whole(block.shape) for block in blocks]...  8.1 us
    pallas_call x1, Pallas kernels, gate_up_product(): call(gate_up_kernel, (cols // TILE,), [columns(rows, width, 0)] + [column...  7.35 us
  transfers between devices with their start and end apart: 38, of which 20 were waited for; matrix products, arithmetic and copies ran while one was open for 8% of the time, Pallas kernels for 10%

profile of v4, /device:TPU:1, one launch (start us, length us, event | category | flops | bytes accessed | tf_op | source)
XLA Modules:
  0.0 226.6 jit_solution(1487810593512454156)
XLA Ops:
  0.7 0.8 constant_dynamic-slice_fusion.1
  1.4 0.8 constant_dynamic-slice_fusion
  2.2 0.8 tile.4
  3.1 9.0 %all-to-all-start = ((bf16[8,16,2048]{2,1,0:T(8,128)(2,1)}), bf16[8,16,2048]{2,1,0:T(8,128)(2,1)S(1)}, u32[]{:S(2)}, u32[]{:S(2)}) async-start(bf16[8,16,2048]{2,1,0:T(8,128)(2,1)} %tile.4), calls=%async_computation | async-start | bytes 1048576 | tf_op jit(solution)/shard_map/all_to_all | solution.py:42
  12.1 1.0 collective-permute-start
  13.1 0.8 collective-permute-done
  14.3 1.3 collective-permute-start.4
  15.6 2.6 %collective-permute-start.3 = (bf16[16,2048]{1,0:T(8,128)(2,1)S(1)}, bf16[16,2048]{1,0:T(8,128)(2,1)S(1)}, u32[]{:S(2)}, u32[]{:S(2)}) collective-permute-start(bf16[16,2048]{1,0:T(8,128)(2,1)S(1)} %constant_dynamic-update-slice_fusion), channel_id=1, source_target_pairs={{0,2},{1,3},{2,0},{3,1},{4,6},{5,7},{6,4},{7,5},{8,10},{9,11},{10,... | collective-permute-start | bytes 196616 | tf_op jit(solution)/shard_map/ppermute | solution.py:386
  18.2 1.1 collective-permute-start.2
  19.2 2.4 %collective-permute-done.3 = bf16[16,2048]{1,0:T(8,128)(2,1)S(1)} collective-permute-done((bf16[16,2048]{1,0:T(8,128)(2,1)S(1)}, bf16[16,2048]{1,0:T(8,128)(2,1)S(1)}, u32[]{:S(2)}, u32[]{:S(2)}) %collective-permute-start.3) | collective-permute-done | bytes 65568 | tf_op jit(solution)/shard_map/ppermute | solution.py:386
  21.7 1.8 collective-permute-start.6
  23.5 1.3 collective-permute-start.5
  24.8 1.8 collective-permute-start.14
  26.6 6.2 %collective-permute-done.6.refs_8_ = bf16[64,2048]{1,0:T(8,128)(2,1)S(1)} collective-permute-done((bf16[64,2048]{1,0:T(8,128)(2,1)S(1)}, bf16[64,2048]{1,0:T(8,128)(2,1)S(1)}, u32[]{:S(2)}, u32[]{:S(2)}) %collective-permute-start.6) | collective-permute-done | bytes 262176 | tf_op jit(solution)/shard_map/ppermute | solution.py:68
  32.8 1.6 tile.5
  34.4 3.6 %all-to-all-start.1 = ((bf16[4,128,2048]{2,1,0:T(8,128)(2,1)}), bf16[4,128,2048]{2,1,0:T(8,128)(2,1)S(1)}, u32[]{:S(2)}, u32[]{:S(2)}) async-start(bf16[4,128,2048]{2,1,0:T(8,128)(2,1)} %tile.5), calls=%async_computation.1 | async-start | bytes 4194304 | tf_op jit(solution)/shard_map/all_to_all | solution.py:42
  38.2 2.6 %collective-permute-start.7 = (bf16[64,2048]{1,0:T(8,128)(2,1)S(1)}, bf16[64,2048]{1,0:T(8,128)(2,1)S(1)}, u32[]{:S(2)}, u32[]{:S(2)}) collective-permute-start(bf16[64,2048]{1,0:T(8,128)(2,1)S(1)} %collective-permute-done.5.refs_1_), channel_id=1, source_target_pairs={{4,0},{5,1},{6,2},{7,3},{8,4},{9,5},{10,6},{11,7},{12,8},{13,9},{1... | collective-permute-start | bytes 786440 | tf_op jit(solution)/shard_map/ppermute | solution.py:69
  40.8 4.8 %collective-permute-done.9.refs_7_ = bf16[64,2048]{1,0:T(8,128)(2,1)S(1)} collective-permute-done((bf16[64,2048]{1,0:T(8,128)(2,1)S(1)}, bf16[64,2048]{1,0:T(8,128)(2,1)S(1)}, u32[]{:S(2)}, u32[]{:S(2)}) %collective-permute-start.9) | collective-permute-done | bytes 262176 | tf_op jit(solution)/shard_map/ppermute | solution.py:68
  45.6 2.7 %collective-permute-start.8 = (bf16[64,2048]{1,0:T(8,128)(2,1)S(1)}, bf16[64,2048]{1,0:T(8,128)(2,1)S(1)}, u32[]{:S(2)}, u32[]{:S(2)}) collective-permute-start(bf16[64,2048]{1,0:T(8,128)(2,1)S(1)} %collective-permute-done.7.refs_2_), channel_id=1, source_target_pairs={{4,0},{5,1},{6,2},{7,3},{8,4},{9,5},{10,6},{11,7},{12,8},{13,9},{1... | collective-permute-start | bytes 786440 | tf_op jit(solution)/shard_map/ppermute | solution.py:69
  48.3 3.0 %collective-permute-start.13 = (bf16[768,1024]{1,0:T(8,128)(2,1)}, bf16[768,1024]{1,0:T(8,128)(2,1)}, u32[]{:S(2)}, u32[]{:S(2)}) collective-permute-start(bf16[768,1024]{1,0:T(8,128)(2,1)} %down_a.1), channel_id=1, source_target_pairs={{0,32},{32,0},{64,96},{96,64},{128,160},{160,128},{192,224},{224,1... | collective-permute-start | bytes 4718600 | tf_op jit(solution)/shard_map/ppermute | solution.py:37
  51.3 1.1 collective-permute-done.10.refs_6_
  52.3 0.7 slice.54
  53.0 0.7 slice.55
  53.7 2.7 %collective-permute-start.12 = (bf16[32,2048]{1,0:T(8,128)(2,1)}, bf16[32,2048]{1,0:T(8,128)(2,1)}, u32[]{:S(2)}, u32[]{:S(2)}) collective-permute-start(bf16[32,2048]{1,0:T(8,128)(2,1)} %slice.55), channel_id=1, source_target_pairs={{4,0},{5,1},{6,2},{7,3},{8,4},{9,5},{10,6},{11,7},{12,8},{13,9},{1... | collective-permute-start | bytes 393224 | tf_op jit(solution)/shard_map/ppermute | solution.py:71
  56.4 2.1 collective-permute-done.11.refs_4_
  58.6 4.1 %all-to-all-done.1 = bf16[4,128,2048]{2,1,0:T(8,128)(2,1)S(1)} async-done(((bf16[4,128,2048]{2,1,0:T(8,128)(2,1)}), bf16[4,128,2048]{2,1,0:T(8,128)(2,1)S(1)}, u32[]{:S(2)}, u32[]{:S(2)}) %all-to-all-start.1) | async-done | bytes 2097184 | tf_op jit(solution)/shard_map/all_to_all | solution.py:42
  62.7 7.4 %shard_map.93 = (bf16[512,1536]{1,0:T(8,128)(2,1)}, bf16[512,1024]{1,0:T(8,128)(2,1)}) custom-call(s32[2]{0:T(128)S(1)} %pad_add_fusion.index, bf16[512,2048]{1,0:T(8,128)(2,1)S(1)} %bitcast.10, bf16[64,2048]{1,0:T(8,128)(2,1)S(1)} %pad_maximum_fusion.3.refs_0_, bf16[64,2048]{1,0:T(8,128)(2,1)S(1)} %collective-permute-done.5.refs_1_, ...), custom_call_target="tpu_custom_call" | custom-call | flops 3221225472 | bytes 10485760 | tf_op jit(solution)/shard_map/pallas_call | solution.py:151
  70.1 4.3 %all-to-all-start.3 = ((bf16[4,128,1536]{2,1,0:T(8,128)(2,1)}), bf16[4,128,1536]{2,1,0:T(8,128)(2,1)}, u32[]{:S(2)}, u32[]{:S(2)}) async-start(bf16[4,128,1536]{2,1,0:T(8,128)(2,1)} %bitcast.16), calls=%async_computation.3 | async-start | bytes 3145728 | tf_op jit(solution)/shard_map/all_to_all | solution.py:42
  74.4 5.5 %shard_map.92 = (bf16[512,768]{1,0:T(8,128)(2,1)}, bf16[512,1024]{1,0:T(8,128)(2,1)}) custom-call(s32[2]{0:T(128)S(1)} %pad_add_fusion.index, bf16[512,2048]{1,0:T(8,128)(2,1)S(1)} %bitcast.11, bf16[64,2048]{1,0:T(8,128)(2,1)S(1)} %pad_maximum_fusion.3.refs_0_, bf16[64,2048]{1,0:T(8,128)(2,1)S(1)} %collective-permute-done.5.refs_1_, ...), custom_call_target="tpu_custom_call" | custom-call | flops 1610612736 | bytes 10485760 | tf_op jit(solution)/shard_map/pallas_call | solution.py:182
  79.9 12.7 %all-to-all-done.3.terms = bf16[4,128,1536]{2,1,0:T(8,128)(2,1)} async-done(((bf16[4,128,1536]{2,1,0:T(8,128)(2,1)}), bf16[4,128,1536]{2,1,0:T(8,128)(2,1)}, u32[]{:S(2)}, u32[]{:S(2)}) %all-to-all-start.3) | async-done | bytes 1572896 | tf_op jit(solution)/shard_map/all_to_all | solution.py:42
  92.7 3.5 %all-to-all-start.2 = ((bf16[4,128,768]{2,1,0:T(8,128)(2,1)}), bf16[4,128,768]{2,1,0:T(8,128)(2,1)S(1)}, u32[]{:S(2)}, u32[]{:S(2)}) async-start(bf16[4,128,768]{2,1,0:T(8,128)(2,1)} %bitcast.17), calls=%async_computation.2 | async-start | bytes 1572864 | tf_op jit(solution)/shard_map/all_to_all | solution.py:42
  96.2 2.5 %shard_map.94 = (f32[128,1536]{1,0:T(8,128)}, bf16[128,768]{1,0:T(8,128)(2,1)S(1)}) custom-call(s32[1]{0:T(128)} %bitcast.index, bf16[4,128,1536]{2,1,0:T(8,128)(2,1)} %all-to-all-done.3.terms), custom_call_target="tpu_custom_call" | custom-call | flops 3145728 | bytes 10485760 | tf_op jit(solution)/shard_map/pallas_call | solution.py:301
  98.7 1.4 collective-permute-start.17
  100.1 1.3 collective-permute-start.16
  101.4 7.4 %collective-permute-done.17.before = bf16[128,768]{1,0:T(8,128)(2,1)S(1)} collective-permute-done((bf16[128,768]{1,0:T(8,128)(2,1)S(1)}, bf16[128,768]{1,0:T(8,128)(2,1)S(1)}, u32[]{:S(2)}, u32[]{:S(2)}) %collective-permute-start.17) | collective-permute-done | bytes 196640 | tf_op jit(solution)/shard_map/ppermute | solution.py:57
  108.8 0.6 slice.56
  109.4 0.7 slice.57
  110.1 2.7 %collective-permute-start.19 = (bf16[64,768]{1,0:T(8,128)(2,1)}, bf16[64,768]{1,0:T(8,128)(2,1)}, u32[]{:S(2)}, u32[]{:S(2)}) collective-permute-start(bf16[64,768]{1,0:T(8,128)(2,1)} %slice.57), channel_id=1, source_target_pairs={{64,0},{96,32},{128,64},{160,96},{192,128},{224,160},{0,192},{32,2... | collective-permute-start | bytes 294920 | tf_op jit(solution)/shard_map/ppermute | solution.py:60
  112.8 1.1 copy-done
  114.7 0.9 copy-done.2
  115.6 0.9 copy-done.4
  116.6 5.7 %shard_map.96 = (bf16[512,2048]{1,0:T(8,128)(2,1)}, bf16[512,768]{1,0:T(8,128)(2,1)}) custom-call(s32[1]{0:T(128)} %bitcast.index, bf16[128,768]{1,0:T(8,128)(2,1)S(1)} %copy-done.4, bf16[128,768]{1,0:T(8,128)(2,1)S(1)} %copy-done.2, bf16[64,768]{1,0:T(8,128)(2,1)} %collective-permute-done.18.top, bf16[64,768]{1,0:T(8,128)(2,1)} %collective-permute-done.19.bottom, ...), custom_call_target="tpu_custom_call" | custom-call | flops 1610612736 | bytes 10485760 | tf_op jit(solution)/shard_map/pallas_call | solution.py:221
  122.3 4.5 %all-to-all-start.4 = ((bf16[4,128,2048]{2,1,0:T(8,128)(2,1)}), bf16[4,128,2048]{2,1,0:T(8,128)(2,1)}, u32[]{:S(2)}, u32[]{:S(2)}) async-start(bf16[4,128,2048]{2,1,0:T(8,128)(2,1)} %bitcast.14), calls=%async_computation.4 | async-start | bytes 4194304 | tf_op jit(solution)/shard_map/all_to_all | solution.py:42
  126.8 1.5 collective-permute-start.21
  128.2 1.8 collective-permute-start.20
  130.0 5.1 %collective-permute-done.21.before = bf16[128,1536]{1,0:T(8,128)(2,1)S(1)} collective-permute-done((bf16[128,1536]{1,0:T(8,128)(2,1)S(1)}, bf16[128,1536]{1,0:T(8,128)(2,1)S(1)}, u32[]{:S(2)}, u32[]{:S(2)}) %collective-permute-start.21) | collective-permute-done | bytes 393248 | tf_op jit(solution)/shard_map/ppermute | solution.py:57
  135.2 2.7 %collective-permute-start.23 = (bf16[64,1536]{1,0:T(8,128)(2,1)S(1)}, bf16[64,1536]{1,0:T(8,128)(2,1)S(1)}, u32[]{:S(2)}, u32[]{:S(2)}) collective-permute-start(bf16[64,1536]{1,0:T(8,128)(2,1)S(1)} %slice.59), channel_id=1, source_target_pairs={{64,0},{96,32},{128,64},{160,96},{192,128},{224,160},{0,192},{32,2... | collective-permute-start | bytes 589832 | tf_op jit(solution)/shard_map/ppermute | solution.py:60
  137.9 9.7 %collective-permute-start.25 = (bf16[512,1024]{1,0:T(8,128)(2,1)}, bf16[512,1024]{1,0:T(8,128)(2,1)}, u32[]{:S(2)}, u32[]{:S(2)}) collective-permute-start(bf16[512,1024]{1,0:T(8,128)(2,1)} %get-tuple-element.35), channel_id=1, source_target_pairs={{0,32},{32,0},{64,96},{96,64},{128,160},{160,128},{192,224},{224,1... | collective-permute-start | bytes 3145736 | tf_op jit(solution)/shard_map/ppermute | solution.py:37
  147.7 8.1 %shard_map.97 = (bf16[512,2048]{1,0:T(8,128)(2,1)}, bf16[512,768]{1,0:T(8,128)(2,1)}, bf16[512,768]{1,0:T(8,128)(2,1)}) custom-call(s32[1]{0:T(128)} %bitcast.index, bf16[128,1536]{1,0:T(8,128)(2,1)S(1)} %shard_map.95.own, bf16[128,1536]{1,0:T(8,128)(2,1)S(1)} %collective-permute-done.20.behind, bf16[64,1536]{1,0:T(8,128)(2,1)S(1)} %collective-permute-done.22.top, ...), custom_call_target="tpu_custom_call" | custom-call | flops 3221225472 | bytes 10485760 | tf_op jit(solution)/shard_map/pallas_call | solution.py:272
  155.8 4.5 %all-to-all-start.5 = ((bf16[4,128,2048]{2,1,0:T(8,128)(2,1)}), bf16[4,128,2048]{2,1,0:T(8,128)(2,1)}, u32[]{:S(2)}, u32[]{:S(2)}) async-start(bf16[4,128,2048]{2,1,0:T(8,128)(2,1)} %bitcast.15), calls=%async_computation.5 | async-start | bytes 4194304 | tf_op jit(solution)/shard_map/all_to_all | solution.py:42
  160.2 3.8 %collective-permute-start.24 = (bf16[512,768]{1,0:T(8,128)(2,1)}, bf16[512,768]{1,0:T(8,128)(2,1)S(1)}, u32[]{:S(2)}, u32[]{:S(2)}) collective-permute-start(bf16[512,768]{1,0:T(8,128)(2,1)} %get-tuple-element.34), channel_id=1, source_target_pairs={{0,32},{32,0},{64,96},{96,64},{128,160},{160,128},{192,224},{224,1... | collective-permute-start | bytes 2359304 | tf_op jit(solution)/shard_map/ppermute | solution.py:37
  164.8 1.4 collective-permute-done.24
  166.2 4.5 %fusion.4 = bf16[768,1024]{1,0:T(8,128)(2,1)} fusion(bf16[512,1024]{1,0:T(8,128)(2,1)} %collective-permute-done.25, bf16[512,1024]{1,0:T(8,128)(2,1)S(1)} %get-tuple-element.42, bf16[512,768]{1,0:T(8,128)(2,1)S(1)} %collective-permute-done.24, bf16[512,768]{1,0:T(8,128)(2,1)} %get-tuple-element.34), kind=kOutput, calls=%fused_computation.5 | convolution fusion | flops 1618739200 | bytes 5242880 | tf_op jit(solution)/shard_map/dot_general | solution.py:33
  170.7 1.0 copy-done.7
  171.6 4.2 %convolution_convert_fusion.1 = bf16[1024,768]{1,0:T(8,128)(2,1)} fusion(bf16[512,768]{1,0:T(8,128)(2,1)S(1)} %collective-permute-done.27, bf16[512,768]{1,0:T(8,128)(2,1)} %get-tuple-element.37, bf16[512,1024]{1,0:T(8,128)(2,1)S(1)} %collective-permute-done.26, bf16[512,1024]{1,0:T(8,128)(2,1)S(1)} %get-tuple-element.41), kind=kOutput, calls=%fused_computation.7 | convolution fusion | flops 1618739200 | bytes 5242880 | tf_op jit(solution)/shard_map/dot_general | solution.py:33
  175.8 7.3 %all-to-all-done.5.two = bf16[4,128,2048]{2,1,0:T(8,128)(2,1)} async-done(((bf16[4,128,2048]{2,1,0:T(8,128)(2,1)}), bf16[4,128,2048]{2,1,0:T(8,128)(2,1)}, u32[]{:S(2)}, u32[]{:S(2)}) %all-to-all-start.5) | async-done | bytes 2097184 | tf_op jit(solution)/shard_map/all_to_all | solution.py:42
  183.2 3.7 %shard_map.98 = bf16[128,4096]{1,0:T(8,128)(2,1)} custom-call(s32[1]{0:T(128)} %bitcast.index, bf16[4,128,2048]{2,1,0:T(8,128)(2,1)} %all-to-all-done.4.one, bf16[4,128,2048]{2,1,0:T(8,128)(2,1)} %all-to-all-done.5.two), custom_call_target="tpu_custom_call" | custom-call | flops 4194304 | bytes 10485760 | tf_op jit(solution)/shard_map/pallas_call | solution.py:348
  186.9 6.9 %all-to-all-start.6 = ((bf16[8,16,4096]{2,1,0:T(8,128)(2,1)}), bf16[8,16,4096]{2,1,0:T(8,128)(2,1)S(1)}, u32[]{:S(2)}, u32[]{:S(2)}) async-start(bf16[8,16,4096]{2,1,0:T(8,128)(2,1)} %bitcast.9), calls=%async_computation.6 | async-start | bytes 2097152 | tf_op jit(solution)/shard_map/all_to_all | solution.py:42
  193.8 4.9 %collective-permute-start.28 = (bf16[512,768]{1,0:T(8,128)(2,1)}, bf16[512,768]{1,0:T(8,128)(2,1)S(1)}, u32[]{:S(2)}, u32[]{:S(2)}) collective-permute-start(bf16[512,768]{1,0:T(8,128)(2,1)} %get-tuple-element.39), channel_id=1, source_target_pairs={{0,32},{32,0},{64,96},{96,64},{128,160},{160,128},{192,224},{224,1... | collective-permute-start | bytes 2359304 | tf_op jit(solution)/shard_map/ppermute | solution.py:37
  198.7 2.1 collective-permute-done.28
  200.8 4.1 %convolution_convert_fusion = bf16[1024,768]{1,0:T(8,128)(2,1)} fusion(bf16[512,768]{1,0:T(8,128)(2,1)S(1)} %collective-permute-done.28, bf16[512,768]{1,0:T(8,128)(2,1)} %get-tuple-element.39, bf16[512,1024]{1,0:T(8,128)(2,1)S(1)} %copy-done.8, bf16[512,1024]{1,0:T(8,128)(2,1)S(1)} %get-tuple-element.41), kind=kOutput, calls=%fused_computation.6 | convolution fusion | flops 1618739200 | bytes 5242880 | tf_op jit(solution)/shard_map/dot_general | solution.py:33
  204.9 14.0 %all-to-all-done.6 = bf16[8,16,4096]{2,1,0:T(8,128)(2,1)S(1)} async-done(((bf16[8,16,4096]{2,1,0:T(8,128)(2,1)}), bf16[8,16,4096]{2,1,0:T(8,128)(2,1)S(1)}, u32[]{:S(2)}, u32[]{:S(2)}) %all-to-all-start.6) | async-done | bytes 1048608 | tf_op jit(solution)/shard_map/all_to_all | solution.py:42
  219.1 4.7 %collective-permute-start.30 = (bf16[16,1024]{1,0:T(8,128)(2,1)S(1)}, bf16[16,1024]{1,0:T(8,128)(2,1)S(1)}, u32[]{:S(2)}, u32[]{:S(2)}) collective-permute-start(bf16[16,1024]{1,0:T(8,128)(2,1)S(1)} %slice.65), channel_id=1, source_target_pairs={{0,32},{32,0},{64,96},{96,64},{128,160},{160,128},{192,224},{224,1... | collective-permute-start | bytes 98312 | tf_op jit(solution)/shard_map/ppermute | solution.py:37
  223.8 0.9 collective-permute-done.30
  (62 shorter events, 4.6 us)
Async XLA Ops:
  3.1 29.7 %all-to-all-start = ((bf16[8,16,2048]{2,1,0:T(8,128)(2,1)}), bf16[8,16,2048]{2,1,0:T(8,128)(2,1)S(1)}, u32[]{:S(2)}, u32[]{:S(2)}) async-start(bf16[8,16,2048]{2,1,0:T(8,128)(2,1)} %tile.4), calls=%async_computation | async-start | bytes 1048576 | tf_op jit(solution)/shard_map/all_to_all | solution.py:42
  12.1 1.8 collective-permute-start
  13.0 1.2 collective-permute-start.1
  14.3 5.0 %collective-permute-start.4 = (bf16[16,2048]{1,0:T(8,128)(2,1)S(1)}, bf16[16,2048]{1,0:T(8,128)(2,1)S(1)}, u32[]{:S(2)}, u32[]{:S(2)}) collective-permute-start(bf16[16,2048]{1,0:T(8,128)(2,1)S(1)} %constant_dynamic-update-slice_fusion), channel_id=1, source_target_pairs={{0,1},{1,2},{2,3},{3,0},{4,5},{5,6},{6,7},{7,4},{8,9},{9,10},{10,1... | collective-permute-start | bytes 196616 | tf_op jit(solution)/shard_map/ppermute | solution.py:386
  15.6 6.1 %collective-permute-start.3 = (bf16[16,2048]{1,0:T(8,128)(2,1)S(1)}, bf16[16,2048]{1,0:T(8,128)(2,1)S(1)}, u32[]{:S(2)}, u32[]{:S(2)}) collective-permute-start(bf16[16,2048]{1,0:T(8,128)(2,1)S(1)} %constant_dynamic-update-slice_fusion), channel_id=1, source_target_pairs={{0,2},{1,3},{2,0},{3,1},{4,6},{5,7},{6,4},{7,5},{8,10},{9,11},{10,... | collective-permute-start | bytes 196616 | tf_op jit(solution)/shard_map/ppermute | solution.py:386
  18.2 3.5 %collective-permute-start.2 = (bf16[16,2048]{1,0:T(8,128)(2,1)S(1)}, bf16[16,2048]{1,0:T(8,128)(2,1)S(1)}, u32[]{:S(2)}, u32[]{:S(2)}) collective-permute-start(bf16[16,2048]{1,0:T(8,128)(2,1)S(1)} %constant_dynamic-update-slice_fusion), channel_id=1, source_target_pairs={{0,3},{1,0},{2,1},{3,2},{4,7},{5,4},{6,5},{7,6},{8,11},{9,8},{10,9... | collective-permute-start | bytes 196616 | tf_op jit(solution)/shard_map/ppermute | solution.py:386
  21.7 11.1 %collective-permute-start.6 = (bf16[64,2048]{1,0:T(8,128)(2,1)S(1)}, bf16[64,2048]{1,0:T(8,128)(2,1)S(1)}, u32[]{:S(2)}, u32[]{:S(2)}) collective-permute-start(bf16[64,2048]{1,0:T(8,128)(2,1)S(1)} %pad_maximum_fusion.3.refs_0_), channel_id=1, source_target_pairs={{0,4},{1,5},{2,6},{3,7},{4,8},{5,9},{6,10},{7,11},{8,12},{9,13},{1... | collective-permute-start | bytes 786440 | tf_op jit(solution)/shard_map/ppermute | solution.py:68
  23.5 9.3 %collective-permute-start.5 = (bf16[64,2048]{1,0:T(8,128)(2,1)S(1)}, bf16[64,2048]{1,0:T(8,128)(2,1)S(1)}, u32[]{:S(2)}, u32[]{:S(2)}) collective-permute-start(bf16[64,2048]{1,0:T(8,128)(2,1)S(1)} %pad_maximum_fusion.3.refs_0_), channel_id=1, source_target_pairs={{4,0},{5,1},{6,2},{7,3},{8,4},{9,5},{10,6},{11,7},{12,8},{13,9},{1... | collective-permute-start | bytes 786440 | tf_op jit(solution)/shard_map/ppermute | solution.py:69
  24.8 33.8 %collective-permute-start.14 = (bf16[1024,768]{1,0:T(8,128)(2,1)}, bf16[1024,768]{1,0:T(8,128)(2,1)}, u32[]{:S(2)}, u32[]{:S(2)}) collective-permute-start(bf16[1024,768]{1,0:T(8,128)(2,1)} %gate_a.1), channel_id=1, source_target_pairs={{0,32},{32,0},{64,96},{96,64},{128,160},{160,128},{192,224},{224,1... | collective-permute-start | bytes 4718600 | tf_op jit(solution)/shard_map/ppermute | solution.py:37
  26.6 32.0 %collective-permute-start.15 = (bf16[1024,768]{1,0:T(8,128)(2,1)}, bf16[1024,768]{1,0:T(8,128)(2,1)}, u32[]{:S(2)}, u32[]{:S(2)}) collective-permute-start(bf16[1024,768]{1,0:T(8,128)(2,1)} %up_a.1), channel_id=1, source_target_pairs={{0,32},{32,0},{64,96},{96,64},{128,160},{160,128},{192,224},{224,1... | collective-permute-start | bytes 4718600 | tf_op jit(solution)/shard_map/ppermute | solution.py:37
  34.4 28.3 %all-to-all-start.1 = ((bf16[4,128,2048]{2,1,0:T(8,128)(2,1)}), bf16[4,128,2048]{2,1,0:T(8,128)(2,1)S(1)}, u32[]{:S(2)}, u32[]{:S(2)}) async-start(bf16[4,128,2048]{2,1,0:T(8,128)(2,1)} %tile.5), calls=%async_computation.1 | async-start | bytes 4194304 | tf_op jit(solution)/shard_map/all_to_all | solution.py:42
  38.0 7.6 %collective-permute-start.9 = (bf16[64,2048]{1,0:T(8,128)(2,1)S(1)}, bf16[64,2048]{1,0:T(8,128)(2,1)S(1)}, u32[]{:S(2)}, u32[]{:S(2)}) collective-permute-start(bf16[64,2048]{1,0:T(8,128)(2,1)S(1)} %collective-permute-done.6.refs_8_), channel_id=1, source_target_pairs={{0,4},{1,5},{2,6},{3,7},{4,8},{5,9},{6,10},{7,11},{8,12},{9,13},{1... | collective-permute-start | bytes 786440 | tf_op jit(solution)/shard_map/ppermute | solution.py:68
  38.2 7.4 %collective-permute-start.7 = (bf16[64,2048]{1,0:T(8,128)(2,1)S(1)}, bf16[64,2048]{1,0:T(8,128)(2,1)S(1)}, u32[]{:S(2)}, u32[]{:S(2)}) collective-permute-start(bf16[64,2048]{1,0:T(8,128)(2,1)S(1)} %collective-permute-done.5.refs_1_), channel_id=1, source_target_pairs={{4,0},{5,1},{6,2},{7,3},{8,4},{9,5},{10,6},{11,7},{12,8},{13,9},{1... | collective-permute-start | bytes 786440 | tf_op jit(solution)/shard_map/ppermute | solution.py:69
  45.6 2.7 %copy-start.5 = (bf16[64,2048]{1,0:T(8,128)(2,1)}, bf16[64,2048]{1,0:T(8,128)(2,1)S(1)}, u32[]{:S(2)}) copy-start(bf16[64,2048]{1,0:T(8,128)(2,1)S(1)} %collective-permute-done.9.refs_7_) | copy-start | bytes 786436
  45.6 6.7 %collective-permute-start.10 = (bf16[64,2048]{1,0:T(8,128)(2,1)S(1)}, bf16[64,2048]{1,0:T(8,128)(2,1)S(1)}, u32[]{:S(2)}, u32[]{:S(2)}) collective-permute-start(bf16[64,2048]{1,0:T(8,128)(2,1)S(1)} %collective-permute-done.9.refs_7_), channel_id=1, source_target_pairs={{0,4},{1,5},{2,6},{3,7},{4,8},{5,9},{6,10},{7,11},{8,12},{9,13},{1... | collective-permute-start | bytes 786440 | tf_op jit(solution)/shard_map/ppermute | solution.py:68
  45.6 7.4 %copy-start.6 = (bf16[64,2048]{1,0:T(8,128)(2,1)}, bf16[64,2048]{1,0:T(8,128)(2,1)S(1)}, u32[]{:S(2)}) copy-start(bf16[64,2048]{1,0:T(8,128)(2,1)S(1)} %collective-permute-done.7.refs_2_) | copy-start | bytes 786436
  45.6 7.4 %collective-permute-start.8 = (bf16[64,2048]{1,0:T(8,128)(2,1)S(1)}, bf16[64,2048]{1,0:T(8,128)(2,1)S(1)}, u32[]{:S(2)}, u32[]{:S(2)}) collective-permute-start(bf16[64,2048]{1,0:T(8,128)(2,1)S(1)} %collective-permute-done.7.refs_2_), channel_id=1, source_target_pairs={{4,0},{5,1},{6,2},{7,3},{8,4},{9,5},{10,6},{11,7},{12,8},{13,9},{1... | collective-permute-start | bytes 786440 | tf_op jit(solution)/shard_map/ppermute | solution.py:69
  48.3 26.1 %collective-permute-start.13 = (bf16[768,1024]{1,0:T(8,128)(2,1)}, bf16[768,1024]{1,0:T(8,128)(2,1)}, u32[]{:S(2)}, u32[]{:S(2)}) collective-permute-start(bf16[768,1024]{1,0:T(8,128)(2,1)} %down_a.1), channel_id=1, source_target_pairs={{0,32},{32,0},{64,96},{96,64},{128,160},{160,128},{192,224},{224,1... | collective-permute-start | bytes 4718600 | tf_op jit(solution)/shard_map/ppermute | solution.py:37
  53.0 5.5 %collective-permute-start.11 = (bf16[32,2048]{1,0:T(8,128)(2,1)}, bf16[32,2048]{1,0:T(8,128)(2,1)S(1)}, u32[]{:S(2)}, u32[]{:S(2)}) collective-permute-start(bf16[32,2048]{1,0:T(8,128)(2,1)} %slice.54), channel_id=1, source_target_pairs={{0,4},{1,5},{2,6},{3,7},{4,8},{5,9},{6,10},{7,11},{8,12},{9,13},{1... | collective-permute-start | bytes 393224 | tf_op jit(solution)/shard_map/ppermute | solution.py:70
  53.7 4.9 %collective-permute-start.12 = (bf16[32,2048]{1,0:T(8,128)(2,1)}, bf16[32,2048]{1,0:T(8,128)(2,1)}, u32[]{:S(2)}, u32[]{:S(2)}) collective-permute-start(bf16[32,2048]{1,0:T(8,128)(2,1)} %slice.55), channel_id=1, source_target_pairs={{4,0},{5,1},{6,2},{7,3},{8,4},{9,5},{10,6},{11,7},{12,8},{13,9},{1... | collective-permute-start | bytes 393224 | tf_op jit(solution)/shard_map/ppermute | solution.py:71
  70.1 22.6 %all-to-all-start.3 = ((bf16[4,128,1536]{2,1,0:T(8,128)(2,1)}), bf16[4,128,1536]{2,1,0:T(8,128)(2,1)}, u32[]{:S(2)}, u32[]{:S(2)}) async-start(bf16[4,128,1536]{2,1,0:T(8,128)(2,1)} %bitcast.16), calls=%async_computation.3 | async-start | bytes 3145728 | tf_op jit(solution)/shard_map/all_to_all | solution.py:42
  92.7 20.1 %all-to-all-start.2 = ((bf16[4,128,768]{2,1,0:T(8,128)(2,1)}), bf16[4,128,768]{2,1,0:T(8,128)(2,1)S(1)}, u32[]{:S(2)}, u32[]{:S(2)}) async-start(bf16[4,128,768]{2,1,0:T(8,128)(2,1)} %bitcast.17), calls=%async_computation.2 | async-start | bytes 1572864 | tf_op jit(solution)/shard_map/all_to_all | solution.py:42
  98.7 14.1 %copy-start.3 = (bf16[128,768]{1,0:T(8,128)(2,1)}, bf16[128,768]{1,0:T(8,128)(2,1)S(1)}, u32[]{:S(2)}) copy-start(bf16[128,768]{1,0:T(8,128)(2,1)S(1)} %get-tuple-element.28.own) | copy-start | bytes 589828
  98.7 10.1 %collective-permute-start.17 = (bf16[128,768]{1,0:T(8,128)(2,1)S(1)}, bf16[128,768]{1,0:T(8,128)(2,1)S(1)}, u32[]{:S(2)}, u32[]{:S(2)}) collective-permute-start(bf16[128,768]{1,0:T(8,128)(2,1)S(1)} %get-tuple-element.28.own), channel_id=1, source_target_pairs={{0,64},{32,96},{64,128},{96,160},{128,192},{160,224},{192,0},{224,... | collective-permute-start | bytes 589832 | tf_op jit(solution)/shard_map/ppermute | solution.py:57
  100.1 9.3 %collective-permute-start.16 = (bf16[128,768]{1,0:T(8,128)(2,1)S(1)}, bf16[128,768]{1,0:T(8,128)(2,1)S(1)}, u32[]{:S(2)}, u32[]{:S(2)}) collective-permute-start(bf16[128,768]{1,0:T(8,128)(2,1)S(1)} %get-tuple-element.28.own), channel_id=1, source_target_pairs={{64,0},{96,32},{128,64},{160,96},{192,128},{224,160},{0,192},{32,2... | collective-permute-start | bytes 589832 | tf_op jit(solution)/shard_map/ppermute | solution.py:58
  109.4 5.0 %collective-permute-start.18 = (bf16[64,768]{1,0:T(8,128)(2,1)}, bf16[64,768]{1,0:T(8,128)(2,1)}, u32[]{:S(2)}, u32[]{:S(2)}) collective-permute-start(bf16[64,768]{1,0:T(8,128)(2,1)} %slice.56), channel_id=1, source_target_pairs={{0,64},{32,96},{64,128},{96,160},{128,192},{160,224},{192,0},{224,... | collective-permute-start | bytes 294920 | tf_op jit(solution)/shard_map/ppermute | solution.py:59
  109.4 3.4 %copy-start.1 = (bf16[128,768]{1,0:T(8,128)(2,1)}, bf16[128,768]{1,0:T(8,128)(2,1)S(1)}, u32[]{:S(2)}) copy-start(bf16[128,768]{1,0:T(8,128)(2,1)S(1)} %collective-permute-done.16.behind) | copy-start | bytes 589828
  110.1 4.6 %collective-permute-start.19 = (bf16[64,768]{1,0:T(8,128)(2,1)}, bf16[64,768]{1,0:T(8,128)(2,1)}, u32[]{:S(2)}, u32[]{:S(2)}) collective-permute-start(bf16[64,768]{1,0:T(8,128)(2,1)} %slice.57), channel_id=1, source_target_pairs={{64,0},{96,32},{128,64},{160,96},{192,128},{224,160},{0,192},{32,2... | collective-permute-start | bytes 294920 | tf_op jit(solution)/shard_map/ppermute | solution.py:60
  112.8 1.1 copy-start
  114.7 0.9 copy-start.2
  115.6 0.9 copy-start.4
  122.3 33.5 %all-to-all-start.4 = ((bf16[4,128,2048]{2,1,0:T(8,128)(2,1)}), bf16[4,128,2048]{2,1,0:T(8,128)(2,1)}, u32[]{:S(2)}, u32[]{:S(2)}) async-start(bf16[4,128,2048]{2,1,0:T(8,128)(2,1)} %bitcast.14), calls=%async_computation.4 | async-start | bytes 4194304 | tf_op jit(solution)/shard_map/all_to_all | solution.py:42
  126.8 8.3 %collective-permute-start.21 = (bf16[128,1536]{1,0:T(8,128)(2,1)S(1)}, bf16[128,1536]{1,0:T(8,128)(2,1)S(1)}, u32[]{:S(2)}, u32[]{:S(2)}) collective-permute-start(bf16[128,1536]{1,0:T(8,128)(2,1)S(1)} %shard_map.95.own), channel_id=1, source_target_pairs={{0,64},{32,96},{64,128},{96,160},{128,192},{160,224},{192,0},{224,... | collective-permute-start | bytes 1179656 | tf_op jit(solution)/shard_map/ppermute | solution.py:57
  128.2 6.9 %collective-permute-start.20 = (bf16[128,1536]{1,0:T(8,128)(2,1)S(1)}, bf16[128,1536]{1,0:T(8,128)(2,1)S(1)}, u32[]{:S(2)}, u32[]{:S(2)}) collective-permute-start(bf16[128,1536]{1,0:T(8,128)(2,1)S(1)} %shard_map.95.own), channel_id=1, source_target_pairs={{64,0},{96,32},{128,64},{160,96},{192,128},{224,160},{0,192},{32,2... | collective-permute-start | bytes 1179656 | tf_op jit(solution)/shard_map/ppermute | solution.py:58
  135.1 12.6 %collective-permute-start.22 = (bf16[64,1536]{1,0:T(8,128)(2,1)S(1)}, bf16[64,1536]{1,0:T(8,128)(2,1)S(1)}, u32[]{:S(2)}, u32[]{:S(2)}) collective-permute-start(bf16[64,1536]{1,0:T(8,128)(2,1)S(1)} %slice.58), channel_id=1, source_target_pairs={{0,64},{32,96},{64,128},{96,160},{128,192},{160,224},{192,0},{224,... | collective-permute-start | bytes 589832 | tf_op jit(solution)/shard_map/ppermute | solution.py:59
  135.2 12.5 %collective-permute-start.23 = (bf16[64,1536]{1,0:T(8,128)(2,1)S(1)}, bf16[64,1536]{1,0:T(8,128)(2,1)S(1)}, u32[]{:S(2)}, u32[]{:S(2)}) collective-permute-start(bf16[64,1536]{1,0:T(8,128)(2,1)S(1)} %slice.59), channel_id=1, source_target_pairs={{64,0},{96,32},{128,64},{160,96},{192,128},{224,160},{0,192},{32,2... | collective-permute-start | bytes 589832 | tf_op jit(solution)/shard_map/ppermute | solution.py:60
  137.9 26.9 %collective-permute-start.25 = (bf16[512,1024]{1,0:T(8,128)(2,1)}, bf16[512,1024]{1,0:T(8,128)(2,1)}, u32[]{:S(2)}, u32[]{:S(2)}) collective-permute-start(bf16[512,1024]{1,0:T(8,128)(2,1)} %get-tuple-element.35), channel_id=1, source_target_pairs={{0,32},{32,0},{64,96},{96,64},{128,160},{160,128},{192,224},{224,1... | collective-permute-start | bytes 3145736 | tf_op jit(solution)/shard_map/ppermute | solution.py:37
  155.8 27.4 %all-to-all-start.5 = ((bf16[4,128,2048]{2,1,0:T(8,128)(2,1)}), bf16[4,128,2048]{2,1,0:T(8,128)(2,1)}, u32[]{:S(2)}, u32[]{:S(2)}) async-start(bf16[4,128,2048]{2,1,0:T(8,128)(2,1)} %bitcast.15), calls=%async_computation.5 | async-start | bytes 4194304 | tf_op jit(solution)/shard_map/all_to_all | solution.py:42
  160.2 6.0 %collective-permute-start.24 = (bf16[512,768]{1,0:T(8,128)(2,1)}, bf16[512,768]{1,0:T(8,128)(2,1)S(1)}, u32[]{:S(2)}, u32[]{:S(2)}) collective-permute-start(bf16[512,768]{1,0:T(8,128)(2,1)} %get-tuple-element.34), channel_id=1, source_target_pairs={{0,32},{32,0},{64,96},{96,64},{128,160},{160,128},{192,224},{224,1... | collective-permute-start | bytes 2359304 | tf_op jit(solution)/shard_map/ppermute | solution.py:37
  164.1 6.6 %collective-permute-start.26 = (bf16[512,1024]{1,0:T(8,128)(2,1)}, bf16[512,1024]{1,0:T(8,128)(2,1)S(1)}, u32[]{:S(2)}, u32[]{:S(2)}) collective-permute-start(bf16[512,1024]{1,0:T(8,128)(2,1)} %get-tuple-element.36), channel_id=1, source_target_pairs={{0,32},{32,0},{64,96},{96,64},{128,160},{160,128},{192,224},{224,1... | collective-permute-start | bytes 3145736 | tf_op jit(solution)/shard_map/ppermute | solution.py:37
  164.2 6.5 %collective-permute-start.27 = (bf16[512,768]{1,0:T(8,128)(2,1)}, bf16[512,768]{1,0:T(8,128)(2,1)S(1)}, u32[]{:S(2)}, u32[]{:S(2)}) collective-permute-start(bf16[512,768]{1,0:T(8,128)(2,1)} %get-tuple-element.37), channel_id=1, source_target_pairs={{0,32},{32,0},{64,96},{96,64},{128,160},{160,128},{192,224},{224,1... | collective-permute-start | bytes 2359304 | tf_op jit(solution)/shard_map/ppermute | solution.py:37
  170.7 1.0 copy-start.7
  186.9 13.9 %copy-start.8 = (bf16[512,1024]{1,0:T(8,128)(2,1)S(1)}, bf16[512,1024]{1,0:T(8,128)(2,1)}, u32[]{:S(2)}) copy-start(bf16[512,1024]{1,0:T(8,128)(2,1)} %copy-done.7) | copy-start | bytes 3145732
  186.9 32.0 %all-to-all-start.6 = ((bf16[8,16,4096]{2,1,0:T(8,128)(2,1)}), bf16[8,16,4096]{2,1,0:T(8,128)(2,1)S(1)}, u32[]{:S(2)}, u32[]{:S(2)}) async-start(bf16[8,16,4096]{2,1,0:T(8,128)(2,1)} %bitcast.9), calls=%async_computation.6 | async-start | bytes 2097152 | tf_op jit(solution)/shard_map/all_to_all | solution.py:42
  193.8 7.0 %collective-permute-start.28 = (bf16[512,768]{1,0:T(8,128)(2,1)}, bf16[512,768]{1,0:T(8,128)(2,1)S(1)}, u32[]{:S(2)}, u32[]{:S(2)}) collective-permute-start(bf16[512,768]{1,0:T(8,128)(2,1)} %get-tuple-element.39), channel_id=1, source_target_pairs={{0,32},{32,0},{64,96},{96,64},{128,160},{160,128},{192,224},{224,1... | collective-permute-start | bytes 2359304 | tf_op jit(solution)/shard_map/ppermute | solution.py:37
  219.1 5.6 %collective-permute-start.30 = (bf16[16,1024]{1,0:T(8,128)(2,1)S(1)}, bf16[16,1024]{1,0:T(8,128)(2,1)S(1)}, u32[]{:S(2)}, u32[]{:S(2)}) collective-permute-start(bf16[16,1024]{1,0:T(8,128)(2,1)S(1)} %slice.65), channel_id=1, source_target_pairs={{0,32},{32,0},{64,96},{96,64},{128,160},{160,128},{192,224},{224,1... | collective-permute-start | bytes 98312 | tf_op jit(solution)/shard_map/ppermute | solution.py:37
  224.7 1.3 collective-permute-start.29
